TPU v7x, 512 devices: a whole 4x4x16 slice. The times are simulated.
512 devices in a mesh: view: 64 (over z_lo, x, core), row: 8 (over z_hi, y).
Axes of the slice: x: 4, y: 4, z: 16 (z_hi: 2, z_lo: 8; z = z_hi * 8 + z_lo), core: 2. Of those that a mesh axis runs over, the one named last changes fastest.
Arguments:
- layers: bfloat16 [3, 3, 384, 1024], P(None, None, 'row'), may hold values from 0.19921875 to 1
- target: bfloat16 [64, 384, 1024], P('view', 'row'), may hold values from 0.049804688 to 0.5
- shifts: int32 [64, 3, 2], P('view'), may hold values from -8 to 8, as said below
Outputs:
- updated: float32 [3, 3, 384, 1024], P(None, None, 'row')
Inputs may be any that keep to these rules, and one draw needn't show every extreme that they name: `shifts`: for every layer and each of the two components, one view has shift 8 and another view has shift -8.
All inputs are finite; a program needn't handle non-finite values.
Results may differ from a plain program's by a relative error of at most 0.0003.
Values may be sent and summed in bfloat16 or wider, within the bound.
No kernel may reach another device: no remote copies, remote signals or barrier semaphores. Data moves between devices by JAX's collectives and lax.ppermute only.
A program may use at most 64 MiB of HBM per device.

v0:
```python
import jax
import jax.numpy as jnp
from jax import lax
from jax.sharding import PartitionSpec as P

HALO = 8


regular = 0.05


def padded(cells, sides, width):
    for axis, dim in sides:
        count = lax.axis_size(axis)
        ends = count - 1
        head = lax.slice_in_dim(cells, 0, width, axis=dim)
        tail = lax.slice_in_dim(cells, cells.shape[dim] - width, cells.shape[dim], axis=dim)
        cells = jnp.concatenate(
            [
                lax.ppermute(tail, axis, [(i, (i + 1) % count) for i in range(ends)]),
                cells,
                lax.ppermute(head, axis, [((i + 1) % count, i) for i in range(ends)]),
            ],
            axis=dim,
        )
    return cells


def product_except(pieces, skip):
    result = None
    for layer in range(len(pieces)):
        if layer != skip:
            result = pieces[layer] if result is None else result * pieces[layer]
    return result


def body(layers, target, shifts):
    frame_count, layer_count, row_count, col_count = layers.shape
    extended = padded(layers, (("row", 2),), HALO)
    widened = jnp.pad(extended, ((0, 0), (0, 0), (0, 0), (HALO, HALO)))
    zero = jnp.zeros((), jnp.int32)
    pieces = []
    for layer in range(layer_count):
        start_row = HALO + shifts[0, layer, 0]
        start_col = HALO + shifts[0, layer, 1]
        piece = lax.dynamic_slice(
            widened[:, layer], (zero, start_row, start_col), (frame_count, row_count, col_count)
        )
        pieces.append(piece.astype(jnp.float32))
    whole_product = pieces[0]
    for layer in range(1, layer_count):
        whole_product = whole_product * pieces[layer]
    shown = jnp.sum(whole_product, axis=0) / frame_count
    image = target[0].astype(jnp.float32)
    target_terms = jnp.stack(
        [image[None] * product_except(pieces, layer) for layer in range(layer_count)], axis=1
    )
    model_terms = jnp.stack(
        [shown[None] * product_except(pieces, layer) for layer in range(layer_count)], axis=1
    )
    stacked = jnp.stack([target_terms, model_terms])
    stacked = padded(stacked, (("row", 3),), HALO)
    stacked = jnp.pad(stacked, ((0, 0), (0, 0), (0, 0), (0, 0), (HALO, HALO)))
    backs = []
    for layer in range(layer_count):
        start_row = HALO - shifts[0, layer, 0]
        start_col = HALO - shifts[0, layer, 1]
        back = lax.dynamic_slice(
            stacked[:, :, layer],
            (zero, zero, start_row, start_col),
            (2, frame_count, row_count, col_count),
        )
        backs.append(back)
    upper = jnp.stack([back[0] for back in backs], axis=1)
    lower = jnp.stack([back[1] for back in backs], axis=1)
    upper_all, lower_all = lax.psum((upper, lower), "view")
    return layers.astype(jnp.float32) * (upper_all + regular) / (lower_all + regular)


def solution(mesh):
    placed = (P(None, None, "row", None), P("view", "row", None), P("view", None, None))
    return jax.shard_map(
        body, mesh=mesh, in_specs=placed, out_specs=P(None, None, "row", None), check_vma=False
    )
```

profile of v0, /device:TPU:25, one launch (start us, length us, event | category | flops | bytes accessed | tf_op | source)
XLA Modules:
  0.0 967.2 jit_solution(1097642098018638871)
XLA Ops:
  6.5 0.0 all-reduce.5.cloned.1.call-start
  6.5 1.0 fusion.17
  7.5 15.1 %collective-permute-start = (bf16[3,3,8,1024]{3,2,0,1:T(8,128)(2,1)S(1)}, bf16[3,3,8,1024]{3,2,0,1:T(8,128)(2,1)S(1)}, u32[]{:S(2)}, u32[]{:S(2)}) collective-permute-start(bf16[3,3,8,1024]{3,2,0,1:T(8,128)(2,1)S(1)} %get-tuple-element.25), channel_id=1, source_target_pairs={{0,1},{1,2},{2,3},{3,4},{4,5},{5,6},{6,7},{8,9},{9,10},{10,11},{11... | collective-permute-start | bytes 442376 | tf_op jit(solution)/shard_map/ppermute | solution.py:20
  22.7 1.9 collective-permute-start.1
  24.6 1.6 fusion.18
  33.5 0.9 bitcast_convert_fusion
  34.5 0.0 collective-permute-done
  34.5 5.3 collective-permute-done.1
  39.8 1.8 fusion.7
  41.6 0.1 fusion.16
  41.7 0.7 fusion.10
  42.4 0.6 fusion.9
  43.1 0.4 maximum_bitcast_fusion
  43.5 1.1 pad_maximum_fusion.3
  44.6 8.9 collective-permute-start.2
  53.5 1.9 collective-permute-start.3
  62.8 2.4 collective-permute-done.2
  65.2 14.7 %collective-permute-done.3 = f32[2,3,3,8,1024]{4,3,1,2,0:T(8,128)} collective-permute-done((f32[2,3,3,8,1024]{4,3,1,2,0:T(8,128)}, f32[2,3,3,8,1024]{4,3,1,2,0:T(8,128)}, u32[]{:S(2)}, u32[]{:S(2)}) %collective-permute-start.3) | collective-permute-done | bytes 589856 | tf_op jit(solution)/shard_map/ppermute | solution.py:22
  79.8 4.9 select_maximum_fusion
  84.7 0.5 fusion.15
  85.2 0.4 dynamic-slice_bitcast_fusion.5
  85.6 0.4 dynamic-slice_bitcast_fusion.4
  85.9 0.4 dynamic-slice_bitcast_fusion.3
  86.3 1.4 pad_maximum_fusion
  87.8 1.4 pad_maximum_fusion.1
  89.2 0.0 copy-start
  89.2 0.0 all-reduce.5.cloned.1.call-update
  89.2 867.3 %all-reduce.5.cloned.1.call-done = (f32[3,3,48,1024]{3,2,0,1:T(8,128)}, f32[3,3,48,1024]{3,2,1,0:T(8,128)}) async-done(((f32[3,3,48,1024]{3,2,0,1:T(8,128)}, f32[3,3,48,1024]{3,2,1,0:T(8,128)}), (f32[3,3,48,1024]{3,2,0,1:T(8,128)}, f32[3,3,48,1024]{3,2,1,0:T(8,128)})) %all-reduce.5.cloned.1.call-update) | async-done | bytes 3538960 | tf_op jit(solution)/shard_map/psum | solution.py:76
  956.5 0.0 copy-done
  956.5 3.8 fusion.2
  (1 shorter events, 0.0 us)
Async XLA Ops:
  6.5 950.0 %all-reduce.5.cloned.1.call-start = ((), (), s32[]{:S(2)}) async-start(), calls=%async_computation | async-start | bytes 7077888 | tf_op jit(solution)/shard_map/psum | solution.py:76
  7.5 26.9 %collective-permute-start = (bf16[3,3,8,1024]{3,2,0,1:T(8,128)(2,1)S(1)}, bf16[3,3,8,1024]{3,2,0,1:T(8,128)(2,1)S(1)}, u32[]{:S(2)}, u32[]{:S(2)}) collective-permute-start(bf16[3,3,8,1024]{3,2,0,1:T(8,128)(2,1)S(1)} %get-tuple-element.25), channel_id=1, source_target_pairs={{0,1},{1,2},{2,3},{3,4},{4,5},{5,6},{6,7},{8,9},{9,10},{10,11},{11... | collective-permute-start | bytes 442376 | tf_op jit(solution)/shard_map/ppermute | solution.py:20
  22.7 17.1 %collective-permute-start.1 = (bf16[3,3,8,1024]{3,2,0,1:T(8,128)(2,1)S(1)}, bf16[3,3,8,1024]{3,2,0,1:T(8,128)(2,1)S(1)}, u32[]{:S(2)}, u32[]{:S(2)}) collective-permute-start(bf16[3,3,8,1024]{3,2,0,1:T(8,128)(2,1)S(1)} %get-tuple-element.26), channel_id=1, source_target_pairs={{1,0},{2,1},{3,2},{4,3},{5,4},{6,5},{7,6},{9,8},{10,9},{11,10},{12... | collective-permute-start | bytes 442376 | tf_op jit(solution)/shard_map/ppermute | solution.py:22
  44.6 20.6 %collective-permute-start.2 = (f32[2,3,3,8,1024]{4,3,1,2,0:T(8,128)}, f32[2,3,3,8,1024]{4,3,1,2,0:T(8,128)}, u32[]{:S(2)}, u32[]{:S(2)}) collective-permute-start(f32[2,3,3,8,1024]{4,3,1,2,0:T(8,128)} %get-tuple-element.10), channel_id=1, source_target_pairs={{0,1},{1,2},{2,3},{3,4},{4,5},{5,6},{6,7},{8,9},{9,10},{10,11},{11... | collective-permute-start | bytes 1769480 | tf_op jit(solution)/shard_map/ppermute | solution.py:20
  53.5 26.3 %collective-permute-start.3 = (f32[2,3,3,8,1024]{4,3,1,2,0:T(8,128)}, f32[2,3,3,8,1024]{4,3,1,2,0:T(8,128)}, u32[]{:S(2)}, u32[]{:S(2)}) collective-permute-start(f32[2,3,3,8,1024]{4,3,1,2,0:T(8,128)} %get-tuple-element.11), channel_id=1, source_target_pairs={{1,0},{2,1},{3,2},{4,3},{5,4},{6,5},{7,6},{9,8},{10,9},{11,10},{12... | collective-permute-start | bytes 1769480 | tf_op jit(solution)/shard_map/ppermute | solution.py:22
  89.2 867.3 %copy-start = (bf16[3,3,48,1024]{3,2,1,0:T(8,128)(2,1)S(1)}, bf16[3,3,48,1024]{3,2,1,0:T(8,128)(2,1)}, u32[]{:S(2)}) copy-start(bf16[3,3,48,1024]{3,2,1,0:T(8,128)(2,1)} %param.3) | copy-start | bytes 2654212
Sparse Core Ops, SparseCore 0:
  89.3 867.1 all-reduce.4
where the time goes:
time: 972 us; the launch traced here: 967 us
  waiting for transfers between devices  890 us (92%)
  between operations  28.3 us (3%)
  starting transfers between devices  27.8 us (3%)
  other arithmetic  17.1 us (2%)
    psum x1, waiting for transfers between devices, body(): upper_all, lower_all = lax.psum((upper, lower), 'view')  867 us
    ppermute x2, starting transfers between devices, padded(): lax.ppermute(tail, axis, [(i, (i + 1) % count) for i in range(ends)])  24 us
    ppermute x2, waiting for transfers between devices, padded(): lax.ppermute(head, axis, [((i + 1) % count, i) for i in range(ends)])  20 us
  transfers between devices with their start and end apart: 5, of which 4 were waited for; matrix products, arithmetic and copies ran while one was open for 0% of the time, Pallas kernels for 0%

commit v1 on v0

v1 whole, which is shorter than its diff:
```python
import jax
import jax.numpy as jnp
from jax import lax
from jax.experimental import pallas as pl
from jax.experimental.pallas import tpu as pltpu
from jax.sharding import Mesh, PartitionSpec as P

HALO = 8
SPAN = 2 * HALO + 1
TILE = 16
SEG = 32
REGULAR = 0.05
CODE_STEPS = 5041.0
CODE_BASE = 7.0
F32 = jnp.float32
BF16 = jnp.bfloat16
VIEW = ("zl", "x", "c")
ROW = ("zh", "y")
PARAMS = pltpu.CompilerParams(vmem_limit_bytes=48 * 1024 * 1024)


def lanes(rows):
    return lax.broadcasted_iota(jnp.int32, (rows, 128), 1)


def my_tile():
    high = lax.axis_index("zh")
    along = lax.rem(lax.axis_index("zl") + 4 * high, 8)
    return along, lax.axis_index("x") * 2 + lax.axis_index("c")


def pack_kernel(layers_ref, target_ref, shifts_ref, chunks_ref, own_ref, head_ref, tail_ref):
    high = lax.axis_index("zh")
    lane = lanes(16)
    extra = jnp.zeros((16, 128), F32)
    for layer in range(3):
        for part in range(2):
            extra = jnp.where(
                lane == 96 + 2 * layer + part, shifts_ref[0, layer, part].astype(F32), extra
            )
    zero = jnp.zeros((16, 128), F32)
    for group in range(8):
        sources = []
        for b in range(3):
            rows = slice(16 * b, 16 * b + 16)
            mid = target_ref[0, rows, 128 * group : 128 * group + 128].astype(F32)
            left = zero
            right = zero
            if group > 0:
                left = target_ref[0, rows, 128 * group - 128 : 128 * group].astype(F32)
            if group < 7:
                right = target_ref[0, rows, 128 * group + 128 : 128 * group + 256].astype(F32)
            sources.append(
                (jnp.where(lane >= 128 - HALO, left, mid), mid, jnp.where(lane < HALO, right, mid))
            )
        for t8 in range(8):
            which = 0 if t8 == 0 else (2 if t8 == 7 else 1)
            chunk = extra
            for b in range(3):
                amount = (SEG * b - (TILE * t8 - HALO)) % 128
                moved = pltpu.roll(sources[b][which], amount, 1) if amount else sources[b][which]
                chunk = jnp.where((lane >= SEG * b) & (lane < SEG * b + SEG), moved, chunk)
            place = lax.rem(group + 4 * high, 8) * 8 + t8
            chunks_ref[place] = chunk.astype(BF16)

    along, t8 = my_tile()
    first = along * 128 + t8 * TILE - 2 * HALO
    window = jnp.clip(jnp.where(first < 0, 0, first // 128), 0, 6)
    start = pl.multiple_of(window * 128, 128)
    row = lax.broadcasted_iota(jnp.int32, (256, 256), 0)
    col = lax.broadcasted_iota(jnp.int32, (256, 256), 1)
    wanted = first - start + (col & (SEG - 1)) + TILE * (col // 128)
    segment = (col & 127) // SEG
    total = None
    for frame in range(3):
        pick = jnp.where((row == wanted) & (segment == frame), 1.0, 0.0).astype(BF16)
        part = layers_ref[frame, :, :, pl.ds(start, 256)].reshape(3 * 48, 256)
        moved = jnp.dot(part, pick, preferred_element_type=F32)
        total = moved if total is None else total + moved
    for layer in range(3):
        for side in range(2):
            cells = total[48 * layer : 48 * layer + 48, 128 * side : 128 * side + 128]
            own_ref[2 * layer + side] = cells
            head_ref[2 * layer + side] = cells[:HALO]
            tail_ref[2 * layer + side] = cells[48 - HALO :]


def view_kernel(
    recv_ref, own_ref, above_ref, below_ref, own_out, up_out, down_out,
    seen_ref, image_ref, shift_ref, shift_smem, sem, *sums,
):
    shift_ref[...] = recv_ref[:, 0, :].astype(F32).astype(jnp.int32)
    copy = pltpu.make_async_copy(shift_ref, shift_smem, sem)
    copy.start()

    lane = lanes(64)
    within = lane & (SEG - 1)
    for layer in range(3):
        low, high = (
            jnp.concatenate(
                [above_ref[2 * layer + s], own_ref[2 * layer + s], below_ref[2 * layer + s]], axis=0
            )
            for s in range(2)
        )
        for d in range(SPAN):
            a = pltpu.roll(low, (128 - d) % 128, 1) if d else low
            b = pltpu.roll(high, 16 - d, 1) if d < 16 else high
            seen_ref[layer, d] = jnp.where(within < SEG - d, a, b)

    row = lax.broadcasted_iota(jnp.int32, (128, 384), 0)
    col = lax.broadcasted_iota(jnp.int32, (128, 384), 1)
    pick = (row == (col // 128) * SEG + (col & (SEG - 1))) & ((col & 127) < 3 * SEG)
    pick = jnp.where(pick, 1.0, 0.0).astype(BF16)
    for part in range(8):
        block = recv_ref[8 * part : 8 * part + 8].reshape(128, 128)
        spread = jnp.dot(block, pick, preferred_element_type=F32)
        for b in range(3):
            image_ref[8 * part : 8 * part + 8, 16 * b : 16 * b + 16, :] = spread[
                :, 128 * b : 128 * b + 128
            ].reshape(8, 16, 128)

    for ref in sums:
        ref[...] = jnp.zeros_like(ref)

    along, t8 = my_tile()
    column = along * 128 + t8 * TILE - HALO + (lanes(8) & (SEG - 1))
    third = jnp.where((column >= 0) & (column < 1024), 1.0 / 3.0, 0.0)[0:1]
    copy.wait()

    def one_view(view, carry):
        rows = [shift_smem[view, 96 + 2 * layer] + HALO for layer in range(3)]
        cols = [shift_smem[view, 97 + 2 * layer] + HALO for layer in range(3)]
        s0, s1, s2 = (
            seen_ref[layer, cols[layer], pl.ds(rows[layer], 48), :] for layer in range(3)
        )
        p01 = s0 * s1
        whole = p01 * s2
        pair = whole + pltpu.roll(whole, 64, 1)
        shown = (pair + pltpu.roll(pair, 32, 1)) * third
        image = image_ref[view]
        for layer, others in enumerate((s1 * s2, s0 * s2, p01)):
            for which, factor in enumerate((image, shown)):
                sums[2 * layer + which][cols[layer], pl.ds(rows[layer], 48), :] += factor * others
        return carry

    lax.fori_loop(0, 64, one_view, 0)

    for at in range(6):
        total = None
        for d in range(SPAN):
            cells = sums[at][d]
            moved = pltpu.roll(cells, (d - HALO) % 128, 1) if d != HALO else cells
            total = moved if total is None else total + moved
        up_out[at] = total[:HALO]
        own_out[at] = total[HALO : HALO + 48]
        down_out[at] = total[HALO + 48 :]


def update_kernel(own_ref, above_ref, below_ref, layer_ref, out_ref):
    lane = lanes(48)
    within = lane & (SEG - 1)
    codes = []
    for layer in range(3):
        low = pltpu.roll(layer_ref[2 * layer], 128 - HALO, 1)
        high = pltpu.roll(layer_ref[2 * layer + 1], HALO, 1)
        cells = jnp.where(within < SEG - HALO, low, high)
        sides = []
        for which in range(2):
            at = 2 * layer + which
            own = own_ref[at]
            sides.append(
                jnp.concatenate(
                    [own[:HALO] + above_ref[at], own[HALO:40], own[40:] + below_ref[at]], axis=0
                )
            )
        value = cells * (sides[0] + REGULAR) / (sides[1] + REGULAR)
        scaled = (jnp.log2(value) + CODE_BASE) * CODE_STEPS + 0.5
        codes.append(jnp.clip(scaled, 0.0, 65535.0).astype(jnp.int32))
    lane = lanes(8)
    blocks = [jnp.zeros((8, 128), jnp.int32) for _ in range(8)]
    for group in range(54):
        frame, layer, g = group // 18, (group // 6) % 3, group % 6
        cells = codes[layer][8 * g : 8 * g + 8]
        amount = (TILE * (group % 8) - (SEG * frame + HALO)) % 128
        moved = pltpu.roll(cells, amount, 1) if amount else cells
        blocks[group // 8] = jnp.where(lane // TILE == group % 8, moved, blocks[group // 8])
    _, t8 = my_tile()
    for j in range(4):
        word = blocks[j] + (blocks[j + 4] - 32768) * 65536
        word = pltpu.roll(word, TILE * t8, 1)
        for copy in range(8):
            out_ref[copy, 8 * j : 8 * j + 8] = word


def spread_kernel(words_ref, out_ref):
    high = lax.axis_index("zh")
    lane = lanes(8) // TILE

    def one(at, carry):
        place = pl.multiple_of(lax.rem(at + 4 * high, 8) * 128, 128)
        for j in range(4):
            words = [words_ref[t8, at, 8 * j : 8 * j + 8] for t8 in range(8)]
            for i in range(8):
                merged = words[0]
                for t8 in range(1, 8):
                    merged = jnp.where(lane == (i + t8) % 8, words[t8], merged)
                if i:
                    merged = pltpu.roll(merged, 128 - TILE * i, 1)
                for group, code in ((8 * j + i, merged & 65535), (8 * j + i + 32, (merged >> 16) + 32768)):
                    if group < 54:
                        value = jnp.exp2(code.astype(F32) * (1.0 / CODE_STEPS) - CODE_BASE)
                        frame, layer, g = group // 18, (group // 6) % 3, group % 6
                        out_ref[frame, layer, 8 * g : 8 * g + 8, pl.ds(place, 128)] = value
        return carry

    lax.fori_loop(0, 8, one, 0)


def row_pairs(step):
    pairs = []
    for zl in range(8):
        for zh in range(2):
            for y in range(4):
                at = zh * 4 + y + step
                if 0 <= at < 8:
                    other = (zl + 4 * (zh != at // 4)) % 8
                    pairs.append(((zl * 2 + zh) * 4 + y, (other * 2 + at // 4) * 4 + at % 4))
    return pairs


def body(layers, target, shifts):
    vmem = pl.BlockSpec(memory_space=pltpu.VMEM)
    smem = pl.BlockSpec(memory_space=pltpu.SMEM)
    shape = jax.ShapeDtypeStruct
    across = ("zl", "zh", "y")

    chunks, own, head, tail = pl.pallas_call(
        pack_kernel,
        out_shape=(
            shape((64, 16, 128), BF16),
            shape((6, 48, 128), F32),
            shape((6, HALO, 128), F32),
            shape((6, HALO, 128), F32),
        ),
        in_specs=[vmem, vmem, smem],
        out_specs=(vmem,) * 4,
        compiler_params=PARAMS,
    )(layers, target, shifts)
    above = lax.ppermute(tail, across, row_pairs(1))
    below = lax.ppermute(head, across, row_pairs(-1))
    received = lax.all_to_all(chunks, VIEW, 0, 0)

    sums, up, down = pl.pallas_call(
        view_kernel,
        out_shape=(
            shape((6, 48, 128), F32),
            shape((6, HALO, 128), F32),
            shape((6, HALO, 128), F32),
        ),
        in_specs=[vmem] * 4,
        out_specs=(vmem,) * 3,
        scratch_shapes=[
            pltpu.VMEM((3, SPAN, 64, 128), F32),
            pltpu.VMEM((64, 48, 128), F32),
            pltpu.VMEM((64, 128), jnp.int32),
            pltpu.SMEM((64, 128), jnp.int32),
            pltpu.SemaphoreType.DMA,
        ]
        + [pltpu.VMEM((SPAN, 64, 128), F32)] * 6,
        compiler_params=PARAMS,
    )(received, own, above, below)
    from_above = lax.ppermute(down, across, row_pairs(1))
    from_below = lax.ppermute(up, across, row_pairs(-1))

    words = pl.pallas_call(
        update_kernel,
        out_shape=shape((8, 32, 128), jnp.int32),
        in_specs=[vmem] * 4,
        out_specs=vmem,
        compiler_params=PARAMS,
    )(sums, from_above, from_below, own)
    words = lax.all_to_all(words, "zl", 0, 0)
    words = lax.all_gather(words, ("x", "c"))

    return pl.pallas_call(
        spread_kernel,
        out_shape=shape((3, 3, 48, 1024), F32),
        in_specs=[vmem],
        out_specs=vmem,
        compiler_params=PARAMS,
    )(words)


def solution(mesh):
    fine = Mesh(mesh.devices.reshape(8, 4, 2, 2, 4), ("zl", "x", "c", "zh", "y"))
    placed = (P(None, None, ROW, None), P(VIEW, ROW, None), P(VIEW, None, None))
    return jax.shard_map(
        body, mesh=fine, in_specs=placed, out_specs=P(None, None, ROW, None), check_vma=False
    )
```

time: 972 us -> 128 us (0.13)
  waiting for transfers between devices: 890 us -> 42.9 us
  blocking collectives: 0 us -> 17.3 us
  Pallas kernels: 0 us -> 17.1 us
  other arithmetic: 17.1 us -> 0 us
  between operations: 28.3 us -> 13.5 us
    psum x1 -> x0, waiting for transfers between devices: 867 us -> none  [body(): upper_all, lower_all = lax.psum((upper, lower), 'view')]
    all_gather x0 -> x1, waiting for transfers between devices: none -> 25.2 us  [body(): words = lax.all_gather(words, ('x', 'c'))]
    all_to_all x0 -> x1, blocking collectives: none -> 17.3 us  [body(): words = lax.all_to_all(words, 'zl', 0, 0)]
    pallas_call x0 -> x4, Pallas kernels: none -> 17.1 us  [the longest x1 13 us: body(): pl.pallas_call(view_kernel, out_shape=(shape((6, 48, 128), F32), shape((6...]
    all_to_all x0 -> x1, starting transfers between devices: none -> 16.2 us  [body(): received = lax.all_to_all(chunks, VIEW, 0, 0)]
    ppermute x4, starting transfers between devices: 27.8 us -> 15.1 us  [the longest x1 7.9 us: body(): above = lax.ppermute(tail, across, row_pairs(1))]
  transfers between devices with their start and end apart: 5 -> 6, of which waited for: 4 -> 4; matrix products, arithmetic and copies ran while one was open for 0% -> 0% of each run, Pallas kernels for 0% -> 0%
where the time goes in v1:
time: 128 us; the launch traced here: 126 us
  waiting for transfers between devices  42.9 us (34%)
  starting transfers between devices  31.4 us (25%)
  blocking collectives  17.3 us (14%)
  Pallas kernels  17.1 us (13%)
  between operations  13.5 us (11%)
  local copies, waits for them, and re-layouts  4.05 us (3%)
    all_gather x1, waiting for transfers between devices, body(): words = lax.all_gather(words, ('x', 'c'))  25.2 us
    all_to_all x1, blocking collectives, body(): words = lax.all_to_all(words, 'zl', 0, 0)  17.3 us
    all_to_all x1, starting transfers between devices, body(): received = lax.all_to_all(chunks, VIEW, 0, 0)  16.2 us
    pallas_call x1, Pallas kernels, body(): pl.pallas_call(view_kernel, out_shape=(shape((6, 48, 128), F32), shape((6...  13 us
    ppermute x1, waiting for transfers between devices, body(): below = lax.ppermute(head, across, row_pairs(-1))  8.7 us
    ppermute x1, starting transfers between devices, body(): above = lax.ppermute(tail, across, row_pairs(1))  7.9 us
    ppermute x1, waiting for transfers between devices, body(): from_below = lax.ppermute(up, across, row_pairs(-1))  7.7 us
    unnamed x7, local copies, waits for them, and re-layouts  4.05 us
  transfers between devices with their start and end apart: 6, of which 4 were waited for; matrix products, arithmetic and copies ran while one was open for 0% of the time, Pallas kernels for 0%

profile of v1, /device:TPU:25, one launch (start us, length us, event | category | flops | bytes accessed | tf_op | source)
XLA Modules:
  0.0 126.1 jit_solution(17998821158546935901)
XLA Ops:
  6.5 0.8 copy.5.shifts_ref
  7.3 0.0 copy-start.1
  7.3 1.2 copy-done.1
  8.5 0.0 copy-start.2
  8.5 0.9 copy-done.2
  9.4 1.6 %shard_map.37 = (bf16[64,16,128]{2,1,0:T(8,128)(2,1)}, f32[6,48,128]{2,1,0:T(8,128)S(1)}, f32[6,8,128]{2,1,0:T(8,128)S(1)}, f32[6,8,128]{2,1,0:T(8,128)S(1)}) custom-call(bf16[3,3,48,1024]{3,2,1,0:T(8,128)(2,1)S(1)} %copy-done.1, bf16[1,48,1024]{2,1,0:T(8,128)(2,1)S(1)} %copy-done.2, s32[1,3,2]{2,1,0:T(4,128)S(1)} %copy.5.shifts_ref), custom_call_target="tpu_custom_call" | custom-call | tf_op jit(solution)/shard_map/pallas_call | solution.py:237
  11.0 16.2 %all-to-all-start = ((bf16[64,16,128]{2,1,0:T(8,128)(2,1)}), bf16[64,16,128]{2,1,0:T(8,128)(2,1)S(1)}, u32[]{:S(2)}, u32[]{:S(2)}) async-start(bf16[64,16,128]{2,1,0:T(8,128)(2,1)} %get-tuple-element.12), calls=%async_computation | async-start | bytes 524288 | tf_op jit(solution)/shard_map/all_to_all | solution.py:251
  27.2 0.0 all-gather.3.cloned.1.call-start
  27.2 7.9 %collective-permute-start = (f32[6,8,128]{2,1,0:T(8,128)S(1)}, f32[6,8,128]{2,1,0:T(8,128)S(1)}, u32[]{:S(2)}, u32[]{:S(2)}) collective-permute-start(f32[6,8,128]{2,1,0:T(8,128)S(1)} %get-tuple-element.14), channel_id=1, source_target_pairs={{0,1},{1,2},{2,3},{3,260},{4,5},{5,6},{6,7},{64,65},{65,66},{66,67... | collective-permute-start | bytes 73736 | tf_op jit(solution)/shard_map/ppermute | solution.py:249
  35.1 1.9 %collective-permute-start.1 = (f32[6,8,128]{2,1,0:T(8,128)S(1)}, f32[6,8,128]{2,1,0:T(8,128)S(1)}, u32[]{:S(2)}, u32[]{:S(2)}) collective-permute-start(f32[6,8,128]{2,1,0:T(8,128)S(1)} %get-tuple-element.15), channel_id=1, source_target_pairs={{1,0},{2,1},{3,2},{4,259},{5,4},{6,5},{7,6},{65,64},{66,65},{67,66... | collective-permute-start | bytes 73736 | tf_op jit(solution)/shard_map/ppermute | solution.py:250
  37.1 0.0 collective-permute-done.above_ref
  37.1 8.7 %collective-permute-done.1.below_ref = f32[6,8,128]{2,1,0:T(8,128)S(1)} collective-permute-done((f32[6,8,128]{2,1,0:T(8,128)S(1)}, f32[6,8,128]{2,1,0:T(8,128)S(1)}, u32[]{:S(2)}, u32[]{:S(2)}) %collective-permute-start.1) | collective-permute-done | bytes 24608 | tf_op jit(solution)/shard_map/ppermute | solution.py:250
  45.8 1.3 %all-to-all-done.recv_ref = bf16[64,16,128]{2,1,0:T(8,128)(2,1)S(1)} async-done(((bf16[64,16,128]{2,1,0:T(8,128)(2,1)}), bf16[64,16,128]{2,1,0:T(8,128)(2,1)S(1)}, u32[]{:S(2)}, u32[]{:S(2)}) %all-to-all-start) | async-done | bytes 262176 | tf_op jit(solution)/shard_map/all_to_all | solution.py:251
  47.0 13.0 %shard_map.38 = (f32[6,48,128]{2,1,0:T(8,128)S(1)}, f32[6,8,128]{2,1,0:T(8,128)S(1)}, f32[6,8,128]{2,1,0:T(8,128)S(1)}) custom-call(bf16[64,16,128]{2,1,0:T(8,128)(2,1)S(1)} %all-to-all-done.recv_ref, f32[6,48,128]{2,1,0:T(8,128)S(1)} %get-tuple-element.13.own_ref.layer_ref, f32[6,8,128]{2,1,0:T(8,128)S(1)} %collective-permute-done.above_ref, ...), custom_call_target="tpu_custom_call" | custom-call | tf_op jit(solution)/shard_map/pallas_call | solution.py:253
  60.1 2.4 %collective-permute-start.2 = (f32[6,8,128]{2,1,0:T(8,128)S(1)}, f32[6,8,128]{2,1,0:T(8,128)S(1)}, u32[]{:S(2)}, u32[]{:S(2)}) collective-permute-start(f32[6,8,128]{2,1,0:T(8,128)S(1)} %get-tuple-element.17), channel_id=1, source_target_pairs={{0,1},{1,2},{2,3},{3,260},{4,5},{5,6},{6,7},{64,65},{65,66},{66,67... | collective-permute-start | bytes 73736 | tf_op jit(solution)/shard_map/ppermute | solution.py:272
  62.5 2.9 %collective-permute-start.3 = (f32[6,8,128]{2,1,0:T(8,128)S(1)}, f32[6,8,128]{2,1,0:T(8,128)S(1)}, u32[]{:S(2)}, u32[]{:S(2)}) collective-permute-start(f32[6,8,128]{2,1,0:T(8,128)S(1)} %get-tuple-element.18), channel_id=1, source_target_pairs={{1,0},{2,1},{3,2},{4,259},{5,4},{6,5},{7,6},{65,64},{66,65},{67,66... | collective-permute-start | bytes 73736 | tf_op jit(solution)/shard_map/ppermute | solution.py:273
  65.4 0.0 collective-permute-done.2.above_ref
  65.4 7.7 %collective-permute-done.3.below_ref = f32[6,8,128]{2,1,0:T(8,128)S(1)} collective-permute-done((f32[6,8,128]{2,1,0:T(8,128)S(1)}, f32[6,8,128]{2,1,0:T(8,128)S(1)}, u32[]{:S(2)}, u32[]{:S(2)}) %collective-permute-start.3) | collective-permute-done | bytes 24608 | tf_op jit(solution)/shard_map/ppermute | solution.py:273
  73.1 0.3 shard_map.39
  73.4 17.3 %all_to_all.10 = s32[8,32,128]{2,1,0:T(8,128)} all-to-all(s32[8,32,128]{2,1,0:T(8,128)S(1)} %shard_map.39), channel_id=1, replica_groups=mesh['zl'=8,'x'=4,'c'=2,'zh'=2,'y'=4] {'zl'}, dimensions={0} | all-to-all | bytes 262144 | tf_op jit(solution)/shard_map/all_to_all | solution.py:282
  90.7 0.0 all-gather.3.cloned.1.call-update
  90.7 25.2 %all-gather.3.cloned.1.call-done = s32[64,32,128]{2,1,0:T(8,128)} async-done(((s32[8,32,128]{2,1,0:T(8,128)}), s32[64,32,128]{2,1,0:T(8,128)}) %all-gather.3.cloned.1.call-update) | async-done | bytes 1048592 | tf_op jit(solution)/shard_map/all_gather | solution.py:283
  115.9 0.0 copy-start
  115.9 1.2 copy-done
  117.1 2.1 %shard_map.40 = f32[3,3,48,1024]{3,2,1,0:T(8,128)} custom-call(s32[8,8,32,128]{3,2,1,0:T(8,128)S(1)} %bitcast.1), custom_call_target="tpu_custom_call" | custom-call | tf_op jit(solution)/shard_map/pallas_call | solution.py:285
Async XLA Ops:
  7.3 1.2 copy-start.1
  8.5 0.9 copy-start.2
  11.0 36.1 %all-to-all-start = ((bf16[64,16,128]{2,1,0:T(8,128)(2,1)}), bf16[64,16,128]{2,1,0:T(8,128)(2,1)S(1)}, u32[]{:S(2)}, u32[]{:S(2)}) async-start(bf16[64,16,128]{2,1,0:T(8,128)(2,1)} %get-tuple-element.12), calls=%async_computation | async-start | bytes 524288 | tf_op jit(solution)/shard_map/all_to_all | solution.py:251
  27.2 88.7 %all-gather.3.cloned.1.call-start = ((), (), s32[]{:S(2)}) async-start(), calls=%async_computation.2 | async-start | bytes 1179648 | tf_op jit(solution)/shard_map/all_gather | solution.py:283
  27.2 9.8 %collective-permute-start = (f32[6,8,128]{2,1,0:T(8,128)S(1)}, f32[6,8,128]{2,1,0:T(8,128)S(1)}, u32[]{:S(2)}, u32[]{:S(2)}) collective-permute-start(f32[6,8,128]{2,1,0:T(8,128)S(1)} %get-tuple-element.14), channel_id=1, source_target_pairs={{0,1},{1,2},{2,3},{3,260},{4,5},{5,6},{6,7},{64,65},{65,66},{66,67... | collective-permute-start | bytes 73736 | tf_op jit(solution)/shard_map/ppermute | solution.py:249
  35.1 10.6 %collective-permute-start.1 = (f32[6,8,128]{2,1,0:T(8,128)S(1)}, f32[6,8,128]{2,1,0:T(8,128)S(1)}, u32[]{:S(2)}, u32[]{:S(2)}) collective-permute-start(f32[6,8,128]{2,1,0:T(8,128)S(1)} %get-tuple-element.15), channel_id=1, source_target_pairs={{1,0},{2,1},{3,2},{4,259},{5,4},{6,5},{7,6},{65,64},{66,65},{67,66... | collective-permute-start | bytes 73736 | tf_op jit(solution)/shard_map/ppermute | solution.py:250
  60.1 5.3 %collective-permute-start.2 = (f32[6,8,128]{2,1,0:T(8,128)S(1)}, f32[6,8,128]{2,1,0:T(8,128)S(1)}, u32[]{:S(2)}, u32[]{:S(2)}) collective-permute-start(f32[6,8,128]{2,1,0:T(8,128)S(1)} %get-tuple-element.17), channel_id=1, source_target_pairs={{0,1},{1,2},{2,3},{3,260},{4,5},{5,6},{6,7},{64,65},{65,66},{66,67... | collective-permute-start | bytes 73736 | tf_op jit(solution)/shard_map/ppermute | solution.py:272
  62.5 10.6 %collective-permute-start.3 = (f32[6,8,128]{2,1,0:T(8,128)S(1)}, f32[6,8,128]{2,1,0:T(8,128)S(1)}, u32[]{:S(2)}, u32[]{:S(2)}) collective-permute-start(f32[6,8,128]{2,1,0:T(8,128)S(1)} %get-tuple-element.18), channel_id=1, source_target_pairs={{1,0},{2,1},{3,2},{4,259},{5,4},{6,5},{7,6},{65,64},{66,65},{67,66... | collective-permute-start | bytes 73736 | tf_op jit(solution)/shard_map/ppermute | solution.py:273
  115.9 1.2 copy-start
Sparse Core Ops, SparseCore 0:
  90.8 25.0 all-gather.2

commit v2 on v0

v2 whole, which is shorter than its diff:
```python
import jax
import jax.numpy as jnp
from jax import lax
from jax.experimental import pallas as pl
from jax.experimental.pallas import tpu as pltpu
from jax.sharding import Mesh, PartitionSpec as P

HALO = 8
SPAN = 2 * HALO + 1
TALL = 12
WIDE = 64
REGULAR = 0.05
CODE_STEPS = 5041.0
CODE_BASE = 7.0
WORDS = 30
F32 = jnp.float32
BF16 = jnp.bfloat16
I32 = jnp.int32
VIEW = ("zl", "x", "c")
ROW = ("zh", "y")
PARAMS = pltpu.CompilerParams(vmem_limit_bytes=48 * 1024 * 1024)


def lanes(rows):
    return lax.broadcasted_iota(I32, (rows, 128), 1)


def mirrored(q):
    return jnp.where(lax.rem(lax.axis_index("y"), 2) == 0, q, 3 - q)


def my_block():
    return lax.rem(lax.axis_index("zl") + 4 * lax.axis_index("zh"), 8)


def pack_kernel(target_ref, shifts_ref, chunks_ref, wide_ref):
    high = lax.axis_index("zh")
    lane = lanes(48)
    blocks = [target_ref[0, :, 128 * d : 128 * d + 128].astype(F32) for d in range(8)]
    zero = jnp.zeros((48, 128), F32)
    for d in range(8):
        left = blocks[d - 1] if d > 0 else zero
        right = blocks[d + 1] if d < 7 else zero
        mid = blocks[d]
        wide_ref[2 * d, :48] = pltpu.roll(jnp.where(lane >= 128 - HALO, left, mid), HALO, 1)
        wide_ref[2 * d + 1, :48] = pltpu.roll(jnp.where(lane < HALO, right, mid), 128 - 56, 1)
    lane = lanes(8)
    upper_half = lax.broadcasted_iota(I32, (8, 128), 0) < 4
    extra = jnp.zeros((8, 128), F32)
    for layer in range(3):
        for part in range(2):
            extra = jnp.where(
                lane == 120 + 2 * layer + part, shifts_ref[0, part, layer].astype(F32), extra
            )
    for q in range(4):
        x = mirrored(q)
        for d in range(8):
            zl = lax.rem(d + 4 * high, 8)
            for h in range(2):
                at = 2 * d + h
                main = wide_ref[at, TALL * q : TALL * q + 8]
                first = wide_ref[at, TALL * q + 8 : TALL * q + 16]
                second = wide_ref[at, TALL * q + 4 : TALL * q + 12]
                pieces = jnp.where(upper_half, pltpu.roll(first, 80, 1), pltpu.roll(second, 40, 1))
                chunk = jnp.where(lane < 80, main, jnp.where(lane < 120, pieces, extra))
                chunks_ref[(zl * 4 + x) * 2 + h] = chunk.astype(BF16)


def strip_kernel(layers_ref, own_ref, head_ref, tail_ref):
    half = lax.axis_index("c")
    block = my_block() - 1 + half
    amount = jnp.where(half == 0, 16, 80)
    left = pl.multiple_of(jnp.maximum(block, 0) * 128, 128)
    right = pl.multiple_of(jnp.minimum(block + 1, 7) * 128, 128)
    left_there = jnp.where(block >= 0, 1.0, 0.0)
    right_there = jnp.where(block + 1 <= 7, 1.0, 0.0)
    lane = lanes(48)
    for layer in range(3):
        for frame in range(3):
            a = layers_ref[frame, layer, :, pl.ds(left, 128)].astype(F32) * left_there
            b = layers_ref[frame, layer, :, pl.ds(right, 128)].astype(F32) * right_there
            cells = pltpu.roll(jnp.where(lane >= 128 - amount, a, b), amount, 1)
            own_ref[layer, frame] = cells
            head_ref[layer, frame] = cells[:HALO]
            tail_ref[layer, frame] = cells[48 - HALO :]


def seen_kernel(own_ref, above_ref, below_ref, seen_ref, tile_ref, tall_ref):
    q = mirrored(lax.axis_index("x"))
    start = q * TALL
    tall_ref[:, :, :HALO] = above_ref[...]
    tall_ref[:, :, HALO : HALO + 48] = own_ref[...]
    tall_ref[:, :, HALO + 48 : 64] = below_ref[...]
    tall_ref[:, :, 64:] = jnp.zeros((3, 3, 8, 128), F32)
    for layer in range(3):
        for frame in range(3):
            cells = tall_ref[layer, frame, pl.ds(start, 32), :]
            for d in range(SPAN):
                moved = pltpu.roll(cells, 128 - d, 1) if d else cells
                seen_ref[layer, d, frame] = moved
                if d == 16:
                    tile_ref[layer, frame] = moved[HALO : HALO + 16]


def view_kernel(
    recv_ref, seen_ref, own_out, up_out, down_out, image_ref, shift_ref, shift_smem, sem, *sums
):
    shift_ref[...] = recv_ref[:, 0, :].astype(F32).astype(I32)
    copy = pltpu.make_async_copy(shift_ref, shift_smem, sem)
    copy.start()

    lane = lanes(8)
    upper_half = lax.broadcasted_iota(I32, (8, 128), 0) < 4
    for view in range(64):
        cells = recv_ref[view].astype(F32)
        image_ref[view, :8] = cells
        low = pltpu.roll(cells, 128 - 80, 1)
        high = pltpu.roll(pltpu.roll(cells, 128 - 40, 1), 4, 0)
        rest = jnp.where(lane < 40, low, high)
        image_ref[view, 8:] = jnp.where(upper_half, rest, 0.0)

    for ref in sums:
        ref[...] = jnp.zeros_like(ref)

    column = my_block() * 128 + lax.axis_index("c") * WIDE - HALO + lanes(16)
    inside = (column >= 0) & (column < 1024)
    inside = inside & (lax.broadcasted_iota(I32, (16, 128), 0) < TALL)
    third = jnp.where(inside, 1.0 / 3.0, 0.0)
    copy.wait()

    def one_view(view, carry):
        rows = [shift_smem[view, 120 + 2 * layer] + HALO for layer in range(3)]
        cols = [shift_smem[view, 121 + 2 * layer] + HALO for layer in range(3)]
        s0, s1, s2 = (
            seen_ref[layer, cols[layer], :, pl.ds(rows[layer], 16), :] for layer in range(3)
        )
        p01 = s0 * s1
        whole = p01 * s2
        shown = (whole[0] + whole[1] + whole[2]) * third
        image = image_ref[view]
        for layer, others in enumerate((s1 * s2, s0 * s2, p01)):
            for which, factor in enumerate((image, shown)):
                sums[2 * layer + which][cols[layer], :, pl.ds(rows[layer], 16), :] += factor * others
        return carry

    lax.fori_loop(0, 64, one_view, 0)

    lane = lanes(32)
    for layer in range(3):
        for frame in range(3):
            sides = []
            for which, base in enumerate((-16, 48)):
                total = None
                for d in range(SPAN):
                    amount = (d + base) % 128
                    cells = sums[2 * layer + which][d, frame]
                    moved = pltpu.roll(cells, amount, 1) if amount else cells
                    total = moved if total is None else total + moved
                sides.append(total)
            both = jnp.where(lane < WIDE, sides[0], sides[1])
            up_out[layer, frame] = both[:HALO]
            own_out[layer, frame] = both[HALO : HALO + 16]
            down_out[layer, frame] = both[HALO + TALL : 2 * HALO + TALL]


def update_kernel(own_ref, above_ref, below_ref, tile_ref, out_ref, code_ref):
    lane = lanes(TALL)
    for layer in range(3):
        for frame in range(3):
            own = own_ref[layer, frame]
            above = above_ref[layer, frame]
            below = below_ref[layer, frame]
            none = jnp.zeros((4, 128), F32)
            both = own[:TALL] + jnp.concatenate([above, none], axis=0)
            both = both + jnp.concatenate([none, below], axis=0)
            lower = pltpu.roll(both, WIDE, 1)
            value = tile_ref[layer, frame, :TALL] * (both + REGULAR) / (lower + REGULAR)
            scaled = (jnp.log2(value) + CODE_BASE) * CODE_STEPS + 0.5
            code_ref[frame * 3 + layer, :TALL] = jnp.clip(scaled, 0.0, 65535.0).astype(I32)
    for pair in range(2):
        parts = []
        for p in (pair, pair + 2):
            even = code_ref[2 * p, :TALL]
            odd = pltpu.roll(code_ref[2 * p + 1, :TALL], WIDE, 1)
            parts.append(jnp.where(lane < WIDE, even, odd))
        word = parts[0] + (parts[1] - 32768) * 65536
        for copy in range(8):
            out_ref[copy, TALL * pair : TALL * pair + TALL] = word
    word = code_ref[8, :6] + (code_ref[8, 6:12] - 32768) * 65536
    for copy in range(8):
        out_ref[copy, 24:30] = word
        out_ref[copy, 30:] = jnp.zeros((2, 128), I32)


def dense_kernel(words_ref, out_ref):
    for zl in range(8):
        out_ref[WORDS * zl : WORDS * zl + WORDS] = words_ref[zl, :WORDS]


def decoded(code):
    return jnp.exp2(code.astype(F32) * (1.0 / CODE_STEPS) - CODE_BASE)


def spread_kernel(words_ref, out_ref):
    zl = lax.rem(pl.program_id(0) + 4 * lax.axis_index("zh"), 8)
    for q in range(4):
        x = mirrored(q)
        rows = slice(TALL * q, TALL * q + TALL)

        def words(c, first, count):
            return words_ref[x * 2 + c, pl.ds(zl * WORDS + first, count), :]

        lane = lanes(TALL)
        for pair in range(2):
            a, b = words(0, TALL * pair, TALL), words(1, TALL * pair, TALL)
            even = jnp.where(lane < WIDE, a, pltpu.roll(b, WIDE, 1))
            odd = jnp.where(lane < WIDE, pltpu.roll(a, WIDE, 1), b)
            for side, word in enumerate((even, odd)):
                for p, code in ((pair, word & 65535), (pair + 2, (word >> 16) + 32768)):
                    at = 2 * p + side
                    out_ref[at // 3, at % 3, rows] = decoded(code)
        a, b = words(0, 24, 6), words(1, 24, 6)
        word = jnp.where(lanes(6) < WIDE, a, pltpu.roll(b, WIDE, 1))
        out_ref[2, 2, TALL * q : TALL * q + 6] = decoded(word & 65535)
        out_ref[2, 2, TALL * q + 6 : TALL * q + TALL] = decoded((word >> 16) + 32768)


def row_pairs(step):
    pairs = []
    for zl in range(8):
        for at in range(8):
            to = at + step
            if 0 <= to < 8:
                other = (zl + 4 * (at // 4 != to // 4)) % 8
                pairs.append(((zl * 2 + at // 4) * 4 + at % 4, (other * 2 + to // 4) * 4 + to % 4))
    return pairs


def strip_pairs(step):
    def index(block, strip):
        at, q = strip // 4, strip % 4
        x = q if at % 2 == 0 else 3 - q
        zl = (block + 4 * (at // 4)) % 8
        return ((zl * 4 + x) * 2 + at // 4) * 4 + at % 4

    return [
        (index(block, strip), index(block, strip + step))
        for block in range(8)
        for strip in range(32)
        if 0 <= strip + step < 32
    ]


VMEM = pl.BlockSpec(memory_space=pltpu.VMEM)
SMEM = pl.BlockSpec(memory_space=pltpu.SMEM)


def call(kernel, outs, ins, scratch=(), **more):
    return pl.pallas_call(
        kernel,
        out_shape=tuple(jax.ShapeDtypeStruct(*out) for out in outs),
        in_specs=ins,
        out_specs=(VMEM,) * len(outs),
        scratch_shapes=scratch,
        compiler_params=PARAMS,
        **more,
    )


def body(layers, target, shifts):
    (chunks,) = call(
        pack_kernel,
        [((64, 8, 128), BF16)],
        [VMEM, SMEM],
        [pltpu.VMEM((16, 56, 128), F32)],
    )(target, shifts.transpose(0, 2, 1))
    received = lax.all_to_all(chunks, VIEW, 0, 0)

    own, head, tail = call(
        strip_kernel,
        [((3, 3, 48, 128), F32), ((3, 3, HALO, 128), F32), ((3, 3, HALO, 128), F32)],
        [VMEM],
    )(layers)
    across = ("zl", "zh", "y")
    above = lax.ppermute(tail, across, row_pairs(1))
    below = lax.ppermute(head, across, row_pairs(-1))
    seen, tile = call(
        seen_kernel,
        [((3, SPAN, 3, 32, 128), F32), ((3, 3, 16, 128), F32)],
        [VMEM] * 3,
        [pltpu.VMEM((3, 3, 72, 128), F32)],
    )(own, above, below)

    sums, up, down = call(
        view_kernel,
        [((3, 3, 16, 128), F32), ((3, 3, HALO, 128), F32), ((3, 3, HALO, 128), F32)],
        [VMEM] * 2,
        [
            pltpu.VMEM((64, 16, 128), F32),
            pltpu.VMEM((64, 128), I32),
            pltpu.SMEM((64, 128), I32),
            pltpu.SemaphoreType.DMA,
        ]
        + [pltpu.VMEM((SPAN, 3, 32, 128), F32)] * 6,
    )(received, seen)
    across = ("zl", "x", "zh", "y")
    from_above = lax.ppermute(down, across, strip_pairs(1))
    from_below = lax.ppermute(up, across, strip_pairs(-1))

    (words,) = call(
        update_kernel,
        [((8, 32, 128), I32)],
        [VMEM] * 4,
        [pltpu.VMEM((9, 16, 128), I32)],
    )(sums, from_above, from_below, tile)
    words = lax.all_to_all(words, "zl", 0, 0)
    (words,) = call(dense_kernel, [((8 * WORDS, 128), I32)], [VMEM])(words)
    words = lax.all_gather(words, ("x", "c"))

    return pl.pallas_call(
        spread_kernel,
        grid=(8,),
        out_shape=jax.ShapeDtypeStruct((3, 3, 48, 1024), F32),
        in_specs=[pl.BlockSpec((8, 8 * WORDS, 128), lambda d: (0, 0, 0))],
        out_specs=pl.BlockSpec((3, 3, 48, 128), lambda d: (0, 0, 0, d)),
        compiler_params=PARAMS,
    )(words)


def solution(mesh):
    fine = Mesh(mesh.devices.reshape(8, 4, 2, 2, 4), ("zl", "x", "c", "zh", "y"))
    placed = (P(None, None, ROW, None), P(VIEW, ROW, None), P(VIEW, None, None))
    return jax.shard_map(
        body, mesh=fine, in_specs=placed, out_specs=P(None, None, ROW, None), check_vma=False
    )
```

time: 972 us -> 95.6 us (0.10)
  waiting for transfers between devices: 890 us -> 16.2 us
  blocking collectives: 0 us -> 34.4 us
  between operations: 28.3 us -> 0.11 us
  other arithmetic: 17.1 us -> 0 us
  Pallas kernels: 0 us -> 10.5 us
    psum x1 -> x0, waiting for transfers between devices: 867 us -> none  [body(): upper_all, lower_all = lax.psum((upper, lower), 'view')]
    all_to_all x0 -> x1, blocking collectives: none -> 18.2 us  [body(): words = lax.all_to_all(words, 'zl', 0, 0)]
    all_to_all x0 -> x1, starting transfers between devices: none -> 16.2 us  [body(): received = lax.all_to_all(chunks, VIEW, 0, 0)]
    all_gather x0 -> x1, blocking collectives: none -> 16.1 us  [body(): words = lax.all_gather(words, ('x', 'c'))]
    ppermute x4, starting transfers between devices: 27.8 us -> 15.1 us  [the longest x1 7.9 us: body(): above = lax.ppermute(tail, across, row_pairs(1))]
    pallas_call x0 -> x7, Pallas kernels: none -> 10.5 us  [the longest x1 4.55 us: body(): call(view_kernel, [((3, 3, 16, 128), F32), ((3, 3, HALO, 128), F32), ((3,...]
  transfers between devices with their start and end apart: 5 -> 5, of which waited for: 4 -> 2; matrix products, arithmetic and copies ran while one was open for 0% -> 0% of each run, Pallas kernels for 0% -> 1%
where the time goes in v2:
time: 95.6 us; the launch traced here: 95.2 us
  blocking collectives  34.4 us (36%)
  starting transfers between devices  31.3 us (33%)
  waiting for transfers between devices  16.2 us (17%)
  Pallas kernels  10.5 us (11%)
  local copies, waits for them, and re-layouts  2.73 us (3%)
    all_to_all x1, blocking collectives, body(): words = lax.all_to_all(words, 'zl', 0, 0)  18.2 us
    all_to_all x1, starting transfers between devices, body(): received = lax.all_to_all(chunks, VIEW, 0, 0)  16.2 us
    all_gather x1, blocking collectives, body(): words = lax.all_gather(words, ('x', 'c'))  16.1 us
    ppermute x1, waiting for transfers between devices, body(): below = lax.ppermute(head, across, row_pairs(-1))  8.87 us
    ppermute x1, starting transfers between devices, body(): above = lax.ppermute(tail, across, row_pairs(1))  7.9 us
    ppermute x1, waiting for transfers between devices, body(): from_below = lax.ppermute(up, across, strip_pairs(-1))  7.34 us
    pallas_call x1, Pallas kernels, body(): call(view_kernel, [((3, 3, 16, 128), F32), ((3, 3, HALO, 128), F32), ((3,...  4.55 us
    pallas_call x1, Pallas kernels, body(): pl.pallas_call(spread_kernel, grid=(8,), out_shape=jax.ShapeDtypeStruct((...  3.44 us
  transfers between devices with their start and end apart: 5, of which 2 were waited for; matrix products, arithmetic and copies ran while one was open for 0% of the time, Pallas kernels for 1%

profile of v2, /device:TPU:25, one launch (start us, length us, event | category | flops | bytes accessed | tf_op | source)
XLA Modules:
  0.0 95.2 jit_solution(11342578813653098797)
XLA Ops:
  0.0 0.0 copy-start.1
  0.0 0.9 copy-done.1
  0.9 0.0 copy-start.2
  0.9 0.7 copy-done.2
  1.6 1.5 %shard_map.37 = bf16[64,8,128]{2,1,0:T(8,128)(2,1)} custom-call(bf16[1,48,1024]{2,1,0:T(8,128)(2,1)S(1)} %copy-done.1, s32[1,2,3]{2,1,0:T(2,128)S(1)} %bitcast.3), custom_call_target="tpu_custom_call" | custom-call | tf_op jit(solution)/shard_map/pallas_call | solution.py:271
  3.0 16.2 %all-to-all-start = ((bf16[64,8,128]{2,1,0:T(8,128)(2,1)}), bf16[64,8,128]{2,1,0:T(8,128)(2,1)S(1)}, u32[]{:S(2)}, u32[]{:S(2)}) async-start(bf16[64,8,128]{2,1,0:T(8,128)(2,1)} %shard_map.37), calls=%async_computation | async-start | bytes 262144 | tf_op jit(solution)/shard_map/all_to_all | solution.py:277
  19.3 0.0 copy-start
  19.3 1.2 %copy-done = bf16[3,3,48,1024]{3,2,1,0:T(8,128)(2,1)S(1)} copy-done((bf16[3,3,48,1024]{3,2,1,0:T(8,128)(2,1)S(1)}, bf16[3,3,48,1024]{3,2,1,0:T(8,128)(2,1)}, u32[]{:S(2)}) %copy-start) | copy-done | bytes 884760
  20.4 0.1 shard_map.38
  20.6 7.9 %collective-permute-start = (f32[3,3,8,128]{3,2,1,0:T(8,128)S(1)}, f32[3,3,8,128]{3,2,1,0:T(8,128)S(1)}, u32[]{:S(2)}, u32[]{:S(2)}) collective-permute-start(f32[3,3,8,128]{3,2,1,0:T(8,128)S(1)} %get-tuple-element.14), channel_id=1, source_target_pairs={{0,1},{1,2},{2,3},{3,260},{4,5},{5,6},{6,7},{64,65},{65,66},{66,67... | collective-permute-start | bytes 110600 | tf_op jit(solution)/shard_map/ppermute | solution.py:285
  28.5 1.9 %collective-permute-start.1 = (f32[3,3,8,128]{3,2,1,0:T(8,128)S(1)}, f32[3,3,8,128]{3,2,1,0:T(8,128)S(1)}, u32[]{:S(2)}, u32[]{:S(2)}) collective-permute-start(f32[3,3,8,128]{3,2,1,0:T(8,128)S(1)} %get-tuple-element.15), channel_id=1, source_target_pairs={{1,0},{2,1},{3,2},{4,259},{5,4},{6,5},{7,6},{65,64},{66,65},{67,66... | collective-permute-start | bytes 110600 | tf_op jit(solution)/shard_map/ppermute | solution.py:286
  30.4 0.0 collective-permute-done.above_ref
  30.4 8.9 %collective-permute-done.1.below_ref = f32[3,3,8,128]{3,2,1,0:T(8,128)S(1)} collective-permute-done((f32[3,3,8,128]{3,2,1,0:T(8,128)S(1)}, f32[3,3,8,128]{3,2,1,0:T(8,128)S(1)}, u32[]{:S(2)}, u32[]{:S(2)}) %collective-permute-start.1) | collective-permute-done | bytes 36896 | tf_op jit(solution)/shard_map/ppermute | solution.py:286
  39.3 0.7 shard_map.39
  40.0 0.0 all-to-all-done.recv_ref
  40.0 4.6 %shard_map.40 = (f32[3,3,16,128]{3,2,1,0:T(8,128)S(1)}, f32[3,3,8,128]{3,2,1,0:T(8,128)S(1)}, f32[3,3,8,128]{3,2,1,0:T(8,128)S(1)}) custom-call(bf16[64,8,128]{2,1,0:T(8,128)(2,1)S(1)} %all-to-all-done.recv_ref, f32[3,17,3,32,128]{4,3,2,1,0:T(8,128)S(1)} %get-tuple-element.16.seen_ref), custom_call_target="tpu_custom_call" | custom-call | tf_op jit(solution)/shard_map/pallas_call | solution.py:294
  44.6 1.9 %collective-permute-start.2 = (f32[3,3,8,128]{3,2,1,0:T(8,128)S(1)}, f32[3,3,8,128]{3,2,1,0:T(8,128)S(1)}, u32[]{:S(2)}, u32[]{:S(2)}) collective-permute-start(f32[3,3,8,128]{3,2,1,0:T(8,128)S(1)} %get-tuple-element.18), channel_id=1, source_target_pairs={{0,16},{16,32},{32,48},{48,49},{49,33},{33,17},{17,1},{1,2},{2,18}... | collective-permute-start | bytes 110600 | tf_op jit(solution)/shard_map/ppermute | solution.py:307
  46.5 3.4 %collective-permute-start.3 = (f32[3,3,8,128]{3,2,1,0:T(8,128)S(1)}, f32[3,3,8,128]{3,2,1,0:T(8,128)S(1)}, u32[]{:S(2)}, u32[]{:S(2)}) collective-permute-start(f32[3,3,8,128]{3,2,1,0:T(8,128)S(1)} %get-tuple-element.19), channel_id=1, source_target_pairs={{16,0},{32,16},{48,32},{49,48},{33,49},{17,33},{1,17},{2,1},{18,2}... | collective-permute-start | bytes 110600 | tf_op jit(solution)/shard_map/ppermute | solution.py:308
  49.9 0.0 collective-permute-done.2.above_ref
  49.9 7.3 %collective-permute-done.3.below_ref = f32[3,3,8,128]{3,2,1,0:T(8,128)S(1)} collective-permute-done((f32[3,3,8,128]{3,2,1,0:T(8,128)S(1)}, f32[3,3,8,128]{3,2,1,0:T(8,128)S(1)}, u32[]{:S(2)}, u32[]{:S(2)}) %collective-permute-start.3) | collective-permute-done | bytes 36896 | tf_op jit(solution)/shard_map/ppermute | solution.py:308
  57.2 0.2 shard_map.41
  57.4 18.2 %all_to_all.10.words_ref = s32[8,32,128]{2,1,0:T(8,128)S(1)} all-to-all(s32[8,32,128]{2,1,0:T(8,128)S(1)} %shard_map.41), channel_id=1, replica_groups=mesh['zl'=8,'x'=4,'c'=2,'zh'=2,'y'=4] {'zl'}, dimensions={0} | all-to-all | bytes 262144 | tf_op jit(solution)/shard_map/all_to_all | solution.py:316
  75.6 16.1 %all-gather = s32[1920,128]{1,0:T(8,128)S(1)} all-gather(s32[240,128]{1,0:T(8,128)S(1)} %shard_map.42), channel_id=2, replica_groups=mesh['zl'=8,'x'=4,'c'=2,'zh'=2,'y'=4] {'x','c'}, dimensions={0}, use_global_device_ids=true | all-gather | bytes 1105920 | tf_op jit(solution)/shard_map/all_gather | solution.py:318
  91.8 3.4 %shard_map.43 = f32[3,3,48,1024]{3,2,1,0:T(8,128)} custom-call(s32[8,240,128]{2,1,0:T(8,128)S(1)} %bitcast.2), custom_call_target="tpu_custom_call" | custom-call | tf_op jit(solution)/shard_map/pallas_call | solution.py:320
  (1 shorter events, 0.0 us)
Async XLA Ops:
  0.0 0.9 copy-start.1
  0.9 0.7 copy-start.2
  3.0 37.0 %all-to-all-start = ((bf16[64,8,128]{2,1,0:T(8,128)(2,1)}), bf16[64,8,128]{2,1,0:T(8,128)(2,1)S(1)}, u32[]{:S(2)}, u32[]{:S(2)}) async-start(bf16[64,8,128]{2,1,0:T(8,128)(2,1)} %shard_map.37), calls=%async_computation | async-start | bytes 262144 | tf_op jit(solution)/shard_map/all_to_all | solution.py:277
  19.3 1.2 %copy-start = (bf16[3,3,48,1024]{3,2,1,0:T(8,128)(2,1)S(1)}, bf16[3,3,48,1024]{3,2,1,0:T(8,128)(2,1)}, u32[]{:S(2)}) copy-start(bf16[3,3,48,1024]{3,2,1,0:T(8,128)(2,1)} %layers_ref.1) | copy-start | bytes 2654212
  20.6 9.8 %collective-permute-start = (f32[3,3,8,128]{3,2,1,0:T(8,128)S(1)}, f32[3,3,8,128]{3,2,1,0:T(8,128)S(1)}, u32[]{:S(2)}, u32[]{:S(2)}) collective-permute-start(f32[3,3,8,128]{3,2,1,0:T(8,128)S(1)} %get-tuple-element.14), channel_id=1, source_target_pairs={{0,1},{1,2},{2,3},{3,260},{4,5},{5,6},{6,7},{64,65},{65,66},{66,67... | collective-permute-start | bytes 110600 | tf_op jit(solution)/shard_map/ppermute | solution.py:285
  28.5 10.8 %collective-permute-start.1 = (f32[3,3,8,128]{3,2,1,0:T(8,128)S(1)}, f32[3,3,8,128]{3,2,1,0:T(8,128)S(1)}, u32[]{:S(2)}, u32[]{:S(2)}) collective-permute-start(f32[3,3,8,128]{3,2,1,0:T(8,128)S(1)} %get-tuple-element.15), channel_id=1, source_target_pairs={{1,0},{2,1},{3,2},{4,259},{5,4},{6,5},{7,6},{65,64},{66,65},{67,66... | collective-permute-start | bytes 110600 | tf_op jit(solution)/shard_map/ppermute | solution.py:286
  44.6 5.3 %collective-permute-start.2 = (f32[3,3,8,128]{3,2,1,0:T(8,128)S(1)}, f32[3,3,8,128]{3,2,1,0:T(8,128)S(1)}, u32[]{:S(2)}, u32[]{:S(2)}) collective-permute-start(f32[3,3,8,128]{3,2,1,0:T(8,128)S(1)} %get-tuple-element.18), channel_id=1, source_target_pairs={{0,16},{16,32},{32,48},{48,49},{49,33},{33,17},{17,1},{1,2},{2,18}... | collective-permute-start | bytes 110600 | tf_op jit(solution)/shard_map/ppermute | solution.py:307
  46.5 10.7 %collective-permute-start.3 = (f32[3,3,8,128]{3,2,1,0:T(8,128)S(1)}, f32[3,3,8,128]{3,2,1,0:T(8,128)S(1)}, u32[]{:S(2)}, u32[]{:S(2)}) collective-permute-start(f32[3,3,8,128]{3,2,1,0:T(8,128)S(1)} %get-tuple-element.19), channel_id=1, source_target_pairs={{16,0},{32,16},{48,32},{49,48},{33,49},{17,33},{1,17},{2,1},{18,2}... | collective-permute-start | bytes 110600 | tf_op jit(solution)/shard_map/ppermute | solution.py:308

commit v3 on v2

--- a/solution.py
+++ b/solution.py
@@ -66,7 +66,8 @@
                 chunks_ref[(zl * 4 + x) * 2 + h] = chunk.astype(BF16)
 
 
-def strip_kernel(layers_ref, own_ref, head_ref, tail_ref):
+def strip_kernel(layers_ref, own_ref, edge_ref):
+    last = mirrored(lax.axis_index("x")) == 3
     half = lax.axis_index("c")
     block = my_block() - 1 + half
     amount = jnp.where(half == 0, 16, 80)
@@ -81,16 +82,15 @@
             b = layers_ref[frame, layer, :, pl.ds(right, 128)].astype(F32) * right_there
             cells = pltpu.roll(jnp.where(lane >= 128 - amount, a, b), amount, 1)
             own_ref[layer, frame] = cells
-            head_ref[layer, frame] = cells[:HALO]
-            tail_ref[layer, frame] = cells[48 - HALO :]
-
-
-def seen_kernel(own_ref, above_ref, below_ref, seen_ref, tile_ref, tall_ref):
+            edge_ref[layer, frame] = jnp.where(last, cells[48 - HALO :], cells[:HALO])
+
+
+def seen_kernel(own_ref, edge_ref, seen_ref, tile_ref, tall_ref):
     q = mirrored(lax.axis_index("x"))
     start = q * TALL
-    tall_ref[:, :, :HALO] = above_ref[...]
+    tall_ref[:, :, :HALO] = edge_ref[...]
     tall_ref[:, :, HALO : HALO + 48] = own_ref[...]
-    tall_ref[:, :, HALO + 48 : 64] = below_ref[...]
+    tall_ref[:, :, HALO + 48 : 64] = edge_ref[...]
     tall_ref[:, :, 64:] = jnp.zeros((3, 3, 8, 128), F32)
     for layer in range(3):
         for frame in range(3):
@@ -103,7 +103,7 @@
 
 
 def view_kernel(
-    recv_ref, seen_ref, own_out, up_out, down_out, image_ref, shift_ref, shift_smem, sem, *sums
+    recv_ref, seen_ref, own_out, near_out, far_out, image_ref, shift_ref, shift_smem, sem, *sums
 ):
     shift_ref[...] = recv_ref[:, 0, :].astype(F32).astype(I32)
     copy = pltpu.make_async_copy(shift_ref, shift_smem, sem)
@@ -145,6 +145,7 @@
 
     lax.fori_loop(0, 64, one_view, 0)
 
+    even = lax.rem(mirrored(lax.axis_index("x")), 2) == 0
     lane = lanes(32)
     for layer in range(3):
         for frame in range(3):
@@ -158,18 +159,23 @@
                     total = moved if total is None else total + moved
                 sides.append(total)
             both = jnp.where(lane < WIDE, sides[0], sides[1])
-            up_out[layer, frame] = both[:HALO]
             own_out[layer, frame] = both[HALO : HALO + 16]
-            down_out[layer, frame] = both[HALO + TALL : 2 * HALO + TALL]
-
-
-def update_kernel(own_ref, above_ref, below_ref, tile_ref, out_ref, code_ref):
+            up = both[:HALO]
+            down = both[HALO + TALL : 2 * HALO + TALL]
+            near_out[layer, frame] = jnp.where(even, down, up)
+            far_out[layer, frame] = jnp.where(even, up, down)
+
+
+def update_kernel(own_ref, near_ref, far_ref, tile_ref, out_ref, code_ref):
     lane = lanes(TALL)
+    even = lax.rem(mirrored(lax.axis_index("x")), 2) == 0
     for layer in range(3):
         for frame in range(3):
             own = own_ref[layer, frame]
-            above = above_ref[layer, frame]
-            below = below_ref[layer, frame]
+            near = near_ref[layer, frame]
+            far = far_ref[layer, frame]
+            above = jnp.where(even, far, near)
+            below = jnp.where(even, near, far)
             none = jnp.zeros((4, 128), F32)
             both = own[:TALL] + jnp.concatenate([above, none], axis=0)
             both = both + jnp.concatenate([none, below], axis=0)
@@ -201,54 +207,56 @@
     return jnp.exp2(code.astype(F32) * (1.0 / CODE_STEPS) - CODE_BASE)
 
 
-def spread_kernel(words_ref, out_ref):
-    zl = lax.rem(pl.program_id(0) + 4 * lax.axis_index("zh"), 8)
-    for q in range(4):
-        x = mirrored(q)
-        rows = slice(TALL * q, TALL * q + TALL)
-
-        def words(c, first, count):
-            return words_ref[x * 2 + c, pl.ds(zl * WORDS + first, count), :]
-
-        lane = lanes(TALL)
-        for pair in range(2):
-            a, b = words(0, TALL * pair, TALL), words(1, TALL * pair, TALL)
-            even = jnp.where(lane < WIDE, a, pltpu.roll(b, WIDE, 1))
-            odd = jnp.where(lane < WIDE, pltpu.roll(a, WIDE, 1), b)
-            for side, word in enumerate((even, odd)):
-                for p, code in ((pair, word & 65535), (pair + 2, (word >> 16) + 32768)):
-                    at = 2 * p + side
-                    out_ref[at // 3, at % 3, rows] = decoded(code)
-        a, b = words(0, 24, 6), words(1, 24, 6)
-        word = jnp.where(lanes(6) < WIDE, a, pltpu.roll(b, WIDE, 1))
-        out_ref[2, 2, TALL * q : TALL * q + 6] = decoded(word & 65535)
-        out_ref[2, 2, TALL * q + 6 : TALL * q + TALL] = decoded((word >> 16) + 32768)
-
-
-def row_pairs(step):
-    pairs = []
-    for zl in range(8):
-        for at in range(8):
-            to = at + step
-            if 0 <= to < 8:
-                other = (zl + 4 * (at // 4 != to // 4)) % 8
-                pairs.append(((zl * 2 + at // 4) * 4 + at % 4, (other * 2 + to // 4) * 4 + to % 4))
-    return pairs
-
-
-def strip_pairs(step):
+def spread_kernel(words_ref, out_ref, block_ref, sems):
+    high = lax.axis_index("zh")
+
+    def sent(d):
+        columns = pl.ds(pl.multiple_of(d * 128, 128), 128)
+        return pltpu.make_async_copy(block_ref.at[d], out_ref.at[:, :, :, columns], sems.at[d])
+
+    def one(d, carry):
+        zl = lax.rem(d + 4 * high, 8)
+        for q in range(4):
+            x = mirrored(q)
+            rows = slice(TALL * q, TALL * q + TALL)
+
+            def words(c, first, count):
+                return words_ref[x * 2 + c, pl.ds(zl * WORDS + first, count), :]
+
+            lane = lanes(TALL)
+            for pair in range(2):
+                a, b = words(0, TALL * pair, TALL), words(1, TALL * pair, TALL)
+                even = jnp.where(lane < WIDE, a, pltpu.roll(b, WIDE, 1))
+                odd = jnp.where(lane < WIDE, pltpu.roll(a, WIDE, 1), b)
+                for side, word in enumerate((even, odd)):
+                    for p, code in ((pair, word & 65535), (pair + 2, (word >> 16) + 32768)):
+                        at = 2 * p + side
+                        block_ref[d, at // 3, at % 3, rows] = decoded(code)
+            a, b = words(0, 24, 6), words(1, 24, 6)
+            word = jnp.where(lanes(6) < WIDE, a, pltpu.roll(b, WIDE, 1))
+            block_ref[d, 2, 2, TALL * q : TALL * q + 6] = decoded(word & 65535)
+            block_ref[d, 2, 2, TALL * q + 6 : TALL * q + TALL] = decoded((word >> 16) + 32768)
+        sent(d).start()
+        return carry
+
+    lax.fori_loop(0, 8, one, 0)
+    for d in range(8):
+        sent(d).wait()
+
+
+def strip_pairs(first, step):
     def index(block, strip):
         at, q = strip // 4, strip % 4
         x = q if at % 2 == 0 else 3 - q
         zl = (block + 4 * (at // 4)) % 8
         return ((zl * 4 + x) * 2 + at // 4) * 4 + at % 4
 
-    return [
-        (index(block, strip), index(block, strip + step))
-        for block in range(8)
-        for strip in range(32)
-        if 0 <= strip + step < 32
-    ]
+    pairs = []
+    for block in range(8):
+        for strip in range(first, 31, step):
+            a, b = index(block, strip), index(block, strip + 1)
+            pairs += [(a, b), (b, a)]
+    return pairs
 
 
 VMEM = pl.BlockSpec(memory_space=pltpu.VMEM)
@@ -276,22 +284,21 @@
     )(target, shifts.transpose(0, 2, 1))
     received = lax.all_to_all(chunks, VIEW, 0, 0)
 
-    own, head, tail = call(
+    own, edge = call(
         strip_kernel,
-        [((3, 3, 48, 128), F32), ((3, 3, HALO, 128), F32), ((3, 3, HALO, 128), F32)],
+        [((3, 3, 48, 128), F32), ((3, 3, HALO, 128), F32)],
         [VMEM],
     )(layers)
-    across = ("zl", "zh", "y")
-    above = lax.ppermute(tail, across, row_pairs(1))
-    below = lax.ppermute(head, across, row_pairs(-1))
+    across = ("zl", "x", "zh", "y")
+    edge = lax.ppermute(edge, across, strip_pairs(3, 4))
     seen, tile = call(
         seen_kernel,
         [((3, SPAN, 3, 32, 128), F32), ((3, 3, 16, 128), F32)],
-        [VMEM] * 3,
+        [VMEM] * 2,
         [pltpu.VMEM((3, 3, 72, 128), F32)],
-    )(own, above, below)
-
-    sums, up, down = call(
+    )(own, edge)
+
+    sums, near, far = call(
         view_kernel,
         [((3, 3, 16, 128), F32), ((3, 3, HALO, 128), F32), ((3, 3, HALO, 128), F32)],
         [VMEM] * 2,
@@ -303,26 +310,25 @@
         ]
         + [pltpu.VMEM((SPAN, 3, 32, 128), F32)] * 6,
     )(received, seen)
-    across = ("zl", "x", "zh", "y")
-    from_above = lax.ppermute(down, across, strip_pairs(1))
-    from_below = lax.ppermute(up, across, strip_pairs(-1))
+    near = lax.ppermute(near, across, strip_pairs(0, 2))
+    far = lax.ppermute(far, across, strip_pairs(1, 2))
 
     (words,) = call(
         update_kernel,
         [((8, 32, 128), I32)],
         [VMEM] * 4,
         [pltpu.VMEM((9, 16, 128), I32)],
-    )(sums, from_above, from_below, tile)
+    )(sums, near, far, tile)
     words = lax.all_to_all(words, "zl", 0, 0)
     (words,) = call(dense_kernel, [((8 * WORDS, 128), I32)], [VMEM])(words)
     words = lax.all_gather(words, ("x", "c"))
 
     return pl.pallas_call(
         spread_kernel,
-        grid=(8,),
         out_shape=jax.ShapeDtypeStruct((3, 3, 48, 1024), F32),
-        in_specs=[pl.BlockSpec((8, 8 * WORDS, 128), lambda d: (0, 0, 0))],
-        out_specs=pl.BlockSpec((3, 3, 48, 128), lambda d: (0, 0, 0, d)),
+        in_specs=[VMEM],
+        out_specs=pl.BlockSpec(memory_space=pl.ANY),
+        scratch_shapes=[pltpu.VMEM((8, 3, 3, 48, 128), F32), pltpu.SemaphoreType.DMA((8,))],
         compiler_params=PARAMS,
     )(words)
 

time: 95.6 us -> 88.9 us (0.930)
  waiting for transfers between devices: 16.2 us -> 9.5 us
  Pallas kernels: 10.5 us -> 8.95 us
    ppermute x4 -> x3, waiting for transfers between devices: 16.2 us -> 8.38 us  [the longest x1 4.79 us: body(): far = lax.ppermute(far, across, strip_pairs(1, 2))]
    pallas_call x2, Pallas kernels: 3.59 us -> 2.02 us  [the longest x1 1.88 us: body(): pl.pallas_call(spread_kernel, out_shape=jax.ShapeDtypeStruct((3, 3, 48, 1...]
    all_gather x1, blocking collectives: 16.1 us -> 17.6 us  [body(): words = lax.all_gather(words, ('x', 'c'))]
    all_to_all x1, waiting for transfers between devices: 0.01 us -> 1.12 us  [body(): received = lax.all_to_all(chunks, VIEW, 0, 0)]
    ppermute x4 -> x3, starting transfers between devices: 15.1 us -> 15.8 us  [the longest x1 7.9 us: body(): edge = lax.ppermute(edge, across, strip_pairs(3, 4))]
  transfers between devices with their start and end apart: 5 -> 4, of which waited for: 2 -> 3; matrix products, arithmetic and copies ran while one was open for 0% -> 0% of each run, Pallas kernels for 1% -> 1%
where the time goes in v3:
time: 88.9 us; the launch traced here: 88.6 us
  blocking collectives  35.3 us (40%)
  starting transfers between devices  32.1 us (36%)
  waiting for transfers between devices  9.5 us (11%)
  Pallas kernels  8.95 us (10%)
  local copies, waits for them, and re-layouts  2.73 us (3%)
    all_to_all x1, blocking collectives, body(): words = lax.all_to_all(words, 'zl', 0, 0)  17.7 us
    all_gather x1, blocking collectives, body(): words = lax.all_gather(words, ('x', 'c'))  17.6 us
    all_to_all x1, starting transfers between devices, body(): received = lax.all_to_all(chunks, VIEW, 0, 0)  16.2 us
    ppermute x1, starting transfers between devices, body(): edge = lax.ppermute(edge, across, strip_pairs(3, 4))  7.9 us
    ppermute x1, starting transfers between devices, body(): far = lax.ppermute(far, across, strip_pairs(1, 2))  6.02 us
    ppermute x1, waiting for transfers between devices, body(): far = lax.ppermute(far, across, strip_pairs(1, 2))  4.79 us
    pallas_call x1, Pallas kernels, body(): call(view_kernel, [((3, 3, 16, 128), F32), ((3, 3, HALO, 128), F32), ((3,...  4.58 us
    ppermute x1, waiting for transfers between devices, body(): edge = lax.ppermute(edge, across, strip_pairs(3, 4))  3.59 us
  transfers between devices with their start and end apart: 4, of which 3 were waited for; matrix products, arithmetic and copies ran while one was open for 0% of the time, Pallas kernels for 1%

profile of v3, /device:TPU:25, one launch (start us, length us, event | category | flops | bytes accessed | tf_op | source)
XLA Modules:
  0.0 88.6 jit_solution(4602760119906610838)
XLA Ops:
  0.0 0.0 copy-start.1
  0.0 0.9 %copy-done.1 = bf16[1,48,1024]{2,1,0:T(8,128)(2,1)S(1)} copy-done((bf16[1,48,1024]{2,1,0:T(8,128)(2,1)S(1)}, bf16[1,48,1024]{2,1,0:T(8,128)(2,1)}, u32[]{:S(2)}) %copy-start.1) | copy-done | bytes 98328
  0.9 0.0 copy-start.2
  0.9 0.7 copy-done.2
  1.6 1.5 %shard_map.37 = bf16[64,8,128]{2,1,0:T(8,128)(2,1)} custom-call(bf16[1,48,1024]{2,1,0:T(8,128)(2,1)S(1)} %copy-done.1, s32[1,2,3]{2,1,0:T(2,128)S(1)} %bitcast.3), custom_call_target="tpu_custom_call" | custom-call | tf_op jit(solution)/shard_map/pallas_call | solution.py:279
  3.0 16.2 %all-to-all-start = ((bf16[64,8,128]{2,1,0:T(8,128)(2,1)}), bf16[64,8,128]{2,1,0:T(8,128)(2,1)S(1)}, u32[]{:S(2)}, u32[]{:S(2)}) async-start(bf16[64,8,128]{2,1,0:T(8,128)(2,1)} %shard_map.37), calls=%async_computation | async-start | bytes 262144 | tf_op jit(solution)/shard_map/all_to_all | solution.py:285
  19.3 0.0 copy-start
  19.3 1.2 %copy-done = bf16[3,3,48,1024]{3,2,1,0:T(8,128)(2,1)S(1)} copy-done((bf16[3,3,48,1024]{3,2,1,0:T(8,128)(2,1)S(1)}, bf16[3,3,48,1024]{3,2,1,0:T(8,128)(2,1)}, u32[]{:S(2)}) %copy-start) | copy-done | bytes 884760
  20.4 0.1 shard_map.38
  20.6 7.9 %collective-permute-start = (f32[3,3,8,128]{3,2,1,0:T(8,128)S(1)}, f32[3,3,8,128]{3,2,1,0:T(8,128)S(1)}, u32[]{:S(2)}, u32[]{:S(2)}) collective-permute-start(f32[3,3,8,128]{3,2,1,0:T(8,128)S(1)} %get-tuple-element.13), channel_id=1, source_target_pairs={{48,49},{49,48},{1,2},{2,1},{50,51},{51,50},{3,260},{260,3},{308,3... | collective-permute-start | bytes 110600 | tf_op jit(solution)/shard_map/ppermute | solution.py:293
  28.5 3.6 %collective-permute-done.edge_ref = f32[3,3,8,128]{3,2,1,0:T(8,128)S(1)} collective-permute-done((f32[3,3,8,128]{3,2,1,0:T(8,128)S(1)}, f32[3,3,8,128]{3,2,1,0:T(8,128)S(1)}, u32[]{:S(2)}, u32[]{:S(2)}) %collective-permute-start) | collective-permute-done | bytes 36896 | tf_op jit(solution)/shard_map/ppermute | solution.py:293
  32.1 0.7 shard_map.39
  32.8 1.1 %all-to-all-done.recv_ref = bf16[64,8,128]{2,1,0:T(8,128)(2,1)S(1)} async-done(((bf16[64,8,128]{2,1,0:T(8,128)(2,1)}), bf16[64,8,128]{2,1,0:T(8,128)(2,1)S(1)}, u32[]{:S(2)}, u32[]{:S(2)}) %all-to-all-start) | async-done | bytes 131104 | tf_op jit(solution)/shard_map/all_to_all | solution.py:285
  33.9 4.6 %shard_map.40 = (f32[3,3,16,128]{3,2,1,0:T(8,128)S(1)}, f32[3,3,8,128]{3,2,1,0:T(8,128)S(1)}, f32[3,3,8,128]{3,2,1,0:T(8,128)S(1)}) custom-call(bf16[64,8,128]{2,1,0:T(8,128)(2,1)S(1)} %all-to-all-done.recv_ref, f32[3,17,3,32,128]{4,3,2,1,0:T(8,128)S(1)} %get-tuple-element.14.seen_ref), custom_call_target="tpu_custom_call" | custom-call | tf_op jit(solution)/shard_map/pallas_call | solution.py:301
  38.5 1.9 %collective-permute-start.1 = (f32[3,3,8,128]{3,2,1,0:T(8,128)S(1)}, f32[3,3,8,128]{3,2,1,0:T(8,128)S(1)}, u32[]{:S(2)}, u32[]{:S(2)}) collective-permute-start(f32[3,3,8,128]{3,2,1,0:T(8,128)S(1)} %get-tuple-element.16), channel_id=1, source_target_pairs={{0,16},{16,0},{32,48},{48,32},{49,33},{33,49},{17,1},{1,17},{2,18}... | collective-permute-start | bytes 110600 | tf_op jit(solution)/shard_map/ppermute | solution.py:313
  40.4 6.0 %collective-permute-start.2 = (f32[3,3,8,128]{3,2,1,0:T(8,128)S(1)}, f32[3,3,8,128]{3,2,1,0:T(8,128)S(1)}, u32[]{:S(2)}, u32[]{:S(2)}) collective-permute-start(f32[3,3,8,128]{3,2,1,0:T(8,128)S(1)} %get-tuple-element.17), channel_id=1, source_target_pairs={{16,32},{32,16},{48,49},{49,48},{33,17},{17,33},{1,2},{2,1},{18,34... | collective-permute-start | bytes 110600 | tf_op jit(solution)/shard_map/ppermute | solution.py:314
  46.4 0.0 collective-permute-done.1.near_ref
  46.4 4.8 %collective-permute-done.2.far_ref = f32[3,3,8,128]{3,2,1,0:T(8,128)S(1)} collective-permute-done((f32[3,3,8,128]{3,2,1,0:T(8,128)S(1)}, f32[3,3,8,128]{3,2,1,0:T(8,128)S(1)}, u32[]{:S(2)}, u32[]{:S(2)}) %collective-permute-start.2) | collective-permute-done | bytes 36896 | tf_op jit(solution)/shard_map/ppermute | solution.py:314
  51.2 0.2 shard_map.41
  51.4 17.7 %all_to_all.10.words_ref = s32[8,32,128]{2,1,0:T(8,128)S(1)} all-to-all(s32[8,32,128]{2,1,0:T(8,128)S(1)} %shard_map.41), channel_id=1, replica_groups=mesh['zl'=8,'x'=4,'c'=2,'zh'=2,'y'=4] {'zl'}, dimensions={0} | all-to-all | bytes 262144 | tf_op jit(solution)/shard_map/all_to_all | solution.py:322
  69.2 17.6 %all-gather = s32[1920,128]{1,0:T(8,128)S(1)} all-gather(s32[240,128]{1,0:T(8,128)S(1)} %shard_map.42), channel_id=2, replica_groups=mesh['zl'=8,'x'=4,'c'=2,'zh'=2,'y'=4] {'x','c'}, dimensions={0}, use_global_device_ids=true | all-gather | bytes 1105920 | tf_op jit(solution)/shard_map/all_gather | solution.py:324
  86.7 1.9 %shard_map.43 = f32[3,3,48,1024]{3,2,1,0:T(8,128)} custom-call(s32[8,240,128]{2,1,0:T(8,128)S(1)} %bitcast.2), custom_call_target="tpu_custom_call" | custom-call | tf_op jit(solution)/shard_map/pallas_call | solution.py:326
  (1 shorter events, 0.0 us)
Async XLA Ops:
  0.0 0.9 %copy-start.1 = (bf16[1,48,1024]{2,1,0:T(8,128)(2,1)S(1)}, bf16[1,48,1024]{2,1,0:T(8,128)(2,1)}, u32[]{:S(2)}) copy-start(bf16[1,48,1024]{2,1,0:T(8,128)(2,1)} %target_ref.1) | copy-start | bytes 294916
  0.9 0.7 copy-start.2
  3.0 30.9 %all-to-all-start = ((bf16[64,8,128]{2,1,0:T(8,128)(2,1)}), bf16[64,8,128]{2,1,0:T(8,128)(2,1)S(1)}, u32[]{:S(2)}, u32[]{:S(2)}) async-start(bf16[64,8,128]{2,1,0:T(8,128)(2,1)} %shard_map.37), calls=%async_computation | async-start | bytes 262144 | tf_op jit(solution)/shard_map/all_to_all | solution.py:285
  19.3 1.2 %copy-start = (bf16[3,3,48,1024]{3,2,1,0:T(8,128)(2,1)S(1)}, bf16[3,3,48,1024]{3,2,1,0:T(8,128)(2,1)}, u32[]{:S(2)}) copy-start(bf16[3,3,48,1024]{3,2,1,0:T(8,128)(2,1)} %layers_ref.1) | copy-start | bytes 2654212
  20.6 11.5 %collective-permute-start = (f32[3,3,8,128]{3,2,1,0:T(8,128)S(1)}, f32[3,3,8,128]{3,2,1,0:T(8,128)S(1)}, u32[]{:S(2)}, u32[]{:S(2)}) collective-permute-start(f32[3,3,8,128]{3,2,1,0:T(8,128)S(1)} %get-tuple-element.13), channel_id=1, source_target_pairs={{48,49},{49,48},{1,2},{2,1},{50,51},{51,50},{3,260},{260,3},{308,3... | collective-permute-start | bytes 110600 | tf_op jit(solution)/shard_map/ppermute | solution.py:293
  38.5 8.0 %collective-permute-start.1 = (f32[3,3,8,128]{3,2,1,0:T(8,128)S(1)}, f32[3,3,8,128]{3,2,1,0:T(8,128)S(1)}, u32[]{:S(2)}, u32[]{:S(2)}) collective-permute-start(f32[3,3,8,128]{3,2,1,0:T(8,128)S(1)} %get-tuple-element.16), channel_id=1, source_target_pairs={{0,16},{16,0},{32,48},{48,32},{49,33},{33,49},{17,1},{1,17},{2,18}... | collective-permute-start | bytes 110600 | tf_op jit(solution)/shard_map/ppermute | solution.py:313
  40.4 10.8 %collective-permute-start.2 = (f32[3,3,8,128]{3,2,1,0:T(8,128)S(1)}, f32[3,3,8,128]{3,2,1,0:T(8,128)S(1)}, u32[]{:S(2)}, u32[]{:S(2)}) collective-permute-start(f32[3,3,8,128]{3,2,1,0:T(8,128)S(1)} %get-tuple-element.17), channel_id=1, source_target_pairs={{16,32},{32,16},{48,49},{49,48},{33,17},{17,33},{1,2},{2,1},{18,34... | collective-permute-start | bytes 110600 | tf_op jit(solution)/shard_map/ppermute | solution.py:314

commit v4 on v3

--- a/solution.py
+++ b/solution.py
@@ -25,16 +25,37 @@
     return lax.broadcasted_iota(I32, (rows, 128), 1)
 
 
-def mirrored(q):
-    return jnp.where(lax.rem(lax.axis_index("y"), 2) == 0, q, 3 - q)
-
-
-def my_block():
-    return lax.rem(lax.axis_index("zl") + 4 * lax.axis_index("zh"), 8)
-
-
-def pack_kernel(target_ref, shifts_ref, chunks_ref, wide_ref):
-    high = lax.axis_index("zh")
+def home(block, q, high, odd):
+    pair = block >> 1
+    zl = pair + 4 * (pair >> 1) if q in (0, 3) else pair + 2
+    x = block & 1 if q < 2 else 3 - (block & 1)
+    return zl ^ (6 * high), x + odd * (3 - 2 * x)
+
+
+def place():
+    return lax.axis_index("zh"), lax.rem(lax.axis_index("y"), 2)
+
+
+def my_tile():
+    high, odd = place()
+    zl = jnp.bitwise_xor(lax.axis_index("zl"), 6 * high)
+    x = lax.axis_index("x")
+    x = x + odd * (3 - 2 * x)
+    outer = (zl < 2) | (zl > 5)
+    pair = jnp.where(zl < 2, zl, jnp.where(zl > 5, zl - 4, zl - 2))
+    block = 2 * pair + jnp.where(x < 2, x, 3 - x)
+    return block, jnp.where(x < 2, jnp.where(outer, 0, 1), jnp.where(outer, 3, 2))
+
+
+def pack_kernel(
+    target_hbm, shifts_hbm, chunks_ref, target_ref, shifts_ref, wide_ref, target_sem, shifts_sem
+):
+    fetch_shifts = pltpu.make_async_copy(shifts_hbm, shifts_ref, shifts_sem)
+    fetch_shifts.start()
+    fetch = pltpu.make_async_copy(target_hbm, target_ref, target_sem)
+    fetch.start()
+    high, odd = place()
+    fetch.wait()
     lane = lanes(48)
     blocks = [target_ref[0, :, 128 * d : 128 * d + 128].astype(F32) for d in range(8)]
     zero = jnp.zeros((48, 128), F32)
@@ -46,6 +67,7 @@
         wide_ref[2 * d + 1, :48] = pltpu.roll(jnp.where(lane < HALO, right, mid), 128 - 56, 1)
     lane = lanes(8)
     upper_half = lax.broadcasted_iota(I32, (8, 128), 0) < 4
+    fetch_shifts.wait()
     extra = jnp.zeros((8, 128), F32)
     for layer in range(3):
         for part in range(2):
@@ -53,9 +75,8 @@
                 lane == 120 + 2 * layer + part, shifts_ref[0, part, layer].astype(F32), extra
             )
     for q in range(4):
-        x = mirrored(q)
         for d in range(8):
-            zl = lax.rem(d + 4 * high, 8)
+            zl, x = home(d, q, high, odd)
             for h in range(2):
                 at = 2 * d + h
                 main = wide_ref[at, TALL * q : TALL * q + 8]
@@ -67,9 +88,10 @@
 
 
 def strip_kernel(layers_ref, own_ref, edge_ref):
-    last = mirrored(lax.axis_index("x")) == 3
+    block, q = my_tile()
+    last = q == 3
     half = lax.axis_index("c")
-    block = my_block() - 1 + half
+    block = block - 1 + half
     amount = jnp.where(half == 0, 16, 80)
     left = pl.multiple_of(jnp.maximum(block, 0) * 128, 128)
     right = pl.multiple_of(jnp.minimum(block + 1, 7) * 128, 128)
@@ -86,7 +108,7 @@
 
 
 def seen_kernel(own_ref, edge_ref, seen_ref, tile_ref, tall_ref):
-    q = mirrored(lax.axis_index("x"))
+    _, q = my_tile()
     start = q * TALL
     tall_ref[:, :, :HALO] = edge_ref[...]
     tall_ref[:, :, HALO : HALO + 48] = own_ref[...]
@@ -122,7 +144,8 @@
     for ref in sums:
         ref[...] = jnp.zeros_like(ref)
 
-    column = my_block() * 128 + lax.axis_index("c") * WIDE - HALO + lanes(16)
+    block, q = my_tile()
+    column = block * 128 + lax.axis_index("c") * WIDE - HALO + lanes(16)
     inside = (column >= 0) & (column < 1024)
     inside = inside & (lax.broadcasted_iota(I32, (16, 128), 0) < TALL)
     third = jnp.where(inside, 1.0 / 3.0, 0.0)
@@ -145,7 +168,7 @@
 
     lax.fori_loop(0, 64, one_view, 0)
 
-    even = lax.rem(mirrored(lax.axis_index("x")), 2) == 0
+    even = lax.rem(q, 2) == 0
     lane = lanes(32)
     for layer in range(3):
         for frame in range(3):
@@ -168,7 +191,8 @@
 
 def update_kernel(own_ref, near_ref, far_ref, tile_ref, out_ref, code_ref):
     lane = lanes(TALL)
-    even = lax.rem(mirrored(lax.axis_index("x")), 2) == 0
+    _, q = my_tile()
+    even = lax.rem(q, 2) == 0
     for layer in range(3):
         for frame in range(3):
             own = own_ref[layer, frame]
@@ -208,16 +232,15 @@
 
 
 def spread_kernel(words_ref, out_ref, block_ref, sems):
-    high = lax.axis_index("zh")
+    high, flip = place()
 
     def sent(d):
         columns = pl.ds(pl.multiple_of(d * 128, 128), 128)
         return pltpu.make_async_copy(block_ref.at[d], out_ref.at[:, :, :, columns], sems.at[d])
 
     def one(d, carry):
-        zl = lax.rem(d + 4 * high, 8)
         for q in range(4):
-            x = mirrored(q)
+            zl, x = home(d, q, high, flip)
             rows = slice(TALL * q, TALL * q + TALL)
 
             def words(c, first, count):
@@ -247,8 +270,7 @@
 def strip_pairs(first, step):
     def index(block, strip):
         at, q = strip // 4, strip % 4
-        x = q if at % 2 == 0 else 3 - q
-        zl = (block + 4 * (at // 4)) % 8
+        zl, x = home(block, q, at // 4, at % 2)
         return ((zl * 4 + x) * 2 + at // 4) * 4 + at % 4
 
     pairs = []
@@ -260,7 +282,6 @@
 
 
 VMEM = pl.BlockSpec(memory_space=pltpu.VMEM)
-SMEM = pl.BlockSpec(memory_space=pltpu.SMEM)
 
 
 def call(kernel, outs, ins, scratch=(), **more):
@@ -279,8 +300,14 @@
     (chunks,) = call(
         pack_kernel,
         [((64, 8, 128), BF16)],
-        [VMEM, SMEM],
-        [pltpu.VMEM((16, 56, 128), F32)],
+        [pl.BlockSpec(memory_space=pl.ANY)] * 2,
+        [
+            pltpu.VMEM((1, 48, 1024), BF16),
+            pltpu.SMEM((1, 2, 3), I32),
+            pltpu.VMEM((16, 56, 128), F32),
+            pltpu.SemaphoreType.DMA,
+            pltpu.SemaphoreType.DMA,
+        ],
     )(target, shifts.transpose(0, 2, 1))
     received = lax.all_to_all(chunks, VIEW, 0, 0)
 

time: 88.9 us -> 85.2 us (0.958)
  blocking collectives: 35.3 us -> 33.3 us
  starting transfers between devices: 32.1 us -> 30.5 us
    all_to_all x1, blocking collectives: 17.7 us -> 15.7 us  [body(): words = lax.all_to_all(words, 'zl', 0, 0)]
    ppermute x1, starting transfers between devices: 6.02 us -> 4.01 us  [body(): far = lax.ppermute(far, across, strip_pairs(1, 2))]
    ppermute x1, waiting for transfers between devices: 3.59 us -> 1.76 us  [body(): edge = lax.ppermute(edge, across, strip_pairs(3, 4))]
    all_to_all x1, waiting for transfers between devices: 1.12 us -> 2.83 us  [body(): received = lax.all_to_all(chunks, VIEW, 0, 0)]
where the time goes in v4:
time: 85.2 us; the launch traced here: 84.9 us
  blocking collectives  33.3 us (39%)
  starting transfers between devices  30.5 us (36%)
  waiting for transfers between devices  9.48 us (11%)
  Pallas kernels  8.8 us (10%)
  local copies, waits for them, and re-layouts  2.73 us (3%)
    all_gather x1, blocking collectives, body(): words = lax.all_gather(words, ('x', 'c'))  17.6 us
    all_to_all x1, starting transfers between devices, body(): received = lax.all_to_all(chunks, VIEW, 0, 0)  16.2 us
    all_to_all x1, blocking collectives, body(): words = lax.all_to_all(words, 'zl', 0, 0)  15.7 us
    ppermute x1, starting transfers between devices, body(): edge = lax.ppermute(edge, across, strip_pairs(3, 4))  8.01 us
    ppermute x1, waiting for transfers between devices, body(): far = lax.ppermute(far, across, strip_pairs(1, 2))  4.89 us
    pallas_call x1, Pallas kernels, body(): call(view_kernel, [((3, 3, 16, 128), F32), ((3, 3, HALO, 128), F32), ((3,...  4.55 us
    ppermute x1, starting transfers between devices, body(): far = lax.ppermute(far, across, strip_pairs(1, 2))  4.01 us
    all_to_all x1, waiting for transfers between devices, body(): received = lax.all_to_all(chunks, VIEW, 0, 0)  2.83 us
  transfers between devices with their start and end apart: 4, of which 3 were waited for; matrix products, arithmetic and copies ran while one was open for 0% of the time, Pallas kernels for 1%

profile of v4, /device:TPU:25, one launch (start us, length us, event | category | flops | bytes accessed | tf_op | source)
XLA Modules:
  0.0 84.9 jit_solution(293171695619289451)
XLA Ops:
  0.0 0.0 copy-start.1
  0.0 0.9 %copy-done.1 = bf16[1,48,1024]{2,1,0:T(8,128)(2,1)S(1)} copy-done((bf16[1,48,1024]{2,1,0:T(8,128)(2,1)S(1)}, bf16[1,48,1024]{2,1,0:T(8,128)(2,1)}, u32[]{:S(2)}) %copy-start.1) | copy-done | bytes 98328
  0.9 0.0 copy-start.2
  0.9 0.7 copy-done.2
  1.6 1.4 %shard_map.37 = bf16[64,8,128]{2,1,0:T(8,128)(2,1)} custom-call(bf16[1,48,1024]{2,1,0:T(8,128)(2,1)S(1)} %copy-done.1, s32[1,2,3]{2,1,0:T(2,128)S(1)} %bitcast.3), custom_call_target="tpu_custom_call" | custom-call | tf_op jit(solution)/shard_map/pallas_call | solution.py:300
  2.9 16.2 %all-to-all-start = ((bf16[64,8,128]{2,1,0:T(8,128)(2,1)}), bf16[64,8,128]{2,1,0:T(8,128)(2,1)S(1)}, u32[]{:S(2)}, u32[]{:S(2)}) async-start(bf16[64,8,128]{2,1,0:T(8,128)(2,1)} %shard_map.37), calls=%async_computation | async-start | bytes 262144 | tf_op jit(solution)/shard_map/all_to_all | solution.py:312
  19.2 0.0 copy-start
  19.2 1.2 %copy-done = bf16[3,3,48,1024]{3,2,1,0:T(8,128)(2,1)S(1)} copy-done((bf16[3,3,48,1024]{3,2,1,0:T(8,128)(2,1)S(1)}, bf16[3,3,48,1024]{3,2,1,0:T(8,128)(2,1)}, u32[]{:S(2)}) %copy-start) | copy-done | bytes 884760
  20.3 0.1 shard_map.38
  20.5 8.0 %collective-permute-start = (f32[3,3,8,128]{3,2,1,0:T(8,128)S(1)}, f32[3,3,8,128]{3,2,1,0:T(8,128)S(1)}, u32[]{:S(2)}, u32[]{:S(2)}) collective-permute-start(f32[3,3,8,128]{3,2,1,0:T(8,128)S(1)} %get-tuple-element.13), channel_id=1, source_target_pairs={{48,49},{49,48},{1,2},{2,1},{50,51},{51,50},{3,388},{388,3},{436,4... | collective-permute-start | bytes 110600 | tf_op jit(solution)/shard_map/ppermute | solution.py:320
  28.5 1.8 %collective-permute-done.edge_ref = f32[3,3,8,128]{3,2,1,0:T(8,128)S(1)} collective-permute-done((f32[3,3,8,128]{3,2,1,0:T(8,128)S(1)}, f32[3,3,8,128]{3,2,1,0:T(8,128)S(1)}, u32[]{:S(2)}, u32[]{:S(2)}) %collective-permute-start) | collective-permute-done | bytes 36896 | tf_op jit(solution)/shard_map/ppermute | solution.py:320
  30.3 0.7 shard_map.39
  31.0 2.8 %all-to-all-done.recv_ref = bf16[64,8,128]{2,1,0:T(8,128)(2,1)S(1)} async-done(((bf16[64,8,128]{2,1,0:T(8,128)(2,1)}), bf16[64,8,128]{2,1,0:T(8,128)(2,1)S(1)}, u32[]{:S(2)}, u32[]{:S(2)}) %all-to-all-start) | async-done | bytes 131104 | tf_op jit(solution)/shard_map/all_to_all | solution.py:312
  33.8 4.5 %shard_map.40 = (f32[3,3,16,128]{3,2,1,0:T(8,128)S(1)}, f32[3,3,8,128]{3,2,1,0:T(8,128)S(1)}, f32[3,3,8,128]{3,2,1,0:T(8,128)S(1)}) custom-call(bf16[64,8,128]{2,1,0:T(8,128)(2,1)S(1)} %all-to-all-done.recv_ref, f32[3,17,3,32,128]{4,3,2,1,0:T(8,128)S(1)} %get-tuple-element.14.seen_ref), custom_call_target="tpu_custom_call" | custom-call | tf_op jit(solution)/shard_map/pallas_call | solution.py:328
  38.4 2.2 %collective-permute-start.1 = (f32[3,3,8,128]{3,2,1,0:T(8,128)S(1)}, f32[3,3,8,128]{3,2,1,0:T(8,128)S(1)}, u32[]{:S(2)}, u32[]{:S(2)}) collective-permute-start(f32[3,3,8,128]{3,2,1,0:T(8,128)S(1)} %get-tuple-element.16), channel_id=1, source_target_pairs={{0,128},{128,0},{176,48},{48,176},{49,177},{177,49},{129,1},{1,129... | collective-permute-start | bytes 110600 | tf_op jit(solution)/shard_map/ppermute | solution.py:340
  40.6 4.0 %collective-permute-start.2 = (f32[3,3,8,128]{3,2,1,0:T(8,128)S(1)}, f32[3,3,8,128]{3,2,1,0:T(8,128)S(1)}, u32[]{:S(2)}, u32[]{:S(2)}) collective-permute-start(f32[3,3,8,128]{3,2,1,0:T(8,128)S(1)} %get-tuple-element.17), channel_id=1, source_target_pairs={{128,176},{176,128},{48,49},{49,48},{177,129},{129,177},{1,2},{2,1... | collective-permute-start | bytes 110600 | tf_op jit(solution)/shard_map/ppermute | solution.py:341
  44.6 0.0 collective-permute-done.1.near_ref
  44.6 4.9 %collective-permute-done.2.far_ref = f32[3,3,8,128]{3,2,1,0:T(8,128)S(1)} collective-permute-done((f32[3,3,8,128]{3,2,1,0:T(8,128)S(1)}, f32[3,3,8,128]{3,2,1,0:T(8,128)S(1)}, u32[]{:S(2)}, u32[]{:S(2)}) %collective-permute-start.2) | collective-permute-done | bytes 36896 | tf_op jit(solution)/shard_map/ppermute | solution.py:341
  49.5 0.2 shard_map.41
  49.7 15.7 %all_to_all.10.words_ref = s32[8,32,128]{2,1,0:T(8,128)S(1)} all-to-all(s32[8,32,128]{2,1,0:T(8,128)S(1)} %shard_map.41), channel_id=1, replica_groups=mesh['zl'=8,'x'=4,'c'=2,'zh'=2,'y'=4] {'zl'}, dimensions={0} | all-to-all | bytes 262144 | tf_op jit(solution)/shard_map/all_to_all | solution.py:349
  65.4 17.6 %all-gather = s32[1920,128]{1,0:T(8,128)S(1)} all-gather(s32[240,128]{1,0:T(8,128)S(1)} %shard_map.42), channel_id=2, replica_groups=mesh['zl'=8,'x'=4,'c'=2,'zh'=2,'y'=4] {'x','c'}, dimensions={0}, use_global_device_ids=true | all-gather | bytes 1105920 | tf_op jit(solution)/shard_map/all_gather | solution.py:351
  83.0 1.9 %shard_map.43 = f32[3,3,48,1024]{3,2,1,0:T(8,128)} custom-call(s32[8,240,128]{2,1,0:T(8,128)S(1)} %bitcast.2), custom_call_target="tpu_custom_call" | custom-call | tf_op jit(solution)/shard_map/pallas_call | solution.py:353
  (1 shorter events, 0.0 us)
Async XLA Ops:
  0.0 0.9 %copy-start.1 = (bf16[1,48,1024]{2,1,0:T(8,128)(2,1)S(1)}, bf16[1,48,1024]{2,1,0:T(8,128)(2,1)}, u32[]{:S(2)}) copy-start(bf16[1,48,1024]{2,1,0:T(8,128)(2,1)} %target_hbm.1) | copy-start | bytes 294916
  0.9 0.7 copy-start.2
  2.9 30.9 %all-to-all-start = ((bf16[64,8,128]{2,1,0:T(8,128)(2,1)}), bf16[64,8,128]{2,1,0:T(8,128)(2,1)S(1)}, u32[]{:S(2)}, u32[]{:S(2)}) async-start(bf16[64,8,128]{2,1,0:T(8,128)(2,1)} %shard_map.37), calls=%async_computation | async-start | bytes 262144 | tf_op jit(solution)/shard_map/all_to_all | solution.py:312
  19.2 1.2 %copy-start = (bf16[3,3,48,1024]{3,2,1,0:T(8,128)(2,1)S(1)}, bf16[3,3,48,1024]{3,2,1,0:T(8,128)(2,1)}, u32[]{:S(2)}) copy-start(bf16[3,3,48,1024]{3,2,1,0:T(8,128)(2,1)} %layers_ref.1) | copy-start | bytes 2654212
  20.5 9.8 %collective-permute-start = (f32[3,3,8,128]{3,2,1,0:T(8,128)S(1)}, f32[3,3,8,128]{3,2,1,0:T(8,128)S(1)}, u32[]{:S(2)}, u32[]{:S(2)}) collective-permute-start(f32[3,3,8,128]{3,2,1,0:T(8,128)S(1)} %get-tuple-element.13), channel_id=1, source_target_pairs={{48,49},{49,48},{1,2},{2,1},{50,51},{51,50},{3,388},{388,3},{436,4... | collective-permute-start | bytes 110600 | tf_op jit(solution)/shard_map/ppermute | solution.py:320
  38.4 6.3 %collective-permute-start.1 = (f32[3,3,8,128]{3,2,1,0:T(8,128)S(1)}, f32[3,3,8,128]{3,2,1,0:T(8,128)S(1)}, u32[]{:S(2)}, u32[]{:S(2)}) collective-permute-start(f32[3,3,8,128]{3,2,1,0:T(8,128)S(1)} %get-tuple-element.16), channel_id=1, source_target_pairs={{0,128},{128,0},{176,48},{48,176},{49,177},{177,49},{129,1},{1,129... | collective-permute-start | bytes 110600 | tf_op jit(solution)/shard_map/ppermute | solution.py:340
  40.6 8.9 %collective-permute-start.2 = (f32[3,3,8,128]{3,2,1,0:T(8,128)S(1)}, f32[3,3,8,128]{3,2,1,0:T(8,128)S(1)}, u32[]{:S(2)}, u32[]{:S(2)}) collective-permute-start(f32[3,3,8,128]{3,2,1,0:T(8,128)S(1)} %get-tuple-element.17), channel_id=1, source_target_pairs={{128,176},{176,128},{48,49},{49,48},{177,129},{129,177},{1,2},{2,1... | collective-permute-start | bytes 110600 | tf_op jit(solution)/shard_map/ppermute | solution.py:341

commit v5 on v4

--- a/solution.py
+++ b/solution.py
@@ -25,11 +25,12 @@
     return lax.broadcasted_iota(I32, (rows, 128), 1)
 
 
-def home(block, q, high, odd):
-    pair = block >> 1
-    zl = pair + 4 * (pair >> 1) if q in (0, 3) else pair + 2
-    x = block & 1 if q < 2 else 3 - (block & 1)
-    return zl ^ (6 * high), x + odd * (3 - 2 * x)
+def home(block, half, q, high, odd):
+    column = 2 * block + half
+    at = column >> 2
+    outer, inner = at + 4 * (at >> 1), at + 2
+    zl = outer + ((q >> 1) ^ odd) * (inner - outer)
+    return zl ^ (6 * high), column & 3, q & 1
 
 
 def place():
@@ -39,12 +40,11 @@
 def my_tile():
     high, odd = place()
     zl = jnp.bitwise_xor(lax.axis_index("zl"), 6 * high)
-    x = lax.axis_index("x")
-    x = x + odd * (3 - 2 * x)
     outer = (zl < 2) | (zl > 5)
-    pair = jnp.where(zl < 2, zl, jnp.where(zl > 5, zl - 4, zl - 2))
-    block = 2 * pair + jnp.where(x < 2, x, 3 - x)
-    return block, jnp.where(x < 2, jnp.where(outer, 0, 1), jnp.where(outer, 3, 2))
+    at = jnp.where(zl < 2, zl, jnp.where(zl > 5, zl - 4, zl - 2))
+    column = 4 * at + lax.axis_index("x")
+    q = 2 * jnp.where(outer, odd, 1 - odd) + lax.axis_index("c")
+    return column >> 1, column & 1, q
 
 
 def pack_kernel(
@@ -76,21 +76,20 @@
             )
     for q in range(4):
         for d in range(8):
-            zl, x = home(d, q, high, odd)
             for h in range(2):
+                zl, x, c = home(d, h, q, high, odd)
                 at = 2 * d + h
                 main = wide_ref[at, TALL * q : TALL * q + 8]
                 first = wide_ref[at, TALL * q + 8 : TALL * q + 16]
                 second = wide_ref[at, TALL * q + 4 : TALL * q + 12]
                 pieces = jnp.where(upper_half, pltpu.roll(first, 80, 1), pltpu.roll(second, 40, 1))
                 chunk = jnp.where(lane < 80, main, jnp.where(lane < 120, pieces, extra))
-                chunks_ref[(zl * 4 + x) * 2 + h] = chunk.astype(BF16)
+                chunks_ref[(zl * 4 + x) * 2 + c] = chunk.astype(BF16)
 
 
 def strip_kernel(layers_ref, own_ref, edge_ref):
-    block, q = my_tile()
+    block, half, q = my_tile()
     last = q == 3
-    half = lax.axis_index("c")
     block = block - 1 + half
     amount = jnp.where(half == 0, 16, 80)
     left = pl.multiple_of(jnp.maximum(block, 0) * 128, 128)
@@ -108,7 +107,7 @@
 
 
 def seen_kernel(own_ref, edge_ref, seen_ref, tile_ref, tall_ref):
-    _, q = my_tile()
+    _, _, q = my_tile()
     start = q * TALL
     tall_ref[:, :, :HALO] = edge_ref[...]
     tall_ref[:, :, HALO : HALO + 48] = own_ref[...]
@@ -144,8 +143,8 @@
     for ref in sums:
         ref[...] = jnp.zeros_like(ref)
 
-    block, q = my_tile()
-    column = block * 128 + lax.axis_index("c") * WIDE - HALO + lanes(16)
+    block, half, q = my_tile()
+    column = block * 128 + half * WIDE - HALO + lanes(16)
     inside = (column >= 0) & (column < 1024)
     inside = inside & (lax.broadcasted_iota(I32, (16, 128), 0) < TALL)
     third = jnp.where(inside, 1.0 / 3.0, 0.0)
@@ -191,7 +190,7 @@
 
 def update_kernel(own_ref, near_ref, far_ref, tile_ref, out_ref, code_ref):
     lane = lanes(TALL)
-    _, q = my_tile()
+    _, _, q = my_tile()
     even = lax.rem(q, 2) == 0
     for layer in range(3):
         for frame in range(3):
@@ -240,10 +239,10 @@
 
     def one(d, carry):
         for q in range(4):
-            zl, x = home(d, q, high, flip)
             rows = slice(TALL * q, TALL * q + TALL)
 
-            def words(c, first, count):
+            def words(half, first, count):
+                zl, x, c = home(d, half, q, high, flip)
                 return words_ref[x * 2 + c, pl.ds(zl * WORDS + first, count), :]
 
             lane = lanes(TALL)
@@ -268,15 +267,15 @@
 
 
 def strip_pairs(first, step):
-    def index(block, strip):
-        at, q = strip // 4, strip % 4
-        zl, x = home(block, q, at // 4, at % 2)
-        return ((zl * 4 + x) * 2 + at // 4) * 4 + at % 4
+    def index(column, strip):
+        at = strip // 4
+        zl, x, c = home(column // 2, column % 2, strip % 4, at // 4, at % 2)
+        return (((zl * 4 + x) * 2 + c) * 2 + at // 4) * 4 + at % 4
 
     pairs = []
-    for block in range(8):
+    for column in range(16):
         for strip in range(first, 31, step):
-            a, b = index(block, strip), index(block, strip + 1)
+            a, b = index(column, strip), index(column, strip + 1)
             pairs += [(a, b), (b, a)]
     return pairs
 
@@ -300,7 +299,7 @@
     (chunks,) = call(
         pack_kernel,
         [((64, 8, 128), BF16)],
-        [pl.BlockSpec(memory_space=pl.ANY)] * 2,
+        [pl.BlockSpec(memory_space=pltpu.HBM)] * 2,
         [
             pltpu.VMEM((1, 48, 1024), BF16),
             pltpu.SMEM((1, 2, 3), I32),
@@ -316,7 +315,7 @@
         [((3, 3, 48, 128), F32), ((3, 3, HALO, 128), F32)],
         [VMEM],
     )(layers)
-    across = ("zl", "x", "zh", "y")
+    across = VIEW + ROW
     edge = lax.ppermute(edge, across, strip_pairs(3, 4))
     seen, tile = call(
         seen_kernel,
@@ -337,8 +336,8 @@
         ]
         + [pltpu.VMEM((SPAN, 3, 32, 128), F32)] * 6,
     )(received, seen)
+    far = lax.ppermute(far, across, strip_pairs(1, 2))
     near = lax.ppermute(near, across, strip_pairs(0, 2))
-    far = lax.ppermute(far, across, strip_pairs(1, 2))
 
     (words,) = call(
         update_kernel,

time: 85.2 us -> 82.7 us (0.971)
  blocking collectives: 33.3 us -> 30 us
  starting transfers between devices: 30.5 us -> 31.6 us
    all_gather x1, blocking collectives: 17.6 us -> 13.9 us  [body(): words = lax.all_gather(words, ('x', 'c'))]
where the time goes in v5:
time: 82.7 us; the launch traced here: 82.4 us
  starting transfers between devices  31.6 us (38%)
  blocking collectives  30 us (36%)
  waiting for transfers between devices  9.21 us (11%)
  Pallas kernels  8.79 us (11%)
  local copies, waits for them, and re-layouts  2.73 us (3%)
    all_to_all x1, starting transfers between devices, body(): received = lax.all_to_all(chunks, VIEW, 0, 0)  16.2 us
    all_to_all x1, blocking collectives, body(): words = lax.all_to_all(words, 'zl', 0, 0)  16.1 us
    all_gather x1, blocking collectives, body(): words = lax.all_gather(words, ('x', 'c'))  13.9 us
    ppermute x1, starting transfers between devices, body(): edge = lax.ppermute(edge, across, strip_pairs(3, 4))  8.26 us
    ppermute x1, waiting for transfers between devices, body(): far = lax.ppermute(far, across, strip_pairs(1, 2))  4.86 us
    ppermute x1, starting transfers between devices, body(): far = lax.ppermute(far, across, strip_pairs(1, 2))  4.76 us
    pallas_call x1, Pallas kernels, body(): call(view_kernel, [((3, 3, 16, 128), F32), ((3, 3, HALO, 128), F32), ((3,...  4.55 us
    unnamed x6, local copies, waits for them, and re-layouts  2.73 us
  transfers between devices with their start and end apart: 4, of which 3 were waited for; matrix products, arithmetic and copies ran while one was open for 0% of the time, Pallas kernels for 1%

profile of v5, /device:TPU:25, one launch (start us, length us, event | category | flops | bytes accessed | tf_op | source)
XLA Modules:
  0.0 82.4 jit_solution(15919397819163035579)
XLA Ops:
  0.0 0.0 copy-start.1
  0.0 0.9 %copy-done.1 = bf16[1,48,1024]{2,1,0:T(8,128)(2,1)S(1)} copy-done((bf16[1,48,1024]{2,1,0:T(8,128)(2,1)S(1)}, bf16[1,48,1024]{2,1,0:T(8,128)(2,1)}, u32[]{:S(2)}) %copy-start.1) | copy-done | bytes 98328
  0.9 0.0 copy-start.2
  0.9 0.7 copy-done.2
  1.6 1.4 %shard_map.37 = bf16[64,8,128]{2,1,0:T(8,128)(2,1)} custom-call(bf16[1,48,1024]{2,1,0:T(8,128)(2,1)S(1)} %copy-done.1, s32[1,2,3]{2,1,0:T(2,128)S(1)} %bitcast.3), custom_call_target="tpu_custom_call" | custom-call | tf_op jit(solution)/shard_map/pallas_call | solution.py:299
  2.9 16.2 %all-to-all-start = ((bf16[64,8,128]{2,1,0:T(8,128)(2,1)}), bf16[64,8,128]{2,1,0:T(8,128)(2,1)S(1)}, u32[]{:S(2)}, u32[]{:S(2)}) async-start(bf16[64,8,128]{2,1,0:T(8,128)(2,1)} %shard_map.37), calls=%async_computation | async-start | bytes 262144 | tf_op jit(solution)/shard_map/all_to_all | solution.py:311
  19.2 0.0 copy-start
  19.2 1.2 %copy-done = bf16[3,3,48,1024]{3,2,1,0:T(8,128)(2,1)S(1)} copy-done((bf16[3,3,48,1024]{3,2,1,0:T(8,128)(2,1)S(1)}, bf16[3,3,48,1024]{3,2,1,0:T(8,128)(2,1)}, u32[]{:S(2)}) %copy-start) | copy-done | bytes 884760
  20.3 0.1 shard_map.38
  20.5 8.3 %collective-permute-start = (f32[3,3,8,128]{3,2,1,0:T(8,128)S(1)}, f32[3,3,8,128]{3,2,1,0:T(8,128)S(1)}, u32[]{:S(2)}, u32[]{:S(2)}) collective-permute-start(f32[3,3,8,128]{3,2,1,0:T(8,128)S(1)} %get-tuple-element.13), channel_id=1, source_target_pairs={{136,129},{129,136},{9,2},{2,9},{138,131},{131,138},{11,388},{388,... | collective-permute-start | bytes 110600 | tf_op jit(solution)/shard_map/ppermute | solution.py:319
  28.8 2.0 %collective-permute-done.edge_ref = f32[3,3,8,128]{3,2,1,0:T(8,128)S(1)} collective-permute-done((f32[3,3,8,128]{3,2,1,0:T(8,128)S(1)}, f32[3,3,8,128]{3,2,1,0:T(8,128)S(1)}, u32[]{:S(2)}, u32[]{:S(2)}) %collective-permute-start) | collective-permute-done | bytes 36896 | tf_op jit(solution)/shard_map/ppermute | solution.py:319
  30.8 0.7 shard_map.39
  31.5 2.3 %all-to-all-done.recv_ref = bf16[64,8,128]{2,1,0:T(8,128)(2,1)S(1)} async-done(((bf16[64,8,128]{2,1,0:T(8,128)(2,1)}), bf16[64,8,128]{2,1,0:T(8,128)(2,1)S(1)}, u32[]{:S(2)}, u32[]{:S(2)}) %all-to-all-start) | async-done | bytes 131104 | tf_op jit(solution)/shard_map/all_to_all | solution.py:311
  33.8 4.6 %shard_map.40 = (f32[3,3,16,128]{3,2,1,0:T(8,128)S(1)}, f32[3,3,8,128]{3,2,1,0:T(8,128)S(1)}, f32[3,3,8,128]{3,2,1,0:T(8,128)S(1)}) custom-call(bf16[64,8,128]{2,1,0:T(8,128)(2,1)S(1)} %all-to-all-done.recv_ref, f32[3,17,3,32,128]{4,3,2,1,0:T(8,128)S(1)} %get-tuple-element.14.seen_ref), custom_call_target="tpu_custom_call" | custom-call | tf_op jit(solution)/shard_map/pallas_call | solution.py:327
  38.4 2.3 %collective-permute-start.1 = (f32[3,3,8,128]{3,2,1,0:T(8,128)S(1)}, f32[3,3,8,128]{3,2,1,0:T(8,128)S(1)}, u32[]{:S(2)}, u32[]{:S(2)}) collective-permute-start(f32[3,3,8,128]{3,2,1,0:T(8,128)S(1)} %get-tuple-element.16), channel_id=1, source_target_pairs={{0,8},{8,0},{128,136},{136,128},{129,137},{137,129},{1,9},{9,1},{2... | collective-permute-start | bytes 110600 | tf_op jit(solution)/shard_map/ppermute | solution.py:340
  40.7 4.8 %collective-permute-start.2 = (f32[3,3,8,128]{3,2,1,0:T(8,128)S(1)}, f32[3,3,8,128]{3,2,1,0:T(8,128)S(1)}, u32[]{:S(2)}, u32[]{:S(2)}) collective-permute-start(f32[3,3,8,128]{3,2,1,0:T(8,128)S(1)} %get-tuple-element.17), channel_id=1, source_target_pairs={{8,128},{128,8},{136,129},{129,136},{137,1},{1,137},{9,2},{2,9},{1... | collective-permute-start | bytes 110600 | tf_op jit(solution)/shard_map/ppermute | solution.py:339
  45.4 0.0 collective-permute-done.1.near_ref
  45.5 4.9 %collective-permute-done.2.far_ref = f32[3,3,8,128]{3,2,1,0:T(8,128)S(1)} collective-permute-done((f32[3,3,8,128]{3,2,1,0:T(8,128)S(1)}, f32[3,3,8,128]{3,2,1,0:T(8,128)S(1)}, u32[]{:S(2)}, u32[]{:S(2)}) %collective-permute-start.2) | collective-permute-done | bytes 36896 | tf_op jit(solution)/shard_map/ppermute | solution.py:339
  50.3 0.2 shard_map.41
  50.5 16.1 %all_to_all.10.words_ref = s32[8,32,128]{2,1,0:T(8,128)S(1)} all-to-all(s32[8,32,128]{2,1,0:T(8,128)S(1)} %shard_map.41), channel_id=1, replica_groups=mesh['zl'=8,'x'=4,'c'=2,'zh'=2,'y'=4] {'zl'}, dimensions={0} | all-to-all | bytes 262144 | tf_op jit(solution)/shard_map/all_to_all | solution.py:348
  66.6 13.9 %all-gather = s32[1920,128]{1,0:T(8,128)S(1)} all-gather(s32[240,128]{1,0:T(8,128)S(1)} %shard_map.42), channel_id=2, replica_groups=mesh['zl'=8,'x'=4,'c'=2,'zh'=2,'y'=4] {'x','c'}, dimensions={0}, use_global_device_ids=true | all-gather | bytes 1105920 | tf_op jit(solution)/shard_map/all_gather | solution.py:350
  80.5 1.9 %shard_map.43 = f32[3,3,48,1024]{3,2,1,0:T(8,128)} custom-call(s32[8,240,128]{2,1,0:T(8,128)S(1)} %bitcast.2), custom_call_target="tpu_custom_call" | custom-call | tf_op jit(solution)/shard_map/pallas_call | solution.py:352
  (1 shorter events, 0.0 us)
Async XLA Ops:
  0.0 0.9 %copy-start.1 = (bf16[1,48,1024]{2,1,0:T(8,128)(2,1)S(1)}, bf16[1,48,1024]{2,1,0:T(8,128)(2,1)}, u32[]{:S(2)}) copy-start(bf16[1,48,1024]{2,1,0:T(8,128)(2,1)} %target_hbm.1) | copy-start | bytes 294916
  0.9 0.7 copy-start.2
  2.9 30.9 %all-to-all-start = ((bf16[64,8,128]{2,1,0:T(8,128)(2,1)}), bf16[64,8,128]{2,1,0:T(8,128)(2,1)S(1)}, u32[]{:S(2)}, u32[]{:S(2)}) async-start(bf16[64,8,128]{2,1,0:T(8,128)(2,1)} %shard_map.37), calls=%async_computation | async-start | bytes 262144 | tf_op jit(solution)/shard_map/all_to_all | solution.py:311
  19.2 1.2 %copy-start = (bf16[3,3,48,1024]{3,2,1,0:T(8,128)(2,1)S(1)}, bf16[3,3,48,1024]{3,2,1,0:T(8,128)(2,1)}, u32[]{:S(2)}) copy-start(bf16[3,3,48,1024]{3,2,1,0:T(8,128)(2,1)} %layers_ref.1) | copy-start | bytes 2654212
  20.5 10.3 %collective-permute-start = (f32[3,3,8,128]{3,2,1,0:T(8,128)S(1)}, f32[3,3,8,128]{3,2,1,0:T(8,128)S(1)}, u32[]{:S(2)}, u32[]{:S(2)}) collective-permute-start(f32[3,3,8,128]{3,2,1,0:T(8,128)S(1)} %get-tuple-element.13), channel_id=1, source_target_pairs={{136,129},{129,136},{9,2},{2,9},{138,131},{131,138},{11,388},{388,... | collective-permute-start | bytes 110600 | tf_op jit(solution)/shard_map/ppermute | solution.py:319
  38.4 7.1 %collective-permute-start.1 = (f32[3,3,8,128]{3,2,1,0:T(8,128)S(1)}, f32[3,3,8,128]{3,2,1,0:T(8,128)S(1)}, u32[]{:S(2)}, u32[]{:S(2)}) collective-permute-start(f32[3,3,8,128]{3,2,1,0:T(8,128)S(1)} %get-tuple-element.16), channel_id=1, source_target_pairs={{0,8},{8,0},{128,136},{136,128},{129,137},{137,129},{1,9},{9,1},{2... | collective-permute-start | bytes 110600 | tf_op jit(solution)/shard_map/ppermute | solution.py:340
  40.7 9.6 %collective-permute-start.2 = (f32[3,3,8,128]{3,2,1,0:T(8,128)S(1)}, f32[3,3,8,128]{3,2,1,0:T(8,128)S(1)}, u32[]{:S(2)}, u32[]{:S(2)}) collective-permute-start(f32[3,3,8,128]{3,2,1,0:T(8,128)S(1)} %get-tuple-element.17), channel_id=1, source_target_pairs={{8,128},{128,8},{136,129},{129,136},{137,1},{1,137},{9,2},{2,9},{1... | collective-permute-start | bytes 110600 | tf_op jit(solution)/shard_map/ppermute | solution.py:339

commit v6 on v5

--- a/solution.py
+++ b/solution.py
@@ -18,7 +18,8 @@
 I32 = jnp.int32
 VIEW = ("zl", "x", "c")
 ROW = ("zh", "y")
-PARAMS = pltpu.CompilerParams(vmem_limit_bytes=48 * 1024 * 1024)
+PARAMS = pltpu.CompilerParams(vmem_limit_bytes=16 * 1024 * 1024)
+WHOLE = pltpu.CompilerParams(vmem_limit_bytes=64 * 1024 * 1024)
 
 
 def lanes(rows):
@@ -124,8 +125,10 @@
 
 
 def view_kernel(
-    recv_ref, seen_ref, own_out, near_out, far_out, image_ref, shift_ref, shift_smem, sem, *sums
+    recv_ref, seen_ref, far_out, near_out, s0_ref, s1_ref, s2_ref, s3_ref, s4_ref, s5_ref,
+    image_ref, shift_ref, shift_smem, sem,
 ):
+    sums = (s0_ref, s1_ref, s2_ref, s3_ref, s4_ref, s5_ref)
     shift_ref[...] = recv_ref[:, 0, :].astype(F32).astype(I32)
     copy = pltpu.make_async_copy(shift_ref, shift_smem, sem)
     copy.start()
@@ -165,37 +168,46 @@
                 sums[2 * layer + which][cols[layer], :, pl.ds(rows[layer], 16), :] += factor * others
         return carry
 
-    lax.fori_loop(0, 64, one_view, 0)
+    lax.fori_loop(0, 64, one_view, 0, unroll=4)
 
     even = lax.rem(q, 2) == 0
-    lane = lanes(32)
-    for layer in range(3):
-        for frame in range(3):
-            sides = []
-            for which, base in enumerate((-16, 48)):
-                total = None
-                for d in range(SPAN):
-                    amount = (d + base) % 128
-                    cells = sums[2 * layer + which][d, frame]
-                    moved = pltpu.roll(cells, amount, 1) if amount else cells
-                    total = moved if total is None else total + moved
-                sides.append(total)
-            both = jnp.where(lane < WIDE, sides[0], sides[1])
-            own_out[layer, frame] = both[HALO : HALO + 16]
-            up = both[:HALO]
-            down = both[HALO + TALL : 2 * HALO + TALL]
-            near_out[layer, frame] = jnp.where(even, down, up)
-            far_out[layer, frame] = jnp.where(even, up, down)
-
-
-def update_kernel(own_ref, near_ref, far_ref, tile_ref, out_ref, code_ref):
+    far_start = jnp.where(even, 0, HALO + TALL)
+    near_start = jnp.where(even, HALO + TALL, 0)
+    for layer in range(3):
+        for frame in range(3):
+            far_out[layer, frame] = folded(sums, layer, frame, far_start, HALO)
+            near_out[layer, frame] = folded(sums, layer, frame, near_start, HALO)
+
+
+def folded(sums, layer, frame, start, rows):
+    sides = []
+    for which, base in enumerate((-16, 48)):
+        total = None
+        for d in range(SPAN):
+            amount = (d + base) % 128
+            cells = sums[2 * layer + which][d, frame, pl.ds(start, rows), :]
+            moved = pltpu.roll(cells, amount, 1) if amount else cells
+            total = moved if total is None else total + moved
+        sides.append(total)
+    return jnp.where(lanes(rows) < WIDE, sides[0], sides[1])
+
+
+def own_kernel(s0_ref, s1_ref, s2_ref, s3_ref, s4_ref, s5_ref, own_out):
+    sums = (s0_ref, s1_ref, s2_ref, s3_ref, s4_ref, s5_ref)
+    for layer in range(3):
+        for frame in range(3):
+            own_out[layer, frame] = folded(sums, layer, frame, HALO, 16)
+
+
+def update_kernel(own_ref, far_ref, near_ref, tile_ref, out_ref, code_ref):
     lane = lanes(TALL)
+    other = 1 - lax.axis_index("c")
     _, _, q = my_tile()
     even = lax.rem(q, 2) == 0
     for layer in range(3):
         for frame in range(3):
             own = own_ref[layer, frame]
-            near = near_ref[layer, frame]
+            near = near_ref[other, layer, frame]
             far = far_ref[layer, frame]
             above = jnp.where(even, far, near)
             below = jnp.where(even, near, far)
@@ -283,15 +295,23 @@
 VMEM = pl.BlockSpec(memory_space=pltpu.VMEM)
 
 
-def call(kernel, outs, ins, scratch=(), **more):
+VIEW_SCRATCH = [
+    pltpu.VMEM((64, 16, 128), F32),
+    pltpu.VMEM((64, 128), I32),
+    pltpu.SMEM((64, 128), I32),
+    pltpu.SemaphoreType.DMA,
+]
+
+
+def call(kernel, outs, ins, scratch=(), params=PARAMS, cost=None):
     return pl.pallas_call(
         kernel,
         out_shape=tuple(jax.ShapeDtypeStruct(*out) for out in outs),
         in_specs=ins,
         out_specs=(VMEM,) * len(outs),
         scratch_shapes=scratch,
-        compiler_params=PARAMS,
-        **more,
+        compiler_params=params,
+        cost_estimate=cost,
     )
 
 
@@ -307,6 +327,7 @@
             pltpu.SemaphoreType.DMA,
             pltpu.SemaphoreType.DMA,
         ],
+        WHOLE,
     )(target, shifts.transpose(0, 2, 1))
     received = lax.all_to_all(chunks, VIEW, 0, 0)
 
@@ -324,27 +345,27 @@
         [pltpu.VMEM((3, 3, 72, 128), F32)],
     )(own, edge)
 
-    sums, near, far = call(
+    far, near, *sums = call(
         view_kernel,
-        [((3, 3, 16, 128), F32), ((3, 3, HALO, 128), F32), ((3, 3, HALO, 128), F32)],
+        [((3, 3, HALO, 128), F32)] * 2 + [((SPAN, 3, 32, 128), F32)] * 6,
         [VMEM] * 2,
-        [
-            pltpu.VMEM((64, 16, 128), F32),
-            pltpu.VMEM((64, 128), I32),
-            pltpu.SMEM((64, 128), I32),
-            pltpu.SemaphoreType.DMA,
-        ]
-        + [pltpu.VMEM((SPAN, 3, 32, 128), F32)] * 6,
+        VIEW_SCRATCH,
     )(received, seen)
     far = lax.ppermute(far, across, strip_pairs(1, 2))
-    near = lax.ppermute(near, across, strip_pairs(0, 2))
+    (own,) = call(
+        own_kernel,
+        [((3, 3, 16, 128), F32)],
+        [VMEM] * 6,
+        cost=pl.CostEstimate(flops=4_000_000, bytes_accessed=5_100_000, transcendentals=0),
+    )(*sums)
+    near = lax.all_gather(near, "c")
 
     (words,) = call(
         update_kernel,
         [((8, 32, 128), I32)],
         [VMEM] * 4,
         [pltpu.VMEM((9, 16, 128), I32)],
-    )(sums, near, far, tile)
+    )(own, far, near, tile)
     words = lax.all_to_all(words, "zl", 0, 0)
     (words,) = call(dense_kernel, [((8 * WORDS, 128), I32)], [VMEM])(words)
     words = lax.all_gather(words, ("x", "c"))

time: 82.7 us -> 78.5 us (0.949)
  waiting for transfers between devices: 9.21 us -> 6.13 us
  blocking collectives: 30 us -> 32.3 us
  starting transfers between devices: 31.6 us -> 29.6 us
  local copies, waits for them, and re-layouts: 2.73 us -> 1.16 us
    ppermute x1, waiting for transfers between devices: 4.86 us -> 1.78 us  [body(): far = lax.ppermute(far, across, strip_pairs(1, 2))]
    ppermute x1 -> x0, starting transfers between devices: 2.31 us -> none  [body(): near = lax.ppermute(near, across, strip_pairs(0, 2))]
    all_gather x0 -> x1, blocking collectives: none -> 1.86 us  [body(): near = lax.all_gather(near, 'c')]
    unnamed x6 -> x2, local copies, waits for them, and re-layouts: 2.73 us -> 1.16 us
    pallas_call x1 -> x2, Pallas kernels: 4.55 us -> 4.11 us  [the longest x1 3.42 us: body(): call(view_kernel, [((3, 3, HALO, 128), F32)] * 2 + [((SPAN, 3, 32, 128),...]
  transfers between devices with their start and end apart: 4 -> 3, of which waited for: 3 -> 3; matrix products, arithmetic and copies ran while one was open for 0% -> 0% of each run, Pallas kernels for 1% -> 2%
where the time goes in v6:
time: 78.5 us; the launch traced here: 78.1 us
  blocking collectives  32.3 us (41%)
  starting transfers between devices  29.6 us (38%)
  Pallas kernels  8.83 us (11%)
  waiting for transfers between devices  6.13 us (8%)
  local copies, waits for them, and re-layouts  1.16 us (1%)
    all_to_all x1, blocking collectives, body(): words = lax.all_to_all(words, 'zl', 0, 0)  16.5 us
    all_to_all x1, starting transfers between devices, body(): received = lax.all_to_all(chunks, VIEW, 0, 0)  16.2 us
    all_gather x1, blocking collectives, body(): words = lax.all_gather(words, ('x', 'c'))  13.9 us
    ppermute x1, starting transfers between devices, body(): edge = lax.ppermute(edge, across, strip_pairs(3, 4))  8.26 us
    ppermute x1, starting transfers between devices, body(): far = lax.ppermute(far, across, strip_pairs(1, 2))  5.15 us
    pallas_call x1, Pallas kernels, body(): call(view_kernel, [((3, 3, HALO, 128), F32)] * 2 + [((SPAN, 3, 32, 128),...  3.42 us
    all_to_all x1, waiting for transfers between devices, body(): received = lax.all_to_all(chunks, VIEW, 0, 0)  2.34 us
    ppermute x1, waiting for transfers between devices, body(): edge = lax.ppermute(edge, across, strip_pairs(3, 4))  2.01 us
  transfers between devices with their start and end apart: 3, of which 3 were waited for; matrix products, arithmetic and copies ran while one was open for 0% of the time, Pallas kernels for 2%

profile of v6, /device:TPU:25, one launch (start us, length us, event | category | flops | bytes accessed | tf_op | source)
XLA Modules:
  0.0 78.1 jit_solution(17659892610715632686)
XLA Ops:
  0.0 1.8 %shard_map.37 = bf16[64,8,128]{2,1,0:T(8,128)(2,1)} custom-call(bf16[1,48,1024]{2,1,0:T(8,128)(2,1)} %target_hbm.1, s32[1,2,3]{2,1,0:T(2,128)} %bitcast.5), custom_call_target="tpu_custom_call" | custom-call | tf_op jit(solution)/shard_map/pallas_call | solution.py:319
  1.8 16.2 %all-to-all-start = ((bf16[64,8,128]{2,1,0:T(8,128)(2,1)}), bf16[64,8,128]{2,1,0:T(8,128)(2,1)S(1)}, u32[]{:S(2)}, u32[]{:S(2)}) async-start(bf16[64,8,128]{2,1,0:T(8,128)(2,1)} %shard_map.37), calls=%async_computation | async-start | bytes 262144 | tf_op jit(solution)/shard_map/all_to_all | solution.py:332
  18.1 0.0 copy-start
  18.1 1.2 %copy-done = bf16[3,3,48,1024]{3,2,1,0:T(8,128)(2,1)S(1)} copy-done((bf16[3,3,48,1024]{3,2,1,0:T(8,128)(2,1)S(1)}, bf16[3,3,48,1024]{3,2,1,0:T(8,128)(2,1)}, u32[]{:S(2)}) %copy-start) | copy-done | bytes 884760
  19.2 0.1 shard_map.38
  19.4 8.3 %collective-permute-start = (f32[3,3,8,128]{3,2,1,0:T(8,128)S(1)}, f32[3,3,8,128]{3,2,1,0:T(8,128)S(1)}, u32[]{:S(2)}, u32[]{:S(2)}) collective-permute-start(f32[3,3,8,128]{3,2,1,0:T(8,128)S(1)} %get-tuple-element.18), channel_id=1, source_target_pairs={{136,129},{129,136},{9,2},{2,9},{138,131},{131,138},{11,388},{388,... | collective-permute-start | bytes 110600 | tf_op jit(solution)/shard_map/ppermute | solution.py:340
  27.7 2.0 %collective-permute-done.edge_ref = f32[3,3,8,128]{3,2,1,0:T(8,128)S(1)} collective-permute-done((f32[3,3,8,128]{3,2,1,0:T(8,128)S(1)}, f32[3,3,8,128]{3,2,1,0:T(8,128)S(1)}, u32[]{:S(2)}, u32[]{:S(2)}) %collective-permute-start) | collective-permute-done | bytes 36896 | tf_op jit(solution)/shard_map/ppermute | solution.py:340
  29.7 0.7 shard_map.39
  30.4 2.3 %all-to-all-done.recv_ref = bf16[64,8,128]{2,1,0:T(8,128)(2,1)S(1)} async-done(((bf16[64,8,128]{2,1,0:T(8,128)(2,1)}), bf16[64,8,128]{2,1,0:T(8,128)(2,1)S(1)}, u32[]{:S(2)}, u32[]{:S(2)}) %all-to-all-start) | async-done | bytes 131104 | tf_op jit(solution)/shard_map/all_to_all | solution.py:332
  32.7 3.4 %shard_map.40 = (f32[3,3,8,128]{3,2,1,0:T(8,128)S(1)}, f32[3,3,8,128]{3,2,1,0:T(8,128)S(1)}, f32[17,3,32,128]{3,2,1,0:T(8,128)S(1)}, f32[17,3,32,128]{3,2,1,0:T(...) custom-call(bf16[64,8,128]{2,1,0:T(8,128)(2,1)S(1)} %all-to-all-done, ...), custom_call_target="tpu_custom_call" | custom-call | tf_op jit(solution)/shard_map/pallas_call | solution.py:348
  36.1 5.2 %collective-permute-start.1 = (f32[3,3,8,128]{3,2,1,0:T(8,128)S(1)}, f32[3,3,8,128]{3,2,1,0:T(8,128)S(1)}, u32[]{:S(2)}, u32[]{:S(2)}) collective-permute-start(f32[3,3,8,128]{3,2,1,0:T(8,128)S(1)} %get-tuple-element.26), channel_id=1, source_target_pairs={{8,128},{128,8},{136,129},{129,136},{137,1},{1,137},{9,2},{2,9},{1... | collective-permute-start | bytes 110600 | tf_op jit(solution)/shard_map/ppermute | solution.py:354
  41.3 0.7 shard_map.41.own_ref
  42.0 1.9 %all-gather = f32[6,3,8,128]{3,2,1,0:T(8,128)S(1)} all-gather(f32[3,3,8,128]{3,2,1,0:T(8,128)S(1)} %get-tuple-element.27), channel_id=2, replica_groups=mesh['zl'=8,'x'=4,'c'=2,'zh'=2,'y'=4] {'c'}, dimensions={0}, use_global_device_ids=true | all-gather | bytes 110592 | tf_op jit(solution)/shard_map/all_gather | solution.py:361
  43.9 1.8 %collective-permute-done.1.far_ref = f32[3,3,8,128]{3,2,1,0:T(8,128)S(1)} collective-permute-done((f32[3,3,8,128]{3,2,1,0:T(8,128)S(1)}, f32[3,3,8,128]{3,2,1,0:T(8,128)S(1)}, u32[]{:S(2)}, u32[]{:S(2)}) %collective-permute-start.1) | collective-permute-done | bytes 36896 | tf_op jit(solution)/shard_map/ppermute | solution.py:354
  45.6 0.2 shard_map.42
  45.8 16.5 %all_to_all.10.words_ref = s32[8,32,128]{2,1,0:T(8,128)S(1)} all-to-all(s32[8,32,128]{2,1,0:T(8,128)S(1)} %shard_map.42), channel_id=1, replica_groups=mesh['zl'=8,'x'=4,'c'=2,'zh'=2,'y'=4] {'zl'}, dimensions={0} | all-to-all | bytes 262144 | tf_op jit(solution)/shard_map/all_to_all | solution.py:369
  62.3 13.9 %all-gather.1 = s32[1920,128]{1,0:T(8,128)S(1)} all-gather(s32[240,128]{1,0:T(8,128)S(1)} %shard_map.43), channel_id=3, replica_groups=mesh['zl'=8,'x'=4,'c'=2,'zh'=2,'y'=4] {'x','c'}, dimensions={0}, use_global_device_ids=true | all-gather | bytes 1105920 | tf_op jit(solution)/shard_map/all_gather | solution.py:371
  76.3 1.9 %shard_map.44 = f32[3,3,48,1024]{3,2,1,0:T(8,128)} custom-call(s32[8,240,128]{2,1,0:T(8,128)S(1)} %bitcast.3), custom_call_target="tpu_custom_call" | custom-call | tf_op jit(solution)/shard_map/pallas_call | solution.py:373
  (1 shorter events, 0.0 us)
Async XLA Ops:
  1.8 30.9 %all-to-all-start = ((bf16[64,8,128]{2,1,0:T(8,128)(2,1)}), bf16[64,8,128]{2,1,0:T(8,128)(2,1)S(1)}, u32[]{:S(2)}, u32[]{:S(2)}) async-start(bf16[64,8,128]{2,1,0:T(8,128)(2,1)} %shard_map.37), calls=%async_computation | async-start | bytes 262144 | tf_op jit(solution)/shard_map/all_to_all | solution.py:332
  18.1 1.2 %copy-start = (bf16[3,3,48,1024]{3,2,1,0:T(8,128)(2,1)S(1)}, bf16[3,3,48,1024]{3,2,1,0:T(8,128)(2,1)}, u32[]{:S(2)}) copy-start(bf16[3,3,48,1024]{3,2,1,0:T(8,128)(2,1)} %layers_ref.1) | copy-start | bytes 2654212
  19.4 10.3 %collective-permute-start = (f32[3,3,8,128]{3,2,1,0:T(8,128)S(1)}, f32[3,3,8,128]{3,2,1,0:T(8,128)S(1)}, u32[]{:S(2)}, u32[]{:S(2)}) collective-permute-start(f32[3,3,8,128]{3,2,1,0:T(8,128)S(1)} %get-tuple-element.18), channel_id=1, source_target_pairs={{136,129},{129,136},{9,2},{2,9},{138,131},{131,138},{11,388},{388,... | collective-permute-start | bytes 110600 | tf_op jit(solution)/shard_map/ppermute | solution.py:340
  36.1 9.5 %collective-permute-start.1 = (f32[3,3,8,128]{3,2,1,0:T(8,128)S(1)}, f32[3,3,8,128]{3,2,1,0:T(8,128)S(1)}, u32[]{:S(2)}, u32[]{:S(2)}) collective-permute-start(f32[3,3,8,128]{3,2,1,0:T(8,128)S(1)} %get-tuple-element.26), channel_id=1, source_target_pairs={{8,128},{128,8},{136,129},{129,136},{137,1},{1,137},{9,2},{2,9},{1... | collective-permute-start | bytes 110600 | tf_op jit(solution)/shard_map/ppermute | solution.py:354

commit v7 on v6

--- a/solution.py
+++ b/solution.py
@@ -12,7 +12,8 @@
 REGULAR = 0.05
 CODE_STEPS = 5041.0
 CODE_BASE = 7.0
-WORDS = 30
+MAIN = 24
+REST = 3
 F32 = jnp.float32
 BF16 = jnp.bfloat16
 I32 = jnp.int32
@@ -48,13 +49,41 @@
     return column >> 1, column & 1, q
 
 
+def window(block, half):
+    first = block - 1 + half
+    left = pl.multiple_of(jnp.maximum(first, 0) * 128, 128)
+    right = pl.multiple_of(jnp.minimum(first + 1, 7) * 128, 128)
+    there = jnp.where(first >= 0, 1.0, 0.0), jnp.where(first < 7, 1.0, 0.0)
+    return left, right, there, jnp.where(half == 0, 16, 80)
+
+
+def joined(a, b, there, amount):
+    lane = lanes(a.shape[0])
+    a = a.astype(F32) * there[0]
+    b = b.astype(F32) * there[1]
+    return pltpu.roll(jnp.where(lane >= 128 - amount, a, b), amount, 1)
+
+
 def pack_kernel(
-    target_hbm, shifts_hbm, chunks_ref, target_ref, shifts_ref, wide_ref, target_sem, shifts_sem
+    target_hbm, shifts_hbm, layers_hbm, chunks_ref, edge_out,
+    target_ref, shifts_ref, near_edge, wide_ref, target_sem, shifts_sem, edge_sems,
 ):
     fetch_shifts = pltpu.make_async_copy(shifts_hbm, shifts_ref, shifts_sem)
     fetch_shifts.start()
     fetch = pltpu.make_async_copy(target_hbm, target_ref, target_sem)
     fetch.start()
+    block, half, q = my_tile()
+    last = q == 3
+    left, right, there, amount = window(block, half)
+    start = pl.multiple_of(jnp.where(last, 32, 0), 16)
+    fetch_edges = [
+        pltpu.make_async_copy(
+            layers_hbm.at[:, :, pl.ds(start, 16), pl.ds(side, 128)], near_edge.at[i], edge_sems.at[i]
+        )
+        for i, side in enumerate((left, right))
+    ]
+    for one in fetch_edges:
+        one.start()
     high, odd = place()
     fetch.wait()
     lane = lanes(48)
@@ -86,42 +115,47 @@
                 pieces = jnp.where(upper_half, pltpu.roll(first, 80, 1), pltpu.roll(second, 40, 1))
                 chunk = jnp.where(lane < 80, main, jnp.where(lane < 120, pieces, extra))
                 chunks_ref[(zl * 4 + x) * 2 + c] = chunk.astype(BF16)
-
-
-def strip_kernel(layers_ref, own_ref, edge_ref):
+    for one in fetch_edges:
+        one.wait()
+    for layer in range(3):
+        for frame in range(3):
+            a, b = near_edge[0, frame, layer], near_edge[1, frame, layer]
+            cells = joined(a, b, there, amount)
+            edge_out[layer, frame] = jnp.where(last, cells[HALO:], cells[:HALO])
+
+
+def seen_kernel(layers_ref, seen_ref, tile_ref, tall_ref):
     block, half, q = my_tile()
-    last = q == 3
-    block = block - 1 + half
-    amount = jnp.where(half == 0, 16, 80)
-    left = pl.multiple_of(jnp.maximum(block, 0) * 128, 128)
-    right = pl.multiple_of(jnp.minimum(block + 1, 7) * 128, 128)
-    left_there = jnp.where(block >= 0, 1.0, 0.0)
-    right_there = jnp.where(block + 1 <= 7, 1.0, 0.0)
-    lane = lanes(48)
+    left, right, there, amount = window(block, half)
+    start = q * TALL
     for layer in range(3):
         for frame in range(3):
-            a = layers_ref[frame, layer, :, pl.ds(left, 128)].astype(F32) * left_there
-            b = layers_ref[frame, layer, :, pl.ds(right, 128)].astype(F32) * right_there
-            cells = pltpu.roll(jnp.where(lane >= 128 - amount, a, b), amount, 1)
-            own_ref[layer, frame] = cells
-            edge_ref[layer, frame] = jnp.where(last, cells[48 - HALO :], cells[:HALO])
-
-
-def seen_kernel(own_ref, edge_ref, seen_ref, tile_ref, tall_ref):
-    _, _, q = my_tile()
-    start = q * TALL
-    tall_ref[:, :, :HALO] = edge_ref[...]
-    tall_ref[:, :, HALO : HALO + 48] = own_ref[...]
-    tall_ref[:, :, HALO + 48 : 64] = edge_ref[...]
-    tall_ref[:, :, 64:] = jnp.zeros((3, 3, 8, 128), F32)
-    for layer in range(3):
-        for frame in range(3):
+            a = layers_ref[frame, layer, :, pl.ds(left, 128)]
+            b = layers_ref[frame, layer, :, pl.ds(right, 128)]
+            tall_ref[layer, frame, :HALO] = jnp.zeros((HALO, 128), F32)
+            tall_ref[layer, frame, HALO : HALO + 48] = joined(a, b, there, amount)
+            tall_ref[layer, frame, HALO + 48 :] = jnp.zeros((16, 128), F32)
             cells = tall_ref[layer, frame, pl.ds(start, 32), :]
             for d in range(SPAN):
                 moved = pltpu.roll(cells, 128 - d, 1) if d else cells
                 seen_ref[layer, d, frame] = moved
                 if d == 16:
                     tile_ref[layer, frame] = moved[HALO : HALO + 16]
+
+
+def edge_kernel(seen_in, edge_ref, seen_ref):
+    _, _, q = my_tile()
+    seen_ref[...] = seen_in[...]
+
+    @pl.when((q == 0) | (q == 3))
+    def _():
+        start = jnp.where(q == 0, 0, HALO + TALL)
+        for layer in range(3):
+            for frame in range(3):
+                cells = edge_ref[layer, frame]
+                for d in range(SPAN):
+                    moved = pltpu.roll(cells, 128 - d, 1) if d else cells
+                    seen_ref[layer, d, frame, pl.ds(start, HALO), :] = moved
 
 
 def view_kernel(
@@ -227,15 +261,20 @@
         word = parts[0] + (parts[1] - 32768) * 65536
         for copy in range(8):
             out_ref[copy, TALL * pair : TALL * pair + TALL] = word
-    word = code_ref[8, :6] + (code_ref[8, 6:12] - 32768) * 65536
+    code_ref[8, :6] = jnp.where(
+        lanes(6) < WIDE, code_ref[8, :6], pltpu.roll(code_ref[8, 6:TALL], WIDE, 1)
+    )
+    word = code_ref[8, :REST] + (code_ref[8, REST : 2 * REST] - 32768) * 65536
     for copy in range(8):
-        out_ref[copy, 24:30] = word
-        out_ref[copy, 30:] = jnp.zeros((2, 128), I32)
+        out_ref[copy, MAIN : MAIN + REST] = word
+        out_ref[copy, MAIN + REST :] = jnp.zeros((5, 128), I32)
 
 
 def dense_kernel(words_ref, out_ref):
     for zl in range(8):
-        out_ref[WORDS * zl : WORDS * zl + WORDS] = words_ref[zl, :WORDS]
+        out_ref[MAIN * zl : MAIN * zl + MAIN] = words_ref[zl, :MAIN]
+        at = 8 * MAIN + REST * zl
+        out_ref[at : at + REST] = words_ref[zl, MAIN : MAIN + REST]
 
 
 def decoded(code):
@@ -253,23 +292,26 @@
         for q in range(4):
             rows = slice(TALL * q, TALL * q + TALL)
 
-            def words(half, first, count):
-                zl, x, c = home(d, half, q, high, flip)
-                return words_ref[x * 2 + c, pl.ds(zl * WORDS + first, count), :]
-
-            lane = lanes(TALL)
-            for pair in range(2):
-                a, b = words(0, TALL * pair, TALL), words(1, TALL * pair, TALL)
+            places = [home(d, half, q, high, flip) for half in range(2)]
+
+            def halves(first, count, step):
+                a, b = (
+                    words_ref[x * 2 + c, pl.ds(first + step * zl, count), :] for zl, x, c in places
+                )
+                lane = lanes(count)
                 even = jnp.where(lane < WIDE, a, pltpu.roll(b, WIDE, 1))
-                odd = jnp.where(lane < WIDE, pltpu.roll(a, WIDE, 1), b)
-                for side, word in enumerate((even, odd)):
-                    for p, code in ((pair, word & 65535), (pair + 2, (word >> 16) + 32768)):
-                        at = 2 * p + side
-                        block_ref[d, at // 3, at % 3, rows] = decoded(code)
-            a, b = words(0, 24, 6), words(1, 24, 6)
-            word = jnp.where(lanes(6) < WIDE, a, pltpu.roll(b, WIDE, 1))
-            block_ref[d, 2, 2, TALL * q : TALL * q + 6] = decoded(word & 65535)
-            block_ref[d, 2, 2, TALL * q + 6 : TALL * q + TALL] = decoded((word >> 16) + 32768)
+                return even, jnp.where(lane < WIDE, pltpu.roll(a, WIDE, 1), b)
+
+            for side, word in enumerate(halves(0, MAIN, MAIN)):
+                for p, code in ((0, word & 65535), (2, (word >> 16) + 32768)):
+                    value = decoded(code)
+                    for pair in range(2):
+                        at = 2 * (p + pair) + side
+                        block_ref[d, at // 3, at % 3, rows] = value[TALL * pair : TALL * pair + TALL]
+            for side, word in enumerate(halves(8 * MAIN, REST, REST)):
+                for part, code in ((0, word & 65535), (1, (word >> 16) + 32768)):
+                    at = TALL * q + 6 * side + REST * part
+                    block_ref[d, 2, 2, at : at + REST] = decoded(code)
         sent(d).start()
         return carry
 
@@ -316,34 +358,33 @@
 
 
 def body(layers, target, shifts):
-    (chunks,) = call(
+    across = VIEW + ROW
+    chunks, edge = call(
         pack_kernel,
-        [((64, 8, 128), BF16)],
-        [pl.BlockSpec(memory_space=pltpu.HBM)] * 2,
+        [((64, 8, 128), BF16), ((3, 3, HALO, 128), F32)],
+        [pl.BlockSpec(memory_space=pltpu.HBM)] * 3,
         [
             pltpu.VMEM((1, 48, 1024), BF16),
             pltpu.SMEM((1, 2, 3), I32),
+            pltpu.VMEM((2, 3, 3, 16, 128), BF16),
             pltpu.VMEM((16, 56, 128), F32),
             pltpu.SemaphoreType.DMA,
             pltpu.SemaphoreType.DMA,
+            pltpu.SemaphoreType.DMA((2,)),
         ],
         WHOLE,
-    )(target, shifts.transpose(0, 2, 1))
+    )(target, shifts.transpose(0, 2, 1), layers)
     received = lax.all_to_all(chunks, VIEW, 0, 0)
 
-    own, edge = call(
-        strip_kernel,
-        [((3, 3, 48, 128), F32), ((3, 3, HALO, 128), F32)],
-        [VMEM],
-    )(layers)
-    across = VIEW + ROW
     edge = lax.ppermute(edge, across, strip_pairs(3, 4))
     seen, tile = call(
         seen_kernel,
         [((3, SPAN, 3, 32, 128), F32), ((3, 3, 16, 128), F32)],
-        [VMEM] * 2,
+        [VMEM],
         [pltpu.VMEM((3, 3, 72, 128), F32)],
-    )(own, edge)
+        cost=pl.CostEstimate(flops=1_000_000, bytes_accessed=3_600_000, transcendentals=0),
+    )(layers)
+    (seen,) = call(edge_kernel, [((3, SPAN, 3, 32, 128), F32)], [VMEM] * 2)(seen, edge)
 
     far, near, *sums = call(
         view_kernel,
@@ -367,7 +408,7 @@
         [pltpu.VMEM((9, 16, 128), I32)],
     )(own, far, near, tile)
     words = lax.all_to_all(words, "zl", 0, 0)
-    (words,) = call(dense_kernel, [((8 * WORDS, 128), I32)], [VMEM])(words)
+    (words,) = call(dense_kernel, [((8 * (MAIN + REST), 128), I32)], [VMEM])(words)
     words = lax.all_gather(words, ("x", "c"))
 
     return pl.pallas_call(

time: 78.5 us -> 77 us (0.981)
  blocking collectives: 32.3 us -> 30.8 us
  starting transfers between devices: 29.6 us -> 28.2 us
  Pallas kernels: 8.83 us -> 9.67 us
    ppermute x1, waiting for transfers between devices: 2.01 us -> 0.01 us  [body(): edge = lax.ppermute(edge, across, strip_pairs(3, 4))]
    ppermute x1, starting transfers between devices: 5.15 us -> 3.72 us  [body(): far = lax.ppermute(far, across, strip_pairs(1, 2))]
    ppermute x1, waiting for transfers between devices: 1.78 us -> 3.21 us  [body(): far = lax.ppermute(far, across, strip_pairs(1, 2))]
    all_to_all x1, blocking collectives: 16.5 us -> 15.3 us  [body(): words = lax.all_to_all(words, 'zl', 0, 0)]
    all_to_all x1, waiting for transfers between devices: 2.34 us -> 3.5 us  [body(): received = lax.all_to_all(chunks, VIEW, 0, 0)]
  transfers between devices with their start and end apart: 3 -> 3, of which waited for: 3 -> 2; matrix products, arithmetic and copies ran while one was open for 0% -> 0% of each run, Pallas kernels for 2% -> 3%
where the time goes in v7:
time: 77 us; the launch traced here: 76.7 us
  blocking collectives  30.8 us (40%)
  starting transfers between devices  28.2 us (37%)
  Pallas kernels  9.67 us (13%)
  waiting for transfers between devices  6.71 us (9%)
  local copies, waits for them, and re-layouts  1.16 us (2%)
    all_to_all x1, starting transfers between devices, body(): received = lax.all_to_all(chunks, VIEW, 0, 0)  16.2 us
    all_to_all x1, blocking collectives, body(): words = lax.all_to_all(words, 'zl', 0, 0)  15.3 us
    all_gather x1, blocking collectives, body(): words = lax.all_gather(words, ('x', 'c'))  13.7 us
    ppermute x1, starting transfers between devices, body(): edge = lax.ppermute(edge, across, strip_pairs(3, 4))  8.26 us
    ppermute x1, starting transfers between devices, body(): far = lax.ppermute(far, across, strip_pairs(1, 2))  3.72 us
    all_to_all x1, waiting for transfers between devices, body(): received = lax.all_to_all(chunks, VIEW, 0, 0)  3.5 us
    pallas_call x1, Pallas kernels, body(): call(view_kernel, [((3, 3, HALO, 128), F32)] * 2 + [((SPAN, 3, 32, 128),...  3.41 us
    ppermute x1, waiting for transfers between devices, body(): far = lax.ppermute(far, across, strip_pairs(1, 2))  3.21 us
  transfers between devices with their start and end apart: 3, of which 2 were waited for; matrix products, arithmetic and copies ran while one was open for 0% of the time, Pallas kernels for 3%

profile of v7, /device:TPU:25, one launch (start us, length us, event | category | flops | bytes accessed | tf_op | source)
XLA Modules:
  0.0 76.7 jit_solution(10151629685124307180)
XLA Ops:
  0.0 1.9 %shard_map.37 = (bf16[64,8,128]{2,1,0:T(8,128)(2,1)}, f32[3,3,8,128]{3,2,1,0:T(8,128)}) custom-call(bf16[1,48,1024]{2,1,0:T(8,128)(2,1)} %target_hbm.1, s32[1,2,3]{2,1,0:T(2,128)} %bitcast.5, bf16[3,3,48,1024]{3,2,1,0:T(8,128)(2,1)} %layers_ref.1), custom_call_target="tpu_custom_call" | custom-call | tf_op jit(solution)/shard_map/pallas_call | solution.py:362
  1.9 16.2 %all-to-all-start = ((bf16[64,8,128]{2,1,0:T(8,128)(2,1)}), bf16[64,8,128]{2,1,0:T(8,128)(2,1)S(1)}, u32[]{:S(2)}, u32[]{:S(2)}) async-start(bf16[64,8,128]{2,1,0:T(8,128)(2,1)} %get-tuple-element.17), calls=%async_computation | async-start | bytes 262144 | tf_op jit(solution)/shard_map/all_to_all | solution.py:377
  18.1 8.3 %collective-permute-start = (f32[3,3,8,128]{3,2,1,0:T(8,128)}, f32[3,3,8,128]{3,2,1,0:T(8,128)S(1)}, u32[]{:S(2)}, u32[]{:S(2)}) collective-permute-start(f32[3,3,8,128]{3,2,1,0:T(8,128)} %get-tuple-element.19), channel_id=1, source_target_pairs={{136,129},{129,136},{9,2},{2,9},{138,131},{131,138},{11,388},{388,... | collective-permute-start | bytes 110600 | tf_op jit(solution)/shard_map/ppermute | solution.py:379
  26.4 0.0 copy-start
  26.4 1.2 %copy-done = bf16[3,3,48,1024]{3,2,1,0:T(8,128)(2,1)S(1)} copy-done((bf16[3,3,48,1024]{3,2,1,0:T(8,128)(2,1)S(1)}, bf16[3,3,48,1024]{3,2,1,0:T(8,128)(2,1)}, u32[]{:S(2)}) %copy-start) | copy-done | bytes 884760
  27.6 1.3 %shard_map.38 = (f32[3,17,3,32,128]{4,3,2,1,0:T(8,128)S(1)}, f32[3,3,16,128]{3,2,1,0:T(8,128)S(1)}) custom-call(bf16[3,3,48,1024]{3,2,1,0:T(8,128)(2,1)S(1)} %copy-done), custom_call_target="tpu_custom_call" | custom-call | flops 1000000 | bytes 3600000 | tf_op jit(solution)/shard_map/pallas_call | solution.py:380
  28.9 0.0 collective-permute-done.edge_ref
  28.9 0.4 shard_map.39.seen_ref
  29.3 3.5 %all-to-all-done.recv_ref = bf16[64,8,128]{2,1,0:T(8,128)(2,1)S(1)} async-done(((bf16[64,8,128]{2,1,0:T(8,128)(2,1)}), bf16[64,8,128]{2,1,0:T(8,128)(2,1)S(1)}, u32[]{:S(2)}, u32[]{:S(2)}) %all-to-all-start) | async-done | bytes 131104 | tf_op jit(solution)/shard_map/all_to_all | solution.py:377
  32.8 3.4 %shard_map.40 = (f32[3,3,8,128]{3,2,1,0:T(8,128)S(1)}, f32[3,3,8,128]{3,2,1,0:T(8,128)S(1)}, f32[17,3,32,128]{3,2,1,0:T(8,128)S(1)}, f32[17,3,32,128]{3,2,1,0:T(...) custom-call(bf16[64,8,128]{2,1,0:T(8,128)(2,1)S(1)} %all-to-all-done, ...), custom_call_target="tpu_custom_call" | custom-call | tf_op jit(solution)/shard_map/pallas_call | solution.py:389
  36.2 3.7 %collective-permute-start.1 = (f32[3,3,8,128]{3,2,1,0:T(8,128)S(1)}, f32[3,3,8,128]{3,2,1,0:T(8,128)S(1)}, u32[]{:S(2)}, u32[]{:S(2)}) collective-permute-start(f32[3,3,8,128]{3,2,1,0:T(8,128)S(1)} %get-tuple-element.26), channel_id=1, source_target_pairs={{8,128},{128,8},{136,129},{129,136},{137,1},{1,137},{9,2},{2,9},{1... | collective-permute-start | bytes 110600 | tf_op jit(solution)/shard_map/ppermute | solution.py:395
  39.9 0.7 shard_map.41.own_ref
  40.6 1.9 %all-gather = f32[6,3,8,128]{3,2,1,0:T(8,128)S(1)} all-gather(f32[3,3,8,128]{3,2,1,0:T(8,128)S(1)} %get-tuple-element.27), channel_id=2, replica_groups=mesh['zl'=8,'x'=4,'c'=2,'zh'=2,'y'=4] {'c'}, dimensions={0}, use_global_device_ids=true | all-gather | bytes 110592 | tf_op jit(solution)/shard_map/all_gather | solution.py:402
  42.5 3.2 %collective-permute-done.1.far_ref = f32[3,3,8,128]{3,2,1,0:T(8,128)S(1)} collective-permute-done((f32[3,3,8,128]{3,2,1,0:T(8,128)S(1)}, f32[3,3,8,128]{3,2,1,0:T(8,128)S(1)}, u32[]{:S(2)}, u32[]{:S(2)}) %collective-permute-start.1) | collective-permute-done | bytes 36896 | tf_op jit(solution)/shard_map/ppermute | solution.py:395
  45.7 0.2 shard_map.42
  45.9 15.3 %all_to_all.10.words_ref = s32[8,32,128]{2,1,0:T(8,128)S(1)} all-to-all(s32[8,32,128]{2,1,0:T(8,128)S(1)} %shard_map.42), channel_id=1, replica_groups=mesh['zl'=8,'x'=4,'c'=2,'zh'=2,'y'=4] {'zl'}, dimensions={0} | all-to-all | bytes 262144 | tf_op jit(solution)/shard_map/all_to_all | solution.py:410
  61.2 13.7 %all-gather.1 = s32[1728,128]{1,0:T(8,128)S(1)} all-gather(s32[216,128]{1,0:T(8,128)S(1)} %shard_map.43), channel_id=3, replica_groups=mesh['zl'=8,'x'=4,'c'=2,'zh'=2,'y'=4] {'x','c'}, dimensions={0}, use_global_device_ids=true | all-gather | bytes 995328 | tf_op jit(solution)/shard_map/all_gather | solution.py:412
  74.9 1.8 %shard_map.44 = f32[3,3,48,1024]{3,2,1,0:T(8,128)} custom-call(s32[8,216,128]{2,1,0:T(8,128)S(1)} %bitcast.3), custom_call_target="tpu_custom_call" | custom-call | tf_op jit(solution)/shard_map/pallas_call | solution.py:414
  (1 shorter events, 0.0 us)
Async XLA Ops:
  1.9 30.9 %all-to-all-start = ((bf16[64,8,128]{2,1,0:T(8,128)(2,1)}), bf16[64,8,128]{2,1,0:T(8,128)(2,1)S(1)}, u32[]{:S(2)}, u32[]{:S(2)}) async-start(bf16[64,8,128]{2,1,0:T(8,128)(2,1)} %get-tuple-element.17), calls=%async_computation | async-start | bytes 262144 | tf_op jit(solution)/shard_map/all_to_all | solution.py:377
  18.1 10.7 %collective-permute-start = (f32[3,3,8,128]{3,2,1,0:T(8,128)}, f32[3,3,8,128]{3,2,1,0:T(8,128)S(1)}, u32[]{:S(2)}, u32[]{:S(2)}) collective-permute-start(f32[3,3,8,128]{3,2,1,0:T(8,128)} %get-tuple-element.19), channel_id=1, source_target_pairs={{136,129},{129,136},{9,2},{2,9},{138,131},{131,138},{11,388},{388,... | collective-permute-start | bytes 110600 | tf_op jit(solution)/shard_map/ppermute | solution.py:379
  26.4 1.2 %copy-start = (bf16[3,3,48,1024]{3,2,1,0:T(8,128)(2,1)S(1)}, bf16[3,3,48,1024]{3,2,1,0:T(8,128)(2,1)}, u32[]{:S(2)}) copy-start(bf16[3,3,48,1024]{3,2,1,0:T(8,128)(2,1)} %layers_ref.1) | copy-start | bytes 2654212
  36.2 9.5 %collective-permute-start.1 = (f32[3,3,8,128]{3,2,1,0:T(8,128)S(1)}, f32[3,3,8,128]{3,2,1,0:T(8,128)S(1)}, u32[]{:S(2)}, u32[]{:S(2)}) collective-permute-start(f32[3,3,8,128]{3,2,1,0:T(8,128)S(1)} %get-tuple-element.26), channel_id=1, source_target_pairs={{8,128},{128,8},{136,129},{129,136},{137,1},{1,137},{9,2},{2,9},{1... | collective-permute-start | bytes 110600 | tf_op jit(solution)/shard_map/ppermute | solution.py:395

commit v8 on v7

--- a/solution.py
+++ b/solution.py
@@ -272,9 +272,12 @@
 
 def dense_kernel(words_ref, out_ref):
     for zl in range(8):
-        out_ref[MAIN * zl : MAIN * zl + MAIN] = words_ref[zl, :MAIN]
+        main = words_ref[zl, :MAIN]
+        rest = words_ref[zl, MAIN : MAIN + REST]
         at = 8 * MAIN + REST * zl
-        out_ref[at : at + REST] = words_ref[zl, MAIN : MAIN + REST]
+        for copy in range(4):
+            out_ref[copy, MAIN * zl : MAIN * zl + MAIN] = main
+            out_ref[copy, at : at + REST] = rest
 
 
 def decoded(code):
@@ -296,7 +299,7 @@
 
             def halves(first, count, step):
                 a, b = (
-                    words_ref[x * 2 + c, pl.ds(first + step * zl, count), :] for zl, x, c in places
+                    words_ref[c, x, pl.ds(first + step * zl, count), :] for zl, x, c in places
                 )
                 lane = lanes(count)
                 even = jnp.where(lane < WIDE, a, pltpu.roll(b, WIDE, 1))
@@ -408,8 +411,9 @@
         [pltpu.VMEM((9, 16, 128), I32)],
     )(own, far, near, tile)
     words = lax.all_to_all(words, "zl", 0, 0)
-    (words,) = call(dense_kernel, [((8 * (MAIN + REST), 128), I32)], [VMEM])(words)
-    words = lax.all_gather(words, ("x", "c"))
+    (words,) = call(dense_kernel, [((4, 8 * (MAIN + REST), 128), I32)], [VMEM])(words)
+    words = lax.all_to_all(words, "x", 0, 0)
+    words = lax.all_gather(words, "c")
 
     return pl.pallas_call(
         spread_kernel,

time: 77 us -> 76.5 us (level)
    all_gather x1, blocking collectives: 13.7 us -> 2.43 us  [body(): words = lax.all_gather(words, 'c')]
    all_to_all x0 -> x1, blocking collectives: none -> 10.7 us  [body(): words = lax.all_to_all(words, 'x', 0, 0)]
where the time goes in v8:
time: 76.5 us; the launch traced here: 76.1 us
  blocking collectives  30.2 us (39%)
  starting transfers between devices  28.2 us (37%)
  Pallas kernels  9.71 us (13%)
  waiting for transfers between devices  6.71 us (9%)
  local copies, waits for them, and re-layouts  1.16 us (2%)
    all_to_all x1, starting transfers between devices, body(): received = lax.all_to_all(chunks, VIEW, 0, 0)  16.2 us
    all_to_all x1, blocking collectives, body(): words = lax.all_to_all(words, 'zl', 0, 0)  15.3 us
    all_to_all x1, blocking collectives, body(): words = lax.all_to_all(words, 'x', 0, 0)  10.7 us
    ppermute x1, starting transfers between devices, body(): edge = lax.ppermute(edge, across, strip_pairs(3, 4))  8.26 us
    ppermute x1, starting transfers between devices, body(): far = lax.ppermute(far, across, strip_pairs(1, 2))  3.72 us
    all_to_all x1, waiting for transfers between devices, body(): received = lax.all_to_all(chunks, VIEW, 0, 0)  3.5 us
    pallas_call x1, Pallas kernels, body(): call(view_kernel, [((3, 3, HALO, 128), F32)] * 2 + [((SPAN, 3, 32, 128),...  3.43 us
    ppermute x1, waiting for transfers between devices, body(): far = lax.ppermute(far, across, strip_pairs(1, 2))  3.21 us
  transfers between devices with their start and end apart: 3, of which 2 were waited for; matrix products, arithmetic and copies ran while one was open for 0% of the time, Pallas kernels for 3%

profile of v8, /device:TPU:25, one launch (start us, length us, event | category | flops | bytes accessed | tf_op | source)
XLA Modules:
  0.0 76.1 jit_solution(3444740261967512011)
XLA Ops:
  0.0 1.9 %shard_map.37 = (bf16[64,8,128]{2,1,0:T(8,128)(2,1)}, f32[3,3,8,128]{3,2,1,0:T(8,128)}) custom-call(bf16[1,48,1024]{2,1,0:T(8,128)(2,1)} %target_hbm.1, s32[1,2,3]{2,1,0:T(2,128)} %bitcast.5, bf16[3,3,48,1024]{3,2,1,0:T(8,128)(2,1)} %layers_ref.1), custom_call_target="tpu_custom_call" | custom-call | tf_op jit(solution)/shard_map/pallas_call | solution.py:365
  1.9 16.2 %all-to-all-start = ((bf16[64,8,128]{2,1,0:T(8,128)(2,1)}), bf16[64,8,128]{2,1,0:T(8,128)(2,1)S(1)}, u32[]{:S(2)}, u32[]{:S(2)}) async-start(bf16[64,8,128]{2,1,0:T(8,128)(2,1)} %get-tuple-element.17), calls=%async_computation | async-start | bytes 262144 | tf_op jit(solution)/shard_map/all_to_all | solution.py:380
  18.1 8.3 %collective-permute-start = (f32[3,3,8,128]{3,2,1,0:T(8,128)}, f32[3,3,8,128]{3,2,1,0:T(8,128)S(1)}, u32[]{:S(2)}, u32[]{:S(2)}) collective-permute-start(f32[3,3,8,128]{3,2,1,0:T(8,128)} %get-tuple-element.19), channel_id=1, source_target_pairs={{136,129},{129,136},{9,2},{2,9},{138,131},{131,138},{11,388},{388,... | collective-permute-start | bytes 110600 | tf_op jit(solution)/shard_map/ppermute | solution.py:382
  26.4 0.0 copy-start
  26.4 1.2 %copy-done = bf16[3,3,48,1024]{3,2,1,0:T(8,128)(2,1)S(1)} copy-done((bf16[3,3,48,1024]{3,2,1,0:T(8,128)(2,1)S(1)}, bf16[3,3,48,1024]{3,2,1,0:T(8,128)(2,1)}, u32[]{:S(2)}) %copy-start) | copy-done | bytes 884760
  27.6 1.3 %shard_map.38 = (f32[3,17,3,32,128]{4,3,2,1,0:T(8,128)S(1)}, f32[3,3,16,128]{3,2,1,0:T(8,128)S(1)}) custom-call(bf16[3,3,48,1024]{3,2,1,0:T(8,128)(2,1)S(1)} %copy-done), custom_call_target="tpu_custom_call" | custom-call | flops 1000000 | bytes 3600000 | tf_op jit(solution)/shard_map/pallas_call | solution.py:383
  28.9 0.0 collective-permute-done.edge_ref
  28.9 0.4 shard_map.39.seen_ref
  29.3 3.5 %all-to-all-done.recv_ref = bf16[64,8,128]{2,1,0:T(8,128)(2,1)S(1)} async-done(((bf16[64,8,128]{2,1,0:T(8,128)(2,1)}), bf16[64,8,128]{2,1,0:T(8,128)(2,1)S(1)}, u32[]{:S(2)}, u32[]{:S(2)}) %all-to-all-start) | async-done | bytes 131104 | tf_op jit(solution)/shard_map/all_to_all | solution.py:380
  32.8 3.4 %shard_map.40 = (f32[3,3,8,128]{3,2,1,0:T(8,128)S(1)}, f32[3,3,8,128]{3,2,1,0:T(8,128)S(1)}, f32[17,3,32,128]{3,2,1,0:T(8,128)S(1)}, f32[17,3,32,128]{3,2,1,0:T(...) custom-call(bf16[64,8,128]{2,1,0:T(8,128)(2,1)S(1)} %all-to-all-done, ...), custom_call_target="tpu_custom_call" | custom-call | tf_op jit(solution)/shard_map/pallas_call | solution.py:392
  36.2 3.7 %collective-permute-start.1 = (f32[3,3,8,128]{3,2,1,0:T(8,128)S(1)}, f32[3,3,8,128]{3,2,1,0:T(8,128)S(1)}, u32[]{:S(2)}, u32[]{:S(2)}) collective-permute-start(f32[3,3,8,128]{3,2,1,0:T(8,128)S(1)} %get-tuple-element.26), channel_id=1, source_target_pairs={{8,128},{128,8},{136,129},{129,136},{137,1},{1,137},{9,2},{2,9},{1... | collective-permute-start | bytes 110600 | tf_op jit(solution)/shard_map/ppermute | solution.py:398
  39.9 0.7 shard_map.41.own_ref
  40.6 1.9 %all-gather = f32[6,3,8,128]{3,2,1,0:T(8,128)S(1)} all-gather(f32[3,3,8,128]{3,2,1,0:T(8,128)S(1)} %get-tuple-element.27), channel_id=2, replica_groups=mesh['zl'=8,'x'=4,'c'=2,'zh'=2,'y'=4] {'c'}, dimensions={0}, use_global_device_ids=true | all-gather | bytes 110592 | tf_op jit(solution)/shard_map/all_gather | solution.py:405
  42.5 3.2 %collective-permute-done.1.far_ref = f32[3,3,8,128]{3,2,1,0:T(8,128)S(1)} collective-permute-done((f32[3,3,8,128]{3,2,1,0:T(8,128)S(1)}, f32[3,3,8,128]{3,2,1,0:T(8,128)S(1)}, u32[]{:S(2)}, u32[]{:S(2)}) %collective-permute-start.1) | collective-permute-done | bytes 36896 | tf_op jit(solution)/shard_map/ppermute | solution.py:398
  45.7 0.2 shard_map.42
  45.9 15.3 %all_to_all.15.words_ref = s32[8,32,128]{2,1,0:T(8,128)S(1)} all-to-all(s32[8,32,128]{2,1,0:T(8,128)S(1)} %shard_map.42), channel_id=1, replica_groups=mesh['zl'=8,'x'=4,'c'=2,'zh'=2,'y'=4] {'zl'}, dimensions={0} | all-to-all | bytes 262144 | tf_op jit(solution)/shard_map/all_to_all | solution.py:413
  61.2 10.7 %all_to_all.16 = s32[4,216,128]{2,1,0:T(8,128)S(1)} all-to-all(s32[4,216,128]{2,1,0:T(8,128)S(1)} %shard_map.43), channel_id=1, replica_groups=mesh['zl'=8,'x'=4,'c'=2,'zh'=2,'y'=4] {'x'}, dimensions={0} | all-to-all | bytes 884736 | tf_op jit(solution)/shard_map/all_to_all | solution.py:415
  71.9 2.4 %all-gather.1 = s32[8,216,128]{2,1,0:T(8,128)S(1)} all-gather(s32[4,216,128]{2,1,0:T(8,128)S(1)} %all_to_all.16), channel_id=3, replica_groups=mesh['zl'=8,'x'=4,'c'=2,'zh'=2,'y'=4] {'c'}, dimensions={0}, use_global_device_ids=true | all-gather | bytes 1327104 | tf_op jit(solution)/shard_map/all_gather | solution.py:416
  74.3 1.8 %shard_map.44 = f32[3,3,48,1024]{3,2,1,0:T(8,128)} custom-call(s32[2,4,216,128]{3,2,1,0:T(8,128)S(1)} %bitcast.3), custom_call_target="tpu_custom_call" | custom-call | tf_op jit(solution)/shard_map/pallas_call | solution.py:418
  (1 shorter events, 0.0 us)
Async XLA Ops:
  1.9 30.9 %all-to-all-start = ((bf16[64,8,128]{2,1,0:T(8,128)(2,1)}), bf16[64,8,128]{2,1,0:T(8,128)(2,1)S(1)}, u32[]{:S(2)}, u32[]{:S(2)}) async-start(bf16[64,8,128]{2,1,0:T(8,128)(2,1)} %get-tuple-element.17), calls=%async_computation | async-start | bytes 262144 | tf_op jit(solution)/shard_map/all_to_all | solution.py:380
  18.1 10.7 %collective-permute-start = (f32[3,3,8,128]{3,2,1,0:T(8,128)}, f32[3,3,8,128]{3,2,1,0:T(8,128)S(1)}, u32[]{:S(2)}, u32[]{:S(2)}) collective-permute-start(f32[3,3,8,128]{3,2,1,0:T(8,128)} %get-tuple-element.19), channel_id=1, source_target_pairs={{136,129},{129,136},{9,2},{2,9},{138,131},{131,138},{11,388},{388,... | collective-permute-start | bytes 110600 | tf_op jit(solution)/shard_map/ppermute | solution.py:382
  26.4 1.2 %copy-start = (bf16[3,3,48,1024]{3,2,1,0:T(8,128)(2,1)S(1)}, bf16[3,3,48,1024]{3,2,1,0:T(8,128)(2,1)}, u32[]{:S(2)}) copy-start(bf16[3,3,48,1024]{3,2,1,0:T(8,128)(2,1)} %layers_ref.1) | copy-start | bytes 2654212
  36.2 9.5 %collective-permute-start.1 = (f32[3,3,8,128]{3,2,1,0:T(8,128)S(1)}, f32[3,3,8,128]{3,2,1,0:T(8,128)S(1)}, u32[]{:S(2)}, u32[]{:S(2)}) collective-permute-start(f32[3,3,8,128]{3,2,1,0:T(8,128)S(1)} %get-tuple-element.26), channel_id=1, source_target_pairs={{8,128},{128,8},{136,129},{129,136},{137,1},{1,137},{9,2},{2,9},{1... | collective-permute-start | bytes 110600 | tf_op jit(solution)/shard_map/ppermute | solution.py:398

commit v9 on v8

--- a/solution.py
+++ b/solution.py
@@ -159,11 +159,17 @@
 
 
 def view_kernel(
-    recv_ref, seen_ref, far_out, near_out, s0_ref, s1_ref, s2_ref, s3_ref, s4_ref, s5_ref,
+    recv_ref, seen_ref, far_out, s0_ref, s1_ref, s2_ref, s3_ref, s4_ref, s5_ref,
     image_ref, shift_ref, shift_smem, sem,
 ):
     sums = (s0_ref, s1_ref, s2_ref, s3_ref, s4_ref, s5_ref)
-    shift_ref[...] = recv_ref[:, 0, :].astype(F32).astype(I32)
+    row = lax.broadcasted_iota(I32, (16, 128), 0)
+    pick = jnp.where(lanes(16) == 120 + row, 1.0, 0.0).astype(BF16)
+    moved = lax.dot_general(
+        pick, recv_ref[:, 0, :], (((1,), (1,)), ((), ())), preferred_element_type=F32
+    )
+    shift_ref[...] = jnp.zeros((8, 128), I32)
+    shift_ref[:, :64] = moved[:8].astype(I32)
     copy = pltpu.make_async_copy(shift_ref, shift_smem, sem)
     copy.start()
 
@@ -188,8 +194,8 @@
     copy.wait()
 
     def one_view(view, carry):
-        rows = [shift_smem[view, 120 + 2 * layer] + HALO for layer in range(3)]
-        cols = [shift_smem[view, 121 + 2 * layer] + HALO for layer in range(3)]
+        rows = [shift_smem[2 * layer, view] + HALO for layer in range(3)]
+        cols = [shift_smem[2 * layer + 1, view] + HALO for layer in range(3)]
         s0, s1, s2 = (
             seen_ref[layer, cols[layer], :, pl.ds(rows[layer], 16), :] for layer in range(3)
         )
@@ -204,13 +210,10 @@
 
     lax.fori_loop(0, 64, one_view, 0, unroll=4)
 
-    even = lax.rem(q, 2) == 0
-    far_start = jnp.where(even, 0, HALO + TALL)
-    near_start = jnp.where(even, HALO + TALL, 0)
+    start = jnp.where(lax.rem(q, 2) == 0, 0, HALO + TALL)
     for layer in range(3):
         for frame in range(3):
-            far_out[layer, frame] = folded(sums, layer, frame, far_start, HALO)
-            near_out[layer, frame] = folded(sums, layer, frame, near_start, HALO)
+            far_out[layer, frame] = folded(sums, layer, frame, start, HALO)
 
 
 def folded(sums, layer, frame, start, rows):
@@ -226,10 +229,13 @@
     return jnp.where(lanes(rows) < WIDE, sides[0], sides[1])
 
 
-def own_kernel(s0_ref, s1_ref, s2_ref, s3_ref, s4_ref, s5_ref, own_out):
+def fold_kernel(s0_ref, s1_ref, s2_ref, s3_ref, s4_ref, s5_ref, near_out, own_out):
     sums = (s0_ref, s1_ref, s2_ref, s3_ref, s4_ref, s5_ref)
+    _, _, q = my_tile()
+    start = jnp.where(lax.rem(q, 2) == 0, HALO + TALL, 0)
     for layer in range(3):
         for frame in range(3):
+            near_out[layer, frame] = folded(sums, layer, frame, start, HALO)
             own_out[layer, frame] = folded(sums, layer, frame, HALO, 16)
 
 
@@ -342,8 +348,8 @@
 
 VIEW_SCRATCH = [
     pltpu.VMEM((64, 16, 128), F32),
-    pltpu.VMEM((64, 128), I32),
-    pltpu.SMEM((64, 128), I32),
+    pltpu.VMEM((8, 128), I32),
+    pltpu.SMEM((8, 128), I32),
     pltpu.SemaphoreType.DMA,
 ]
 
@@ -389,16 +395,16 @@
     )(layers)
     (seen,) = call(edge_kernel, [((3, SPAN, 3, 32, 128), F32)], [VMEM] * 2)(seen, edge)
 
-    far, near, *sums = call(
+    far, *sums = call(
         view_kernel,
-        [((3, 3, HALO, 128), F32)] * 2 + [((SPAN, 3, 32, 128), F32)] * 6,
+        [((3, 3, HALO, 128), F32)] + [((SPAN, 3, 32, 128), F32)] * 6,
         [VMEM] * 2,
         VIEW_SCRATCH,
     )(received, seen)
     far = lax.ppermute(far, across, strip_pairs(1, 2))
-    (own,) = call(
-        own_kernel,
-        [((3, 3, 16, 128), F32)],
+    near, own = call(
+        fold_kernel,
+        [((3, 3, HALO, 128), F32), ((3, 3, 16, 128), F32)],
         [VMEM] * 6,
         cost=pl.CostEstimate(flops=4_000_000, bytes_accessed=5_100_000, transcendentals=0),
     )(*sums)

time: 76.5 us -> 76.1 us (level)
  transfers between devices with their start and end apart: 3 -> 3, of which waited for: 2 -> 2; matrix products, arithmetic and copies ran while one was open for 0% -> 0% of each run, Pallas kernels for 3% -> 4%
where the time goes in v9:
time: 76.1 us; the launch traced here: 75.7 us
  blocking collectives  30.6 us (40%)
  starting transfers between devices  28.2 us (37%)
  Pallas kernels  9.31 us (12%)
  waiting for transfers between devices  6.38 us (8%)
  local copies, waits for them, and re-layouts  1.16 us (2%)
    all_to_all x1, starting transfers between devices, body(): received = lax.all_to_all(chunks, VIEW, 0, 0)  16.2 us
    all_to_all x1, blocking collectives, body(): words = lax.all_to_all(words, 'zl', 0, 0)  15.8 us
    all_to_all x1, blocking collectives, body(): words = lax.all_to_all(words, 'x', 0, 0)  10.5 us
    ppermute x1, starting transfers between devices, body(): edge = lax.ppermute(edge, across, strip_pairs(3, 4))  8.26 us
    ppermute x1, starting transfers between devices, body(): far = lax.ppermute(far, across, strip_pairs(1, 2))  3.72 us
    all_to_all x1, waiting for transfers between devices, body(): received = lax.all_to_all(chunks, VIEW, 0, 0)  3.5 us
    ppermute x1, waiting for transfers between devices, body(): far = lax.ppermute(far, across, strip_pairs(1, 2))  2.87 us
    pallas_call x1, Pallas kernels, body(): call(view_kernel, [((3, 3, HALO, 128), F32)] + [((SPAN, 3, 32, 128), F32)...  2.69 us
  transfers between devices with their start and end apart: 3, of which 2 were waited for; matrix products, arithmetic and copies ran while one was open for 0% of the time, Pallas kernels for 4%

profile of v9, /device:TPU:25, one launch (start us, length us, event | category | flops | bytes accessed | tf_op | source)
XLA Modules:
  0.0 75.7 jit_solution(6172063772082342072)
XLA Ops:
  0.0 1.9 %shard_map.37 = (bf16[64,8,128]{2,1,0:T(8,128)(2,1)}, f32[3,3,8,128]{3,2,1,0:T(8,128)}) custom-call(bf16[1,48,1024]{2,1,0:T(8,128)(2,1)} %target_hbm.1, s32[1,2,3]{2,1,0:T(2,128)} %bitcast.5, bf16[3,3,48,1024]{3,2,1,0:T(8,128)(2,1)} %layers_ref.1), custom_call_target="tpu_custom_call" | custom-call | tf_op jit(solution)/shard_map/pallas_call | solution.py:371
  1.9 16.2 %all-to-all-start = ((bf16[64,8,128]{2,1,0:T(8,128)(2,1)}), bf16[64,8,128]{2,1,0:T(8,128)(2,1)S(1)}, u32[]{:S(2)}, u32[]{:S(2)}) async-start(bf16[64,8,128]{2,1,0:T(8,128)(2,1)} %get-tuple-element.18), calls=%async_computation | async-start | bytes 262144 | tf_op jit(solution)/shard_map/all_to_all | solution.py:386
  18.1 8.3 %collective-permute-start = (f32[3,3,8,128]{3,2,1,0:T(8,128)}, f32[3,3,8,128]{3,2,1,0:T(8,128)S(1)}, u32[]{:S(2)}, u32[]{:S(2)}) collective-permute-start(f32[3,3,8,128]{3,2,1,0:T(8,128)} %get-tuple-element.20), channel_id=1, source_target_pairs={{136,129},{129,136},{9,2},{2,9},{138,131},{131,138},{11,388},{388,... | collective-permute-start | bytes 110600 | tf_op jit(solution)/shard_map/ppermute | solution.py:388
  26.4 0.0 copy-start
  26.4 1.2 %copy-done = bf16[3,3,48,1024]{3,2,1,0:T(8,128)(2,1)S(1)} copy-done((bf16[3,3,48,1024]{3,2,1,0:T(8,128)(2,1)S(1)}, bf16[3,3,48,1024]{3,2,1,0:T(8,128)(2,1)}, u32[]{:S(2)}) %copy-start) | copy-done | bytes 884760
  27.6 1.3 %shard_map.38 = (f32[3,17,3,32,128]{4,3,2,1,0:T(8,128)S(1)}, f32[3,3,16,128]{3,2,1,0:T(8,128)S(1)}) custom-call(bf16[3,3,48,1024]{3,2,1,0:T(8,128)(2,1)S(1)} %copy-done), custom_call_target="tpu_custom_call" | custom-call | flops 1000000 | bytes 3600000 | tf_op jit(solution)/shard_map/pallas_call | solution.py:389
  28.9 0.0 collective-permute-done.edge_ref
  28.9 0.4 shard_map.39.seen_ref
  29.3 3.5 %all-to-all-done.recv_ref = bf16[64,8,128]{2,1,0:T(8,128)(2,1)S(1)} async-done(((bf16[64,8,128]{2,1,0:T(8,128)(2,1)}), bf16[64,8,128]{2,1,0:T(8,128)(2,1)S(1)}, u32[]{:S(2)}, u32[]{:S(2)}) %all-to-all-start) | async-done | bytes 131104 | tf_op jit(solution)/shard_map/all_to_all | solution.py:386
  32.8 2.7 %shard_map.40 = (f32[3,3,8,128]{3,2,1,0:T(8,128)S(1)}, f32[17,3,32,128]{3,2,1,0:T(8,128)S(1)}, f32[17,3,32,128]{3,2,1,0:T(8,128)S(1)}, f32[17,3,32,128]{3,2,1,0:...) custom-call(bf16[64,8,128]{2,1,0:T(8,128)(2,1)S(1)} %all-to-all-done.re, ...), custom_call_target="tpu_custom_call" | custom-call | tf_op jit(solution)/shard_map/pallas_call | solution.py:398
  35.5 3.7 %collective-permute-start.1 = (f32[3,3,8,128]{3,2,1,0:T(8,128)S(1)}, f32[3,3,8,128]{3,2,1,0:T(8,128)S(1)}, u32[]{:S(2)}, u32[]{:S(2)}) collective-permute-start(f32[3,3,8,128]{3,2,1,0:T(8,128)S(1)} %get-tuple-element.28), channel_id=1, source_target_pairs={{8,128},{128,8},{136,129},{129,136},{137,1},{1,137},{9,2},{2,9},{1... | collective-permute-start | bytes 110600 | tf_op jit(solution)/shard_map/ppermute | solution.py:404
  39.2 1.0 %shard_map.41 = (f32[3,3,8,128]{3,2,1,0:T(8,128)S(1)}, f32[3,3,16,128]{3,2,1,0:T(8,128)S(1)}) custom-call(f32[17,3,32,128]{3,2,1,0:T(8,128)S(1)} %get-tuple-element.21.s0_ref, f32[17,3,32,128]{3,2,1,0:T(8,128)S(1)} %get-tuple-element.22.s1_ref, f32[17,3,32,128]{3,2,1,0:T(8,128)S(1)} %get-tuple-element.23.s2_ref, ...), custom_call_target="tpu_custom_call" | custom-call | flops 4000000 | bytes 5100000 | tf_op jit(solution)/shard_map/pallas_call | solution.py:405
  40.2 1.9 %all-gather = f32[6,3,8,128]{3,2,1,0:T(8,128)S(1)} all-gather(f32[3,3,8,128]{3,2,1,0:T(8,128)S(1)} %get-tuple-element.29), channel_id=2, replica_groups=mesh['zl'=8,'x'=4,'c'=2,'zh'=2,'y'=4] {'c'}, dimensions={0}, use_global_device_ids=true | all-gather | bytes 110592 | tf_op jit(solution)/shard_map/all_gather | solution.py:411
  42.1 2.9 %collective-permute-done.1.far_ref = f32[3,3,8,128]{3,2,1,0:T(8,128)S(1)} collective-permute-done((f32[3,3,8,128]{3,2,1,0:T(8,128)S(1)}, f32[3,3,8,128]{3,2,1,0:T(8,128)S(1)}, u32[]{:S(2)}, u32[]{:S(2)}) %collective-permute-start.1) | collective-permute-done | bytes 36896 | tf_op jit(solution)/shard_map/ppermute | solution.py:404
  45.0 0.2 shard_map.42
  45.2 15.8 %all_to_all.15.words_ref = s32[8,32,128]{2,1,0:T(8,128)S(1)} all-to-all(s32[8,32,128]{2,1,0:T(8,128)S(1)} %shard_map.42), channel_id=1, replica_groups=mesh['zl'=8,'x'=4,'c'=2,'zh'=2,'y'=4] {'zl'}, dimensions={0} | all-to-all | bytes 262144 | tf_op jit(solution)/shard_map/all_to_all | solution.py:419
  61.0 10.5 %all_to_all.16 = s32[4,216,128]{2,1,0:T(8,128)S(1)} all-to-all(s32[4,216,128]{2,1,0:T(8,128)S(1)} %shard_map.43), channel_id=1, replica_groups=mesh['zl'=8,'x'=4,'c'=2,'zh'=2,'y'=4] {'x'}, dimensions={0} | all-to-all | bytes 884736 | tf_op jit(solution)/shard_map/all_to_all | solution.py:421
  71.5 2.4 %all-gather.1 = s32[8,216,128]{2,1,0:T(8,128)S(1)} all-gather(s32[4,216,128]{2,1,0:T(8,128)S(1)} %all_to_all.16), channel_id=3, replica_groups=mesh['zl'=8,'x'=4,'c'=2,'zh'=2,'y'=4] {'c'}, dimensions={0}, use_global_device_ids=true | all-gather | bytes 1327104 | tf_op jit(solution)/shard_map/all_gather | solution.py:422
  73.9 1.8 %shard_map.44 = f32[3,3,48,1024]{3,2,1,0:T(8,128)} custom-call(s32[2,4,216,128]{3,2,1,0:T(8,128)S(1)} %bitcast.3), custom_call_target="tpu_custom_call" | custom-call | tf_op jit(solution)/shard_map/pallas_call | solution.py:424
  (1 shorter events, 0.0 us)
Async XLA Ops:
  1.9 30.9 %all-to-all-start = ((bf16[64,8,128]{2,1,0:T(8,128)(2,1)}), bf16[64,8,128]{2,1,0:T(8,128)(2,1)S(1)}, u32[]{:S(2)}, u32[]{:S(2)}) async-start(bf16[64,8,128]{2,1,0:T(8,128)(2,1)} %get-tuple-element.18), calls=%async_computation | async-start | bytes 262144 | tf_op jit(solution)/shard_map/all_to_all | solution.py:386
  18.1 10.7 %collective-permute-start = (f32[3,3,8,128]{3,2,1,0:T(8,128)}, f32[3,3,8,128]{3,2,1,0:T(8,128)S(1)}, u32[]{:S(2)}, u32[]{:S(2)}) collective-permute-start(f32[3,3,8,128]{3,2,1,0:T(8,128)} %get-tuple-element.20), channel_id=1, source_target_pairs={{136,129},{129,136},{9,2},{2,9},{138,131},{131,138},{11,388},{388,... | collective-permute-start | bytes 110600 | tf_op jit(solution)/shard_map/ppermute | solution.py:388
  26.4 1.2 %copy-start = (bf16[3,3,48,1024]{3,2,1,0:T(8,128)(2,1)S(1)}, bf16[3,3,48,1024]{3,2,1,0:T(8,128)(2,1)}, u32[]{:S(2)}) copy-start(bf16[3,3,48,1024]{3,2,1,0:T(8,128)(2,1)} %layers_ref.1) | copy-start | bytes 2654212
  35.5 9.5 %collective-permute-start.1 = (f32[3,3,8,128]{3,2,1,0:T(8,128)S(1)}, f32[3,3,8,128]{3,2,1,0:T(8,128)S(1)}, u32[]{:S(2)}, u32[]{:S(2)}) collective-permute-start(f32[3,3,8,128]{3,2,1,0:T(8,128)S(1)} %get-tuple-element.28), channel_id=1, source_target_pairs={{8,128},{128,8},{136,129},{129,136},{137,1},{1,137},{9,2},{2,9},{1... | collective-permute-start | bytes 110600 | tf_op jit(solution)/shard_map/ppermute | solution.py:404

commit v10 on v9

--- a/solution.py
+++ b/solution.py
@@ -270,20 +270,18 @@
     code_ref[8, :6] = jnp.where(
         lanes(6) < WIDE, code_ref[8, :6], pltpu.roll(code_ref[8, 6:TALL], WIDE, 1)
     )
-    word = code_ref[8, :REST] + (code_ref[8, REST : 2 * REST] - 32768) * 65536
+    word = code_ref[8, :8] + (code_ref[8, REST : REST + 8] - 32768) * 65536
     for copy in range(8):
-        out_ref[copy, MAIN : MAIN + REST] = word
-        out_ref[copy, MAIN + REST :] = jnp.zeros((5, 128), I32)
+        out_ref[copy, MAIN : MAIN + 8] = word
 
 
 def dense_kernel(words_ref, out_ref):
     for zl in range(8):
         main = words_ref[zl, :MAIN]
         rest = words_ref[zl, MAIN : MAIN + REST]
-        at = 8 * MAIN + REST * zl
         for copy in range(4):
-            out_ref[copy, MAIN * zl : MAIN * zl + MAIN] = main
-            out_ref[copy, at : at + REST] = rest
+            out_ref[copy, REST * zl : REST * zl + REST] = rest
+            out_ref[copy, 8 * REST + MAIN * zl : 8 * REST + MAIN * zl + MAIN] = main
 
 
 def decoded(code):
@@ -295,7 +293,7 @@
 
     def sent(d):
         columns = pl.ds(pl.multiple_of(d * 128, 128), 128)
-        return pltpu.make_async_copy(block_ref.at[d], out_ref.at[:, :, :, columns], sems.at[d])
+        return pltpu.make_async_copy(block_ref.at[d, :, :, :48], out_ref.at[:, :, :, columns], sems.at[d])
 
     def one(d, carry):
         for q in range(4):
@@ -311,13 +309,13 @@
                 even = jnp.where(lane < WIDE, a, pltpu.roll(b, WIDE, 1))
                 return even, jnp.where(lane < WIDE, pltpu.roll(a, WIDE, 1), b)
 
-            for side, word in enumerate(halves(0, MAIN, MAIN)):
+            for side, word in enumerate(halves(8 * REST, MAIN, MAIN)):
                 for p, code in ((0, word & 65535), (2, (word >> 16) + 32768)):
                     value = decoded(code)
                     for pair in range(2):
                         at = 2 * (p + pair) + side
                         block_ref[d, at // 3, at % 3, rows] = value[TALL * pair : TALL * pair + TALL]
-            for side, word in enumerate(halves(8 * MAIN, REST, REST)):
+            for side, word in enumerate(halves(0, REST, REST)):
                 for part, code in ((0, word & 65535), (1, (word >> 16) + 32768)):
                     at = TALL * q + 6 * side + REST * part
                     block_ref[d, 2, 2, at : at + REST] = decoded(code)
@@ -426,7 +424,7 @@
         out_shape=jax.ShapeDtypeStruct((3, 3, 48, 1024), F32),
         in_specs=[VMEM],
         out_specs=pl.BlockSpec(memory_space=pl.ANY),
-        scratch_shapes=[pltpu.VMEM((8, 3, 3, 48, 128), F32), pltpu.SemaphoreType.DMA((8,))],
+        scratch_shapes=[pltpu.VMEM((8, 3, 3, 56, 128), F32), pltpu.SemaphoreType.DMA((8,))],
         compiler_params=PARAMS,
     )(words)
 

time: 76.1 us -> 76.1 us (level)
  no operation moved by 1% of the time
where the time goes in v10:
time: 76.1 us; the launch traced here: 75.7 us
  blocking collectives  30.6 us (40%)
  starting transfers between devices  28.2 us (37%)
  Pallas kernels  9.31 us (12%)
  waiting for transfers between devices  6.38 us (8%)
  local copies, waits for them, and re-layouts  1.16 us (2%)
    all_to_all x1, starting transfers between devices, body(): received = lax.all_to_all(chunks, VIEW, 0, 0)  16.2 us
    all_to_all x1, blocking collectives, body(): words = lax.all_to_all(words, 'zl', 0, 0)  15.8 us
    all_to_all x1, blocking collectives, body(): words = lax.all_to_all(words, 'x', 0, 0)  10.5 us
    ppermute x1, starting transfers between devices, body(): edge = lax.ppermute(edge, across, strip_pairs(3, 4))  8.26 us
    ppermute x1, starting transfers between devices, body(): far = lax.ppermute(far, across, strip_pairs(1, 2))  3.72 us
    all_to_all x1, waiting for transfers between devices, body(): received = lax.all_to_all(chunks, VIEW, 0, 0)  3.5 us
    ppermute x1, waiting for transfers between devices, body(): far = lax.ppermute(far, across, strip_pairs(1, 2))  2.87 us
    pallas_call x1, Pallas kernels, body(): call(view_kernel, [((3, 3, HALO, 128), F32)] + [((SPAN, 3, 32, 128), F32)...  2.68 us
  transfers between devices with their start and end apart: 3, of which 2 were waited for; matrix products, arithmetic and copies ran while one was open for 0% of the time, Pallas kernels for 4%

profile of v10, /device:TPU:25, one launch (start us, length us, event | category | flops | bytes accessed | tf_op | source)
XLA Modules:
  0.0 75.7 jit_solution(10763820710626791079)
XLA Ops:
  0.0 1.9 %shard_map.37 = (bf16[64,8,128]{2,1,0:T(8,128)(2,1)}, f32[3,3,8,128]{3,2,1,0:T(8,128)}) custom-call(bf16[1,48,1024]{2,1,0:T(8,128)(2,1)} %target_hbm.1, s32[1,2,3]{2,1,0:T(2,128)} %bitcast.5, bf16[3,3,48,1024]{3,2,1,0:T(8,128)(2,1)} %layers_ref.1), custom_call_target="tpu_custom_call" | custom-call | tf_op jit(solution)/shard_map/pallas_call | solution.py:369
  1.9 16.2 %all-to-all-start = ((bf16[64,8,128]{2,1,0:T(8,128)(2,1)}), bf16[64,8,128]{2,1,0:T(8,128)(2,1)S(1)}, u32[]{:S(2)}, u32[]{:S(2)}) async-start(bf16[64,8,128]{2,1,0:T(8,128)(2,1)} %get-tuple-element.18), calls=%async_computation | async-start | bytes 262144 | tf_op jit(solution)/shard_map/all_to_all | solution.py:384
  18.1 8.3 %collective-permute-start = (f32[3,3,8,128]{3,2,1,0:T(8,128)}, f32[3,3,8,128]{3,2,1,0:T(8,128)S(1)}, u32[]{:S(2)}, u32[]{:S(2)}) collective-permute-start(f32[3,3,8,128]{3,2,1,0:T(8,128)} %get-tuple-element.20), channel_id=1, source_target_pairs={{136,129},{129,136},{9,2},{2,9},{138,131},{131,138},{11,388},{388,... | collective-permute-start | bytes 110600 | tf_op jit(solution)/shard_map/ppermute | solution.py:386
  26.4 0.0 copy-start
  26.4 1.2 %copy-done = bf16[3,3,48,1024]{3,2,1,0:T(8,128)(2,1)S(1)} copy-done((bf16[3,3,48,1024]{3,2,1,0:T(8,128)(2,1)S(1)}, bf16[3,3,48,1024]{3,2,1,0:T(8,128)(2,1)}, u32[]{:S(2)}) %copy-start) | copy-done | bytes 884760
  27.6 1.3 %shard_map.38 = (f32[3,17,3,32,128]{4,3,2,1,0:T(8,128)S(1)}, f32[3,3,16,128]{3,2,1,0:T(8,128)S(1)}) custom-call(bf16[3,3,48,1024]{3,2,1,0:T(8,128)(2,1)S(1)} %copy-done), custom_call_target="tpu_custom_call" | custom-call | flops 1000000 | bytes 3600000 | tf_op jit(solution)/shard_map/pallas_call | solution.py:387
  28.9 0.0 collective-permute-done.edge_ref
  28.9 0.4 shard_map.39.seen_ref
  29.3 3.5 %all-to-all-done.recv_ref = bf16[64,8,128]{2,1,0:T(8,128)(2,1)S(1)} async-done(((bf16[64,8,128]{2,1,0:T(8,128)(2,1)}), bf16[64,8,128]{2,1,0:T(8,128)(2,1)S(1)}, u32[]{:S(2)}, u32[]{:S(2)}) %all-to-all-start) | async-done | bytes 131104 | tf_op jit(solution)/shard_map/all_to_all | solution.py:384
  32.8 2.7 %shard_map.40 = (f32[3,3,8,128]{3,2,1,0:T(8,128)S(1)}, f32[17,3,32,128]{3,2,1,0:T(8,128)S(1)}, f32[17,3,32,128]{3,2,1,0:T(8,128)S(1)}, f32[17,3,32,128]{3,2,1,0:...) custom-call(bf16[64,8,128]{2,1,0:T(8,128)(2,1)S(1)} %all-to-all-done.re, ...), custom_call_target="tpu_custom_call" | custom-call | tf_op jit(solution)/shard_map/pallas_call | solution.py:396
  35.5 3.7 %collective-permute-start.1 = (f32[3,3,8,128]{3,2,1,0:T(8,128)S(1)}, f32[3,3,8,128]{3,2,1,0:T(8,128)S(1)}, u32[]{:S(2)}, u32[]{:S(2)}) collective-permute-start(f32[3,3,8,128]{3,2,1,0:T(8,128)S(1)} %get-tuple-element.28), channel_id=1, source_target_pairs={{8,128},{128,8},{136,129},{129,136},{137,1},{1,137},{9,2},{2,9},{1... | collective-permute-start | bytes 110600 | tf_op jit(solution)/shard_map/ppermute | solution.py:402
  39.2 1.0 %shard_map.41 = (f32[3,3,8,128]{3,2,1,0:T(8,128)S(1)}, f32[3,3,16,128]{3,2,1,0:T(8,128)S(1)}) custom-call(f32[17,3,32,128]{3,2,1,0:T(8,128)S(1)} %get-tuple-element.21.s0_ref, f32[17,3,32,128]{3,2,1,0:T(8,128)S(1)} %get-tuple-element.22.s1_ref, f32[17,3,32,128]{3,2,1,0:T(8,128)S(1)} %get-tuple-element.23.s2_ref, ...), custom_call_target="tpu_custom_call" | custom-call | flops 4000000 | bytes 5100000 | tf_op jit(solution)/shard_map/pallas_call | solution.py:403
  40.2 1.9 %all-gather = f32[6,3,8,128]{3,2,1,0:T(8,128)S(1)} all-gather(f32[3,3,8,128]{3,2,1,0:T(8,128)S(1)} %get-tuple-element.29), channel_id=2, replica_groups=mesh['zl'=8,'x'=4,'c'=2,'zh'=2,'y'=4] {'c'}, dimensions={0}, use_global_device_ids=true | all-gather | bytes 110592 | tf_op jit(solution)/shard_map/all_gather | solution.py:409
  42.1 2.9 %collective-permute-done.1.far_ref = f32[3,3,8,128]{3,2,1,0:T(8,128)S(1)} collective-permute-done((f32[3,3,8,128]{3,2,1,0:T(8,128)S(1)}, f32[3,3,8,128]{3,2,1,0:T(8,128)S(1)}, u32[]{:S(2)}, u32[]{:S(2)}) %collective-permute-start.1) | collective-permute-done | bytes 36896 | tf_op jit(solution)/shard_map/ppermute | solution.py:402
  45.0 0.2 shard_map.42
  45.2 15.8 %all_to_all.15.words_ref = s32[8,32,128]{2,1,0:T(8,128)S(1)} all-to-all(s32[8,32,128]{2,1,0:T(8,128)S(1)} %shard_map.42), channel_id=1, replica_groups=mesh['zl'=8,'x'=4,'c'=2,'zh'=2,'y'=4] {'zl'}, dimensions={0} | all-to-all | bytes 262144 | tf_op jit(solution)/shard_map/all_to_all | solution.py:417
  61.0 10.5 %all_to_all.16 = s32[4,216,128]{2,1,0:T(8,128)S(1)} all-to-all(s32[4,216,128]{2,1,0:T(8,128)S(1)} %shard_map.43), channel_id=1, replica_groups=mesh['zl'=8,'x'=4,'c'=2,'zh'=2,'y'=4] {'x'}, dimensions={0} | all-to-all | bytes 884736 | tf_op jit(solution)/shard_map/all_to_all | solution.py:419
  71.5 2.4 %all-gather.1 = s32[8,216,128]{2,1,0:T(8,128)S(1)} all-gather(s32[4,216,128]{2,1,0:T(8,128)S(1)} %all_to_all.16), channel_id=3, replica_groups=mesh['zl'=8,'x'=4,'c'=2,'zh'=2,'y'=4] {'c'}, dimensions={0}, use_global_device_ids=true | all-gather | bytes 1327104 | tf_op jit(solution)/shard_map/all_gather | solution.py:420
  73.9 1.8 %shard_map.44 = f32[3,3,48,1024]{3,2,1,0:T(8,128)} custom-call(s32[2,4,216,128]{3,2,1,0:T(8,128)S(1)} %bitcast.3), custom_call_target="tpu_custom_call" | custom-call | tf_op jit(solution)/shard_map/pallas_call | solution.py:422
  (1 shorter events, 0.0 us)
Async XLA Ops:
  1.9 30.9 %all-to-all-start = ((bf16[64,8,128]{2,1,0:T(8,128)(2,1)}), bf16[64,8,128]{2,1,0:T(8,128)(2,1)S(1)}, u32[]{:S(2)}, u32[]{:S(2)}) async-start(bf16[64,8,128]{2,1,0:T(8,128)(2,1)} %get-tuple-element.18), calls=%async_computation | async-start | bytes 262144 | tf_op jit(solution)/shard_map/all_to_all | solution.py:384
  18.1 10.7 %collective-permute-start = (f32[3,3,8,128]{3,2,1,0:T(8,128)}, f32[3,3,8,128]{3,2,1,0:T(8,128)S(1)}, u32[]{:S(2)}, u32[]{:S(2)}) collective-permute-start(f32[3,3,8,128]{3,2,1,0:T(8,128)} %get-tuple-element.20), channel_id=1, source_target_pairs={{136,129},{129,136},{9,2},{2,9},{138,131},{131,138},{11,388},{388,... | collective-permute-start | bytes 110600 | tf_op jit(solution)/shard_map/ppermute | solution.py:386
  26.4 1.2 %copy-start = (bf16[3,3,48,1024]{3,2,1,0:T(8,128)(2,1)S(1)}, bf16[3,3,48,1024]{3,2,1,0:T(8,128)(2,1)}, u32[]{:S(2)}) copy-start(bf16[3,3,48,1024]{3,2,1,0:T(8,128)(2,1)} %layers_ref.1) | copy-start | bytes 2654212
  35.5 9.5 %collective-permute-start.1 = (f32[3,3,8,128]{3,2,1,0:T(8,128)S(1)}, f32[3,3,8,128]{3,2,1,0:T(8,128)S(1)}, u32[]{:S(2)}, u32[]{:S(2)}) collective-permute-start(f32[3,3,8,128]{3,2,1,0:T(8,128)S(1)} %get-tuple-element.28), channel_id=1, source_target_pairs={{8,128},{128,8},{136,129},{129,136},{137,1},{1,137},{9,2},{2,9},{1... | collective-permute-start | bytes 110600 | tf_op jit(solution)/shard_map/ppermute | solution.py:402

commit v11 on v10

--- a/solution.py
+++ b/solution.py
@@ -104,17 +104,20 @@
             extra = jnp.where(
                 lane == 120 + 2 * layer + part, shifts_ref[0, part, layer].astype(F32), extra
             )
-    for q in range(4):
+    def strip(at_q, carry):
         for d in range(8):
             for h in range(2):
-                zl, x, c = home(d, h, q, high, odd)
+                zl, x, c = home(d, h, at_q, high, odd)
                 at = 2 * d + h
-                main = wide_ref[at, TALL * q : TALL * q + 8]
-                first = wide_ref[at, TALL * q + 8 : TALL * q + 16]
-                second = wide_ref[at, TALL * q + 4 : TALL * q + 12]
+                main = wide_ref[at, pl.ds(TALL * at_q, 8), :]
+                first = wide_ref[at, pl.ds(TALL * at_q + 8, 8), :]
+                second = wide_ref[at, pl.ds(TALL * at_q + 4, 8), :]
                 pieces = jnp.where(upper_half, pltpu.roll(first, 80, 1), pltpu.roll(second, 40, 1))
                 chunk = jnp.where(lane < 80, main, jnp.where(lane < 120, pieces, extra))
                 chunks_ref[(zl * 4 + x) * 2 + c] = chunk.astype(BF16)
+        return carry
+
+    lax.fori_loop(0, 4, strip, 0)
     for one in fetch_edges:
         one.wait()
     for layer in range(3):

time: 76.1 us -> 76.3 us (level)
  no operation moved by 1% of the time
where the time goes in v11:
time: 76.3 us; the launch traced here: 75.9 us
  blocking collectives  30.6 us (40%)
  starting transfers between devices  28.2 us (37%)
  Pallas kernels  9.54 us (13%)
  waiting for transfers between devices  6.38 us (8%)
  local copies, waits for them, and re-layouts  1.16 us (2%)
    all_to_all x1, starting transfers between devices, body(): received = lax.all_to_all(chunks, VIEW, 0, 0)  16.2 us
    all_to_all x1, blocking collectives, body(): words = lax.all_to_all(words, 'zl', 0, 0)  15.8 us
    all_to_all x1, blocking collectives, body(): words = lax.all_to_all(words, 'x', 0, 0)  10.5 us
    ppermute x1, starting transfers between devices, body(): edge = lax.ppermute(edge, across, strip_pairs(3, 4))  8.26 us
    ppermute x1, starting transfers between devices, body(): far = lax.ppermute(far, across, strip_pairs(1, 2))  3.72 us
    all_to_all x1, waiting for transfers between devices, body(): received = lax.all_to_all(chunks, VIEW, 0, 0)  3.5 us
    ppermute x1, waiting for transfers between devices, body(): far = lax.ppermute(far, across, strip_pairs(1, 2))  2.87 us
    pallas_call x1, Pallas kernels, body(): call(view_kernel, [((3, 3, HALO, 128), F32)] + [((SPAN, 3, 32, 128), F32)...  2.69 us
  transfers between devices with their start and end apart: 3, of which 2 were waited for; matrix products, arithmetic and copies ran while one was open for 0% of the time, Pallas kernels for 4%

profile of v11, /device:TPU:25, one launch (start us, length us, event | category | flops | bytes accessed | tf_op | source)
XLA Modules:
  0.0 75.9 jit_solution(13870688718444224250)
XLA Ops:
  0.0 2.1 %shard_map.37 = (bf16[64,8,128]{2,1,0:T(8,128)(2,1)}, f32[3,3,8,128]{3,2,1,0:T(8,128)}) custom-call(bf16[1,48,1024]{2,1,0:T(8,128)(2,1)} %target_hbm.1, s32[1,2,3]{2,1,0:T(2,128)} %bitcast.5, bf16[3,3,48,1024]{3,2,1,0:T(8,128)(2,1)} %layers_ref.1), custom_call_target="tpu_custom_call" | custom-call | tf_op jit(solution)/shard_map/pallas_call | solution.py:372
  2.1 16.2 %all-to-all-start = ((bf16[64,8,128]{2,1,0:T(8,128)(2,1)}), bf16[64,8,128]{2,1,0:T(8,128)(2,1)S(1)}, u32[]{:S(2)}, u32[]{:S(2)}) async-start(bf16[64,8,128]{2,1,0:T(8,128)(2,1)} %get-tuple-element.18), calls=%async_computation | async-start | bytes 262144 | tf_op jit(solution)/shard_map/all_to_all | solution.py:387
  18.4 8.3 %collective-permute-start = (f32[3,3,8,128]{3,2,1,0:T(8,128)}, f32[3,3,8,128]{3,2,1,0:T(8,128)S(1)}, u32[]{:S(2)}, u32[]{:S(2)}) collective-permute-start(f32[3,3,8,128]{3,2,1,0:T(8,128)} %get-tuple-element.20), channel_id=1, source_target_pairs={{136,129},{129,136},{9,2},{2,9},{138,131},{131,138},{11,388},{388,... | collective-permute-start | bytes 110600 | tf_op jit(solution)/shard_map/ppermute | solution.py:389
  26.6 0.0 copy-start
  26.6 1.2 %copy-done = bf16[3,3,48,1024]{3,2,1,0:T(8,128)(2,1)S(1)} copy-done((bf16[3,3,48,1024]{3,2,1,0:T(8,128)(2,1)S(1)}, bf16[3,3,48,1024]{3,2,1,0:T(8,128)(2,1)}, u32[]{:S(2)}) %copy-start) | copy-done | bytes 884760
  27.8 1.3 %shard_map.38 = (f32[3,17,3,32,128]{4,3,2,1,0:T(8,128)S(1)}, f32[3,3,16,128]{3,2,1,0:T(8,128)S(1)}) custom-call(bf16[3,3,48,1024]{3,2,1,0:T(8,128)(2,1)S(1)} %copy-done), custom_call_target="tpu_custom_call" | custom-call | flops 1000000 | bytes 3600000 | tf_op jit(solution)/shard_map/pallas_call | solution.py:390
  29.1 0.0 collective-permute-done.edge_ref
  29.1 0.4 shard_map.39.seen_ref
  29.5 3.5 %all-to-all-done.recv_ref = bf16[64,8,128]{2,1,0:T(8,128)(2,1)S(1)} async-done(((bf16[64,8,128]{2,1,0:T(8,128)(2,1)}), bf16[64,8,128]{2,1,0:T(8,128)(2,1)S(1)}, u32[]{:S(2)}, u32[]{:S(2)}) %all-to-all-start) | async-done | bytes 131104 | tf_op jit(solution)/shard_map/all_to_all | solution.py:387
  33.0 2.7 %shard_map.40 = (f32[3,3,8,128]{3,2,1,0:T(8,128)S(1)}, f32[17,3,32,128]{3,2,1,0:T(8,128)S(1)}, f32[17,3,32,128]{3,2,1,0:T(8,128)S(1)}, f32[17,3,32,128]{3,2,1,0:...) custom-call(bf16[64,8,128]{2,1,0:T(8,128)(2,1)S(1)} %all-to-all-done.re, ...), custom_call_target="tpu_custom_call" | custom-call | tf_op jit(solution)/shard_map/pallas_call | solution.py:399
  35.7 3.7 %collective-permute-start.1 = (f32[3,3,8,128]{3,2,1,0:T(8,128)S(1)}, f32[3,3,8,128]{3,2,1,0:T(8,128)S(1)}, u32[]{:S(2)}, u32[]{:S(2)}) collective-permute-start(f32[3,3,8,128]{3,2,1,0:T(8,128)S(1)} %get-tuple-element.28), channel_id=1, source_target_pairs={{8,128},{128,8},{136,129},{129,136},{137,1},{1,137},{9,2},{2,9},{1... | collective-permute-start | bytes 110600 | tf_op jit(solution)/shard_map/ppermute | solution.py:405
  39.4 1.0 %shard_map.41 = (f32[3,3,8,128]{3,2,1,0:T(8,128)S(1)}, f32[3,3,16,128]{3,2,1,0:T(8,128)S(1)}) custom-call(f32[17,3,32,128]{3,2,1,0:T(8,128)S(1)} %get-tuple-element.21.s0_ref, f32[17,3,32,128]{3,2,1,0:T(8,128)S(1)} %get-tuple-element.22.s1_ref, f32[17,3,32,128]{3,2,1,0:T(8,128)S(1)} %get-tuple-element.23.s2_ref, ...), custom_call_target="tpu_custom_call" | custom-call | flops 4000000 | bytes 5100000 | tf_op jit(solution)/shard_map/pallas_call | solution.py:406
  40.5 1.9 %all-gather = f32[6,3,8,128]{3,2,1,0:T(8,128)S(1)} all-gather(f32[3,3,8,128]{3,2,1,0:T(8,128)S(1)} %get-tuple-element.29), channel_id=2, replica_groups=mesh['zl'=8,'x'=4,'c'=2,'zh'=2,'y'=4] {'c'}, dimensions={0}, use_global_device_ids=true | all-gather | bytes 110592 | tf_op jit(solution)/shard_map/all_gather | solution.py:412
  42.3 2.9 %collective-permute-done.1.far_ref = f32[3,3,8,128]{3,2,1,0:T(8,128)S(1)} collective-permute-done((f32[3,3,8,128]{3,2,1,0:T(8,128)S(1)}, f32[3,3,8,128]{3,2,1,0:T(8,128)S(1)}, u32[]{:S(2)}, u32[]{:S(2)}) %collective-permute-start.1) | collective-permute-done | bytes 36896 | tf_op jit(solution)/shard_map/ppermute | solution.py:405
  45.2 0.2 shard_map.42
  45.4 15.8 %all_to_all.15.words_ref = s32[8,32,128]{2,1,0:T(8,128)S(1)} all-to-all(s32[8,32,128]{2,1,0:T(8,128)S(1)} %shard_map.42), channel_id=1, replica_groups=mesh['zl'=8,'x'=4,'c'=2,'zh'=2,'y'=4] {'zl'}, dimensions={0} | all-to-all | bytes 262144 | tf_op jit(solution)/shard_map/all_to_all | solution.py:420
  61.2 10.5 %all_to_all.16 = s32[4,216,128]{2,1,0:T(8,128)S(1)} all-to-all(s32[4,216,128]{2,1,0:T(8,128)S(1)} %shard_map.43), channel_id=1, replica_groups=mesh['zl'=8,'x'=4,'c'=2,'zh'=2,'y'=4] {'x'}, dimensions={0} | all-to-all | bytes 884736 | tf_op jit(solution)/shard_map/all_to_all | solution.py:422
  71.7 2.4 %all-gather.1 = s32[8,216,128]{2,1,0:T(8,128)S(1)} all-gather(s32[4,216,128]{2,1,0:T(8,128)S(1)} %all_to_all.16), channel_id=3, replica_groups=mesh['zl'=8,'x'=4,'c'=2,'zh'=2,'y'=4] {'c'}, dimensions={0}, use_global_device_ids=true | all-gather | bytes 1327104 | tf_op jit(solution)/shard_map/all_gather | solution.py:423
  74.1 1.8 %shard_map.44 = f32[3,3,48,1024]{3,2,1,0:T(8,128)} custom-call(s32[2,4,216,128]{3,2,1,0:T(8,128)S(1)} %bitcast.3), custom_call_target="tpu_custom_call" | custom-call | tf_op jit(solution)/shard_map/pallas_call | solution.py:425
  (1 shorter events, 0.0 us)
Async XLA Ops:
  2.1 30.9 %all-to-all-start = ((bf16[64,8,128]{2,1,0:T(8,128)(2,1)}), bf16[64,8,128]{2,1,0:T(8,128)(2,1)S(1)}, u32[]{:S(2)}, u32[]{:S(2)}) async-start(bf16[64,8,128]{2,1,0:T(8,128)(2,1)} %get-tuple-element.18), calls=%async_computation | async-start | bytes 262144 | tf_op jit(solution)/shard_map/all_to_all | solution.py:387
  18.4 10.7 %collective-permute-start = (f32[3,3,8,128]{3,2,1,0:T(8,128)}, f32[3,3,8,128]{3,2,1,0:T(8,128)S(1)}, u32[]{:S(2)}, u32[]{:S(2)}) collective-permute-start(f32[3,3,8,128]{3,2,1,0:T(8,128)} %get-tuple-element.20), channel_id=1, source_target_pairs={{136,129},{129,136},{9,2},{2,9},{138,131},{131,138},{11,388},{388,... | collective-permute-start | bytes 110600 | tf_op jit(solution)/shard_map/ppermute | solution.py:389
  26.6 1.2 %copy-start = (bf16[3,3,48,1024]{3,2,1,0:T(8,128)(2,1)S(1)}, bf16[3,3,48,1024]{3,2,1,0:T(8,128)(2,1)}, u32[]{:S(2)}) copy-start(bf16[3,3,48,1024]{3,2,1,0:T(8,128)(2,1)} %layers_ref.1) | copy-start | bytes 2654212
  35.7 9.5 %collective-permute-start.1 = (f32[3,3,8,128]{3,2,1,0:T(8,128)S(1)}, f32[3,3,8,128]{3,2,1,0:T(8,128)S(1)}, u32[]{:S(2)}, u32[]{:S(2)}) collective-permute-start(f32[3,3,8,128]{3,2,1,0:T(8,128)S(1)} %get-tuple-element.28), channel_id=1, source_target_pairs={{8,128},{128,8},{136,129},{129,136},{137,1},{1,137},{9,2},{2,9},{1... | collective-permute-start | bytes 110600 | tf_op jit(solution)/shard_map/ppermute | solution.py:405

commit v12 on v10

--- a/solution.py
+++ b/solution.py
@@ -322,7 +322,7 @@
         sent(d).start()
         return carry
 
-    lax.fori_loop(0, 8, one, 0)
+    lax.fori_loop(0, 8, one, 0, unroll=8)
     for d in range(8):
         sent(d).wait()
 

time: 76.1 us -> 76 us (level)
  no operation moved by 1% of the time
where the time goes in v12:
time: 76 us; the launch traced here: 75.7 us
  blocking collectives  30.6 us (40%)
  starting transfers between devices  28.2 us (37%)
  Pallas kernels  9.29 us (12%)
  waiting for transfers between devices  6.38 us (8%)
  local copies, waits for them, and re-layouts  1.16 us (2%)
    all_to_all x1, starting transfers between devices, body(): received = lax.all_to_all(chunks, VIEW, 0, 0)  16.2 us
    all_to_all x1, blocking collectives, body(): words = lax.all_to_all(words, 'zl', 0, 0)  15.8 us
    all_to_all x1, blocking collectives, body(): words = lax.all_to_all(words, 'x', 0, 0)  10.5 us
    ppermute x1, starting transfers between devices, body(): edge = lax.ppermute(edge, across, strip_pairs(3, 4))  8.26 us
    ppermute x1, starting transfers between devices, body(): far = lax.ppermute(far, across, strip_pairs(1, 2))  3.72 us
    all_to_all x1, waiting for transfers between devices, body(): received = lax.all_to_all(chunks, VIEW, 0, 0)  3.5 us
    ppermute x1, waiting for transfers between devices, body(): far = lax.ppermute(far, across, strip_pairs(1, 2))  2.87 us
    pallas_call x1, Pallas kernels, body(): call(view_kernel, [((3, 3, HALO, 128), F32)] + [((SPAN, 3, 32, 128), F32)...  2.69 us
  transfers between devices with their start and end apart: 3, of which 2 were waited for; matrix products, arithmetic and copies ran while one was open for 0% of the time, Pallas kernels for 4%

profile of v12, /device:TPU:25, one launch (start us, length us, event | category | flops | bytes accessed | tf_op | source)
XLA Modules:
  0.0 75.7 jit_solution(9021417279845306624)
XLA Ops:
  0.0 1.9 %shard_map.37 = (bf16[64,8,128]{2,1,0:T(8,128)(2,1)}, f32[3,3,8,128]{3,2,1,0:T(8,128)}) custom-call(bf16[1,48,1024]{2,1,0:T(8,128)(2,1)} %target_hbm.1, s32[1,2,3]{2,1,0:T(2,128)} %bitcast.5, bf16[3,3,48,1024]{3,2,1,0:T(8,128)(2,1)} %layers_ref.1), custom_call_target="tpu_custom_call" | custom-call | tf_op jit(solution)/shard_map/pallas_call | solution.py:369
  1.9 16.2 %all-to-all-start = ((bf16[64,8,128]{2,1,0:T(8,128)(2,1)}), bf16[64,8,128]{2,1,0:T(8,128)(2,1)S(1)}, u32[]{:S(2)}, u32[]{:S(2)}) async-start(bf16[64,8,128]{2,1,0:T(8,128)(2,1)} %get-tuple-element.18), calls=%async_computation | async-start | bytes 262144 | tf_op jit(solution)/shard_map/all_to_all | solution.py:384
  18.1 8.3 %collective-permute-start = (f32[3,3,8,128]{3,2,1,0:T(8,128)}, f32[3,3,8,128]{3,2,1,0:T(8,128)S(1)}, u32[]{:S(2)}, u32[]{:S(2)}) collective-permute-start(f32[3,3,8,128]{3,2,1,0:T(8,128)} %get-tuple-element.20), channel_id=1, source_target_pairs={{136,129},{129,136},{9,2},{2,9},{138,131},{131,138},{11,388},{388,... | collective-permute-start | bytes 110600 | tf_op jit(solution)/shard_map/ppermute | solution.py:386
  26.4 0.0 copy-start
  26.4 1.2 %copy-done = bf16[3,3,48,1024]{3,2,1,0:T(8,128)(2,1)S(1)} copy-done((bf16[3,3,48,1024]{3,2,1,0:T(8,128)(2,1)S(1)}, bf16[3,3,48,1024]{3,2,1,0:T(8,128)(2,1)}, u32[]{:S(2)}) %copy-start) | copy-done | bytes 884760
  27.6 1.3 %shard_map.38 = (f32[3,17,3,32,128]{4,3,2,1,0:T(8,128)S(1)}, f32[3,3,16,128]{3,2,1,0:T(8,128)S(1)}) custom-call(bf16[3,3,48,1024]{3,2,1,0:T(8,128)(2,1)S(1)} %copy-done), custom_call_target="tpu_custom_call" | custom-call | flops 1000000 | bytes 3600000 | tf_op jit(solution)/shard_map/pallas_call | solution.py:387
  28.9 0.0 collective-permute-done.edge_ref
  28.9 0.4 shard_map.39.seen_ref
  29.3 3.5 %all-to-all-done.recv_ref = bf16[64,8,128]{2,1,0:T(8,128)(2,1)S(1)} async-done(((bf16[64,8,128]{2,1,0:T(8,128)(2,1)}), bf16[64,8,128]{2,1,0:T(8,128)(2,1)S(1)}, u32[]{:S(2)}, u32[]{:S(2)}) %all-to-all-start) | async-done | bytes 131104 | tf_op jit(solution)/shard_map/all_to_all | solution.py:384
  32.8 2.7 %shard_map.40 = (f32[3,3,8,128]{3,2,1,0:T(8,128)S(1)}, f32[17,3,32,128]{3,2,1,0:T(8,128)S(1)}, f32[17,3,32,128]{3,2,1,0:T(8,128)S(1)}, f32[17,3,32,128]{3,2,1,0:...) custom-call(bf16[64,8,128]{2,1,0:T(8,128)(2,1)S(1)} %all-to-all-done.re, ...), custom_call_target="tpu_custom_call" | custom-call | tf_op jit(solution)/shard_map/pallas_call | solution.py:396
  35.5 3.7 %collective-permute-start.1 = (f32[3,3,8,128]{3,2,1,0:T(8,128)S(1)}, f32[3,3,8,128]{3,2,1,0:T(8,128)S(1)}, u32[]{:S(2)}, u32[]{:S(2)}) collective-permute-start(f32[3,3,8,128]{3,2,1,0:T(8,128)S(1)} %get-tuple-element.28), channel_id=1, source_target_pairs={{8,128},{128,8},{136,129},{129,136},{137,1},{1,137},{9,2},{2,9},{1... | collective-permute-start | bytes 110600 | tf_op jit(solution)/shard_map/ppermute | solution.py:402
  39.2 1.0 %shard_map.41 = (f32[3,3,8,128]{3,2,1,0:T(8,128)S(1)}, f32[3,3,16,128]{3,2,1,0:T(8,128)S(1)}) custom-call(f32[17,3,32,128]{3,2,1,0:T(8,128)S(1)} %get-tuple-element.21.s0_ref, f32[17,3,32,128]{3,2,1,0:T(8,128)S(1)} %get-tuple-element.22.s1_ref, f32[17,3,32,128]{3,2,1,0:T(8,128)S(1)} %get-tuple-element.23.s2_ref, ...), custom_call_target="tpu_custom_call" | custom-call | flops 4000000 | bytes 5100000 | tf_op jit(solution)/shard_map/pallas_call | solution.py:403
  40.2 1.9 %all-gather = f32[6,3,8,128]{3,2,1,0:T(8,128)S(1)} all-gather(f32[3,3,8,128]{3,2,1,0:T(8,128)S(1)} %get-tuple-element.29), channel_id=2, replica_groups=mesh['zl'=8,'x'=4,'c'=2,'zh'=2,'y'=4] {'c'}, dimensions={0}, use_global_device_ids=true | all-gather | bytes 110592 | tf_op jit(solution)/shard_map/all_gather | solution.py:409
  42.1 2.9 %collective-permute-done.1.far_ref = f32[3,3,8,128]{3,2,1,0:T(8,128)S(1)} collective-permute-done((f32[3,3,8,128]{3,2,1,0:T(8,128)S(1)}, f32[3,3,8,128]{3,2,1,0:T(8,128)S(1)}, u32[]{:S(2)}, u32[]{:S(2)}) %collective-permute-start.1) | collective-permute-done | bytes 36896 | tf_op jit(solution)/shard_map/ppermute | solution.py:402
  45.0 0.2 shard_map.42
  45.2 15.8 %all_to_all.15.words_ref = s32[8,32,128]{2,1,0:T(8,128)S(1)} all-to-all(s32[8,32,128]{2,1,0:T(8,128)S(1)} %shard_map.42), channel_id=1, replica_groups=mesh['zl'=8,'x'=4,'c'=2,'zh'=2,'y'=4] {'zl'}, dimensions={0} | all-to-all | bytes 262144 | tf_op jit(solution)/shard_map/all_to_all | solution.py:417
  61.0 10.5 %all_to_all.16 = s32[4,216,128]{2,1,0:T(8,128)S(1)} all-to-all(s32[4,216,128]{2,1,0:T(8,128)S(1)} %shard_map.43), channel_id=1, replica_groups=mesh['zl'=8,'x'=4,'c'=2,'zh'=2,'y'=4] {'x'}, dimensions={0} | all-to-all | bytes 884736 | tf_op jit(solution)/shard_map/all_to_all | solution.py:419
  71.5 2.4 %all-gather.1 = s32[8,216,128]{2,1,0:T(8,128)S(1)} all-gather(s32[4,216,128]{2,1,0:T(8,128)S(1)} %all_to_all.16), channel_id=3, replica_groups=mesh['zl'=8,'x'=4,'c'=2,'zh'=2,'y'=4] {'c'}, dimensions={0}, use_global_device_ids=true | all-gather | bytes 1327104 | tf_op jit(solution)/shard_map/all_gather | solution.py:420
  73.9 1.8 %shard_map.44 = f32[3,3,48,1024]{3,2,1,0:T(8,128)} custom-call(s32[2,4,216,128]{3,2,1,0:T(8,128)S(1)} %bitcast.3), custom_call_target="tpu_custom_call" | custom-call | tf_op jit(solution)/shard_map/pallas_call | solution.py:422
  (1 shorter events, 0.0 us)
Async XLA Ops:
  1.9 30.9 %all-to-all-start = ((bf16[64,8,128]{2,1,0:T(8,128)(2,1)}), bf16[64,8,128]{2,1,0:T(8,128)(2,1)S(1)}, u32[]{:S(2)}, u32[]{:S(2)}) async-start(bf16[64,8,128]{2,1,0:T(8,128)(2,1)} %get-tuple-element.18), calls=%async_computation | async-start | bytes 262144 | tf_op jit(solution)/shard_map/all_to_all | solution.py:384
  18.1 10.7 %collective-permute-start = (f32[3,3,8,128]{3,2,1,0:T(8,128)}, f32[3,3,8,128]{3,2,1,0:T(8,128)S(1)}, u32[]{:S(2)}, u32[]{:S(2)}) collective-permute-start(f32[3,3,8,128]{3,2,1,0:T(8,128)} %get-tuple-element.20), channel_id=1, source_target_pairs={{136,129},{129,136},{9,2},{2,9},{138,131},{131,138},{11,388},{388,... | collective-permute-start | bytes 110600 | tf_op jit(solution)/shard_map/ppermute | solution.py:386
  26.4 1.2 %copy-start = (bf16[3,3,48,1024]{3,2,1,0:T(8,128)(2,1)S(1)}, bf16[3,3,48,1024]{3,2,1,0:T(8,128)(2,1)}, u32[]{:S(2)}) copy-start(bf16[3,3,48,1024]{3,2,1,0:T(8,128)(2,1)} %layers_ref.1) | copy-start | bytes 2654212
  35.5 9.5 %collective-permute-start.1 = (f32[3,3,8,128]{3,2,1,0:T(8,128)S(1)}, f32[3,3,8,128]{3,2,1,0:T(8,128)S(1)}, u32[]{:S(2)}, u32[]{:S(2)}) collective-permute-start(f32[3,3,8,128]{3,2,1,0:T(8,128)S(1)} %get-tuple-element.28), channel_id=1, source_target_pairs={{8,128},{128,8},{136,129},{129,136},{137,1},{1,137},{9,2},{2,9},{1... | collective-permute-start | bytes 110600 | tf_op jit(solution)/shard_map/ppermute | solution.py:402
